TPU v7x, 128 devices: a whole 4x4x4 slice. The times are simulated.
128 devices in a mesh: seq: 4 (over z), vocab: 32 (over y, x, core).
Axes of the slice: x: 4, y: 4, z: 4, core: 2. Of those that a mesh axis runs over, the one named last changes fastest.
Arguments:
- hidden: bfloat16 [2048, 5376], P('seq', 'vocab'), may hold values from -64 to 64
- embed_cotangent: bfloat16 [2048, 5376], P('seq', 'vocab'), may hold values from -24 to 24
- table: bfloat16 [24576, 5376], P('vocab'), may hold values from -3 to 3
- token_ids: int32 [2048], P('seq'), may hold values from 0 to 24575
- target_ids: int32 [2048], P('seq'), may hold values from 0 to 24575
- loss_scale: float32 [2048], P('seq'), may hold values from 8 to 32
Outputs:
- grad_hidden: bfloat16 [2048, 5376], P('seq', 'vocab')
- grad_table: float32 [24576, 5376], P('vocab', 'seq')
- token_loss: float32 [2048], P('seq')
All inputs are finite; a program needn't handle non-finite values.
Results may differ from a plain program's by a relative error of at most 0.0047.
Values may be sent and summed in bfloat16 or wider, within the bound.
No kernel may reach another device: no remote copies, remote signals or barrier semaphores. Data moves between devices by JAX's collectives and lax.ppermute only.
A program may use at most 192 MiB of HBM per device.

v0:
```python
import jax
import jax.numpy as jnp
from jax import lax
from jax.experimental import pallas as pl
from jax.experimental.pallas import tpu as pltpu
from jax.sharding import PartitionSpec as P

BF, F32 = jnp.bfloat16, jnp.float32


def vocab_perm(move):
    pairs = []
    for v in range(32):
        y, x, c = move(v // 8, (v // 2) % 4, v % 2)
        pairs.append((v, (y % 4) * 8 + (x % 4) * 2 + c))
    return pairs


def send_x(a, d):
    return lax.ppermute(a, "vocab", vocab_perm(lambda y, x, c: (y, x + d, c)))


def send_y(a, d):
    return lax.ppermute(a, "vocab", vocab_perm(lambda y, x, c: (y + d, x, c)))


def send_core(a):
    return lax.ppermute(a, "vocab", vocab_perm(lambda y, x, c: (y, x, 1 - c)))


def send_z(a, d):
    return lax.ppermute(a, "seq", [(i, (i + d) % 4) for i in range(4)])


def swap_zy(a):
    pairs = []
    for z in range(4):
        for v in range(32):
            pairs.append((z * 32 + v, (v // 8) * 32 + z * 8 + v % 8))
    return lax.ppermute(a, ("seq", "vocab"), pairs)


def ring_near(a, send):
    return send(a, 1), send(a, -1)


def ring_far(near, send):
    low, high = near
    half = low.shape[-1] // 2
    return send(low[..., :half], 1), send(high[..., half:], -1)


def ring_place(a, near, far, me):
    out = jnp.zeros((4,) + a.shape, a.dtype)
    out = lax.dynamic_update_index_in_dim(out, a, me, 0)
    out = lax.dynamic_update_index_in_dim(out, near[0], (me + 3) % 4, 0)
    out = lax.dynamic_update_index_in_dim(out, near[1], (me + 1) % 4, 0)
    return lax.dynamic_update_index_in_dim(out, jnp.concatenate(far, -1), (me + 2) % 4, 0)


PAD = 176
NN = (((1,), (0,)), ((), ()))


def mm(a, b):
    return lax.dot_general(a, b, NN, preferred_element_type=F32)


def hidden_kernel(own_ref, pair_ref, g_ref, pg_ref, out_ref, again_ref):
    again_ref[...] = g_ref[...]
    out_ref[...] = (mm(own_ref[...], g_ref[...]) + mm(pair_ref[...], pg_ref[...])).astype(BF)


def hidden_terms(own_table, pair_table, grad, pair_grad):
    rows, tokens = grad.shape
    columns, tile = own_table.shape[0], 672
    table = pl.BlockSpec((tile, rows), lambda i: (i, 0))
    whole = pl.BlockSpec((rows, tokens), lambda i: (0, 0))
    return pl.pallas_call(
        hidden_kernel,
        out_shape=[jax.ShapeDtypeStruct((columns, tokens), BF), jax.ShapeDtypeStruct((rows, tokens), BF)],
        grid=(columns // tile,),
        in_specs=[table, table, whole, whole],
        out_specs=[pl.BlockSpec((tile, tokens), lambda i: (i, 0)), whole],
        compiler_params=pltpu.CompilerParams(vmem_limit_bytes=56 << 20),
        cost_estimate=pl.CostEstimate(flops=4 << 30, bytes_accessed=12 << 20, transcendentals=0),
        name="hidden_terms",
    )(own_table, pair_table, grad, pair_grad)


NT = (((1,), (1,)), ((), ()))


def table_kernel(core_ref, *refs):
    cots, hids, grads = refs[:8], refs[8:16], refs[18:22]
    ids_ref, entry_ref, out_ref = refs[16], refs[17], refs[22]
    width, tile = out_ref.shape[2:]
    hots = [(ids_ref[k] == entry_ref[...]).astype(F32).astype(BF) for k in range(4)]
    for core in range(2):
        total = jnp.zeros((4 * width, tile), F32)
        for k in range(4):
            total += lax.dot_general(cots[2 * k + core][...], hots[k], NT, preferred_element_type=F32)
            total += lax.dot_general(hids[2 * k + core][...], grads[k][...], NT, preferred_element_type=F32)
        place = core_ref[0] if core == 0 else 1 - core_ref[0]
        out_ref[:, pl.ds(place, 1)] = total.reshape(4, 1, width, tile)


def table_terms(core, cots, hids, ids, entry, grads, width):
    rows, tokens = grads[0].shape
    tile = 256
    return pl.pallas_call(
        table_kernel,
        out_shape=jax.ShapeDtypeStruct((4, 2, width, rows), F32),
        grid_spec=pltpu.PrefetchScalarGridSpec(
            num_scalar_prefetch=1,
            grid=(rows // tile,),
            in_specs=[pl.BlockSpec((4 * width, tokens), lambda i, core: (0, 0))] * 16
            + [pl.BlockSpec((4, 1, tokens), lambda i, core: (0, 0, 0)), pl.BlockSpec((tile, 1), lambda i, core: (i, 0))]
            + [pl.BlockSpec((tile, tokens), lambda i, core: (i, 0))] * 4,
            out_specs=pl.BlockSpec((4, 2, width, tile), lambda i, core: (0, 0, 0, i)),
        ),
        compiler_params=pltpu.CompilerParams(vmem_limit_bytes=48 << 20),
        cost_estimate=pl.CostEstimate(flops=8 << 30, bytes_accessed=16 << 20, transcendentals=0),
        name="table_terms",
    )(core, *cots, *hids, ids, entry, *grads)


def body(hidden, embed_cotangent, table, token_ids, target_ids, loss_scale):
    tie = lax.optimization_barrier
    z, v = lax.axis_index("seq"), lax.axis_index("vocab")
    y, x, c = v // 8, (v // 2) % 4, v % 2
    rows = table.shape[0]
    entry = v * rows + lax.broadcasted_iota(jnp.int32, (rows, 1), 0)
    order = [z, (z + 3) % 4, (z + 1) % 4, (z + 2) % 4]
    hid, cot = hidden.T, embed_cotangent.T
    width, tokens = hid.shape
    same_core = [[2 * k + i for k in range(16)] for i in range(2)]
    first = (((0,), (0,)), ((), ()))
    dot = lambda a, b: lax.dot_general(a, b, first, preferred_element_type=F32)

    id_rows = jnp.stack([token_ids // 256, token_ids % 256]).astype(BF)
    gap = PAD - width
    both = jnp.concatenate([cot, id_rows, jnp.zeros((gap - 2, tokens), BF)], 0)
    both = swap_zy(both)
    hid_near = ring_near(hid, send_x)
    hid_far = ring_far(hid_near, send_x)
    across = ring_place(hid, hid_near, hid_far, x)
    across, both = tie((across, both))
    across_near = ring_near(across, send_y)
    table_t = table.T.reshape(16, 2, width, rows)
    across_near, table_t = tie((across_near, table_t))
    across_far = ring_far(across_near, send_y)
    own_table = lax.dynamic_index_in_dim(table_t, c, 1, keepdims=False).reshape(16 * width, rows)
    other_table = lax.dynamic_index_in_dim(table_t, 1 - c, 1, keepdims=False).reshape(16 * width, rows)
    own_part = ring_place(across, across_near, across_far, y)
    own_part, own_table, other_table, both = tie((own_part, own_table, other_table, both))
    cols = lax.all_gather(both, "vocab", axis=0, axis_index_groups=same_core)

    pick_z = lambda d, part=own_part: lax.dynamic_index_in_dim(part, (z + d) % 4, 0, keepdims=False).reshape(4 * width, tokens)
    opposite = pick_z(2)
    hid_low, hid_high = send_z(pick_z(1), 1), send_z(pick_z(3), -1)
    mid = tokens // 2
    pass_low, pass_high = send_z(opposite[:, :mid], 1), send_z(opposite[:, mid:], -1)
    own_part = own_part.reshape(16 * width, tokens)
    other_part = send_core(own_part)
    logits = dot(own_table, own_part)
    logits, other_part = tie((logits, other_part))
    logits = logits + dot(other_table, other_part)
    pair_table = send_core(other_table)
    hot = target_ids[None, :] == entry
    top = jnp.max(logits, axis=0)
    total = jnp.sum(jnp.exp(logits - top[None, :]), axis=0)
    target = jnp.sum(jnp.where(hot, logits, 0.0), axis=0)
    stats = jnp.stack([top, total, target])
    stats, hid_low, hid_high, pass_low, pass_high = tie((stats, hid_low, hid_high, pass_low, pass_high))
    hid_far = [send_z(pass_low, 1), send_z(pass_high, -1)]
    stats = lax.all_to_all(jnp.broadcast_to(stats[None], (32,) + stats.shape), "vocab", 0, 0)
    row_top = jnp.max(stats[:, 0], axis=0)
    exp_total = jnp.sum(stats[:, 1] * jnp.exp(stats[:, 0] - row_top[None]), axis=0)
    target_logit = jnp.sum(stats[:, 2], axis=0)
    log_norm = row_top + jnp.log(exp_total)
    token_loss = log_norm - target_logit

    grad = loss_scale[None, :] * (jnp.exp(logits - log_norm[None, :]) - hot.astype(F32))
    grad = grad.astype(BF)
    grads = [grad] + [send_z(grad, d) for d in (1, 3, 2)]
    pair_grad = send_core(grad)
    terms, again = hidden_terms(own_table, pair_table, grad, pair_grad)
    terms = lax.all_to_all(terms.reshape(16, width, tokens), "vocab", 0, 0, axis_index_groups=same_core)
    grads[0] = again
    cols, grads, hid_far = tie((cols, grads, hid_far))
    hid_got = [pick_z(0), hid_low, hid_high, jnp.concatenate(hid_far, 1)]
    cols = cols.reshape(4, 4, PAD, tokens)
    cots, hids, ids = [], [], []
    for block, hid_piece in zip(order, hid_got):
        piece = lax.dynamic_index_in_dim(cols, block, 0, keepdims=False)
        pair = piece[0, width : width + 2].astype(F32)
        ids.append((pair[0] * 256.0 + pair[1]).astype(jnp.int32))
        piece = piece[:, :width].reshape(4 * width, tokens)
        cots += [piece, send_core(piece)]
        hids += [hid_piece, send_core(hid_piece)]
    grad_table = table_terms(c.astype(jnp.int32)[None], cots, hids, jnp.stack(ids)[:, None], entry, grads, width)
    terms, grad_table = tie((terms, grad_table))
    grad_hidden = jnp.sum(terms.astype(F32), axis=0).astype(BF).T
    return (grad_hidden, grad_table.reshape(8 * width, rows).T, token_loss)


def solution(mesh):
    placed = (P("seq", "vocab"), P("seq", "vocab"), P("vocab", None), P("seq"), P("seq"), P("seq"))
    return jax.shard_map(
        body,
        mesh=mesh,
        in_specs=placed,
        out_specs=(P("seq", "vocab"), P("vocab", "seq"), P("seq")),
        check_vma=False,
    )
```

profile of v0, /device:TPU:1, one launch (start us, length us, event | category | flops | bytes accessed | tf_op | source)
XLA Modules:
  0.0 185.0 jit_solution(10252865551202150839)
XLA Ops:
  7.2 2.1 %collective-permute-start = (bf16[168,512]{1,0:T(8,128)(2,1)}, bf16[168,512]{1,0:T(8,128)(2,1)S(1)}, u32[]{:S(2)}, u32[]{:S(2)}) collective-permute-start(bf16[168,512]{1,0:T(8,128)(2,1)} %bitcast.103), channel_id=1, source_target_pairs={{0,2},{1,3},{2,4},{3,5},{4,6},{5,7},{6,0},{7,1},{8,10},{9,11},{10,... | collective-permute-start | bytes 516104 | tf_op jit(solution)/shard_map/ppermute | solution.py:20
  9.3 1.4 collective-permute-start.1
  10.7 0.7 fusion.10
  11.5 1.0 maximum_maximum_fusion
  12.5 0.7 collective-permute-start.4
  13.3 0.9 bitcast_dynamic-update-slice_fusion.3
  14.3 0.2 collective-permute-done.1
  14.5 2.6 %collective-permute-start.3 = (bf16[168,256]{1,0:T(8,128)(2,1)S(1)}, bf16[168,256]{1,0:T(8,128)(2,1)S(1)}, u32[]{:S(2)}, u32[]{:S(2)}) collective-permute-start(bf16[168,256]{1,0:T(8,128)(2,1)S(1)} %slice.110), channel_id=1, source_target_pairs={{0,6},{1,7},{2,0},{3,1},{4,2},{5,3},{6,4},{7,5},{8,14},{9,15},{10,... | collective-permute-start | bytes 258056 | tf_op jit(solution)/shard_map/ppermute | solution.py:20
  17.2 1.4 collective-permute-done.3
  18.6 3.1 %collective-permute-done.2 = bf16[168,256]{1,0:T(8,128)(2,1)S(1)} collective-permute-done((bf16[168,256]{1,0:T(8,128)(2,1)S(1)}, bf16[168,256]{1,0:T(8,128)(2,1)S(1)}, u32[]{:S(2)}, u32[]{:S(2)}) %collective-permute-start.2) | collective-permute-done | bytes 86048 | tf_op jit(solution)/shard_map/ppermute | solution.py:20
  21.7 2.8 %collective-permute-start.5 = (bf16[4,168,512]{2,1,0:T(8,128)(2,1)S(1)}, bf16[4,168,512]{2,1,0:T(8,128)(2,1)}, u32[]{:S(2)}, u32[]{:S(2)}) collective-permute-start(bf16[4,168,512]{2,1,0:T(8,128)(2,1)S(1)} %fusion.5), channel_id=1, source_target_pairs={{0,8},{1,9},{2,10},{3,11},{4,12},{5,13},{6,14},{7,15},{8,16},{9,17... | collective-permute-start | bytes 2064392 | tf_op jit(solution)/shard_map/ppermute | solution.py:24
  24.5 4.1 %collective-permute-start.6 = (bf16[4,168,512]{2,1,0:T(8,128)(2,1)S(1)}, bf16[4,168,512]{2,1,0:T(8,128)(2,1)}, u32[]{:S(2)}, u32[]{:S(2)}) collective-permute-start(bf16[4,168,512]{2,1,0:T(8,128)(2,1)S(1)} %fusion.5), channel_id=1, source_target_pairs={{0,24},{1,25},{2,26},{3,27},{4,28},{5,29},{6,30},{7,31},{8,0},{9,1... | collective-permute-start | bytes 2064392 | tf_op jit(solution)/shard_map/ppermute | solution.py:24
  28.7 11.8 %copy.15 = bf16[768,5376]{0,1:T(8,128)(2,1)} copy(bf16[768,5376]{1,0:T(8,128)(2,1)} %param.8) | data formatting | bytes 16515072 | tf_op args[2]
  40.5 0.2 broadcast_in_dim.56
  40.8 1.0 collective-permute-done.5
  41.8 1.5 slice.87
  43.3 2.1 %collective-permute-start.8 = (bf16[4,168,256]{2,1,0:T(8,128)(2,1)S(1)}, bf16[4,168,256]{2,1,0:T(8,128)(2,1)S(1)}, u32[]{:S(2)}, u32[]{:S(2)}) collective-permute-start(bf16[4,168,256]{2,1,0:T(8,128)(2,1)S(1)} %slice.87), channel_id=1, source_target_pairs={{0,24},{1,25},{2,26},{3,27},{4,28},{5,29},{6,30},{7,31},{8,0},{9,1... | collective-permute-start | bytes 1032200 | tf_op jit(solution)/shard_map/ppermute | solution.py:24
  45.4 1.0 slice.86
  46.5 1.2 bitcast_dynamic-update-slice_fusion.1
  47.6 1.2 bitcast_dynamic-update-slice_fusion
  48.8 3.8 %constant_dynamic-slice_fusion.4 = (bf16[16,1,168,768]{3,2,1,0:T(8,128)(2,1)}, bf16[16,1,168,768]{3,2,1,0:T(8,128)(2,1)}) fusion(bf16[16,2,168,768]{3,2,1,0:T(8,128)(2,1)S(1)} %bitcast.88, s32[]{:T(128)S(6)} %select_n.153, s32[]{:T(128)S(6)} %select_n.152), kind=kLoop, calls=%fused_computation.37 | loop fusion | bytes 16515080 | tf_op jit(solution)/shard_map/jit(dynamic_index_in_dim)/dynamic_slice | solution.py:154
  52.6 1.1 collective-permute-done.7
  53.8 5.0 %collective-permute-start.10 = (bf16[2688,512]{1,0:T(8,128)(2,1)S(1)}, bf16[2688,512]{1,0:T(8,128)(2,1)}, u32[]{:S(2)}, u32[]{:S(2)}) collective-permute-start(bf16[2688,512]{1,0:T(8,128)(2,1)S(1)} %bitcast.89), channel_id=1, source_target_pairs={{0,1},{1,0},{2,3},{3,2},{4,5},{5,4},{6,7},{7,6},{8,9},{9,8},{10,11... | collective-permute-start | bytes 8257544 | tf_op jit(solution)/shard_map/ppermute | solution.py:28
  58.9 0.1 collective-permute-start.9
  59.0 1.2 constant_dynamic-slice_fusion
  60.2 1.2 collective-permute-start.11
  61.4 5.8 %collective-permute-start.12 = (bf16[672,512]{1,0:T(8,128)(2,1)S(1)}, bf16[672,512]{1,0:T(8,128)(2,1)S(1)}, u32[]{:S(2)}, u32[]{:S(2)}) collective-permute-start(bf16[672,512]{1,0:T(8,128)(2,1)S(1)} %bitcast.100), channel_id=1, source_target_pairs={{0,96},{32,0},{64,32},{96,64},{1,97},{33,1},{65,33},{97,65},{2,98}... | collective-permute-start | bytes 2064392 | tf_op jit(solution)/shard_map/ppermute | solution.py:32
  67.2 0.1 collective-permute-start.13
  67.3 2.4 %fusion.24 = f32[768,512]{1,0:T(8,128)S(1)} fusion(bf16[2688,768]{1,0:T(8,128)(2,1)S(1)} %bitcast.92, bf16[2688,512]{1,0:T(8,128)(2,1)S(1)} %bitcast.90), kind=kOutput, calls=%fused_computation.75 | convolution fusion | flops 2113929216 | bytes 8454144 | tf_op jit(solution)/shard_map/dot_general | solution.py:139
  69.7 2.9 %collective-permute-start.14 = (bf16[672,256]{1,0:T(8,128)(2,1)S(1)}, bf16[672,256]{1,0:T(8,128)(2,1)}, u32[]{:S(2)}, u32[]{:S(2)}) collective-permute-start(bf16[672,256]{1,0:T(8,128)(2,1)S(1)} %get-tuple-element.75), channel_id=1, source_target_pairs={{0,96},{32,0},{64,32},{96,64},{1,97},{33,1},{65,33},{97,65},{2,98}... | collective-permute-start | bytes 1032200 | tf_op jit(solution)/shard_map/ppermute | solution.py:32
  72.6 4.2 %fusion.25 = f32[768,512]{1,0:T(8,128)S(1)} fusion(bf16[2688,768]{1,0:T(8,128)(2,1)S(1)} %bitcast.94, bf16[2688,512]{1,0:T(8,128)(2,1)} %collective-permute-done.10), kind=kOutput, calls=%fused_computation.76 | convolution fusion | flops 2113929216 | bytes 8454144 | tf_op jit(solution)/shard_map/dot_general | solution.py:139
  76.8 0.4 fusion.22
  77.2 0.2 copy-done.5
  77.5 0.4 exponential_reduce_fusion
  77.9 12.1 %collective-permute-done.13 = bf16[672,256]{1,0:T(8,128)(2,1)} collective-permute-done((bf16[672,256]{1,0:T(8,128)(2,1)S(1)}, bf16[672,256]{1,0:T(8,128)(2,1)}, u32[]{:S(2)}, u32[]{:S(2)}) %collective-permute-start.13) | collective-permute-done | bytes 344096 | tf_op jit(solution)/shard_map/ppermute | solution.py:32
  90.1 15.1 %all_to_all.10 = f32[32,3,512]{2,1,0:T(4,128)S(1)} all-to-all(f32[32,3,512]{2,1,0:T(4,128)S(1)} %broadcast_in_dim.68), channel_id=1, replica_groups=mesh['seq'=4,'vocab'=32] {'vocab'}, dimensions={0} | all-to-all | bytes 393216 | tf_op jit(solution)/shard_map/all_to_all | solution.py:177
  105.1 0.2 slice_reduce_fusion
  105.4 0.6 fusion.21
  106.0 1.3 fusion.3.g_ref
  107.3 1.2 collective-permute-start.15
  108.4 0.8 collective-permute-start.16
  109.3 1.8 collective-permute-start.17
  111.1 1.4 collective-permute-start.18
  112.6 0.7 collective-permute-start.19
  113.3 2.1 %collective-permute-start.20 = (bf16[672,256]{1,0:T(8,128)(2,1)}, bf16[672,256]{1,0:T(8,128)(2,1)}, u32[]{:S(2)}, u32[]{:S(2)}) collective-permute-start(bf16[672,256]{1,0:T(8,128)(2,1)} %collective-permute-done.14), channel_id=1, source_target_pairs={{0,96},{32,0},{64,32},{96,64},{1,97},{33,1},{65,33},{97,65},{2,98}... | collective-permute-start | bytes 1032200 | tf_op jit(solution)/shard_map/ppermute | solution.py:32
  115.4 8.7 %hidden_terms.1 = (bf16[2688,512]{1,0:T(8,128)(2,1)}, bf16[768,512]{1,0:T(8,128)(2,1)}) custom-call(bf16[2688,768]{1,0:T(8,128)(2,1)} %bitcast.91, bf16[2688,768]{1,0:T(8,128)(2,1)} %collective-permute-done.9.pair_ref, bf16[768,512]{1,0:T(8,128)(2,1)} %fusion.3.g_ref, bf16[768,512]{1,0:T(8,128)(2,1)} %copy-done.7), custom_call_target="tpu_custom_call" | custom-call | flops 4294967296 | bytes 12582912 | tf_op jit(solution)/shard_map/hidden_terms/pallas_call | solution.py:79
  124.1 3.7 %all-to-all-start.1 = ((bf16[16,168,512]{2,1,0:T(8,128)(2,1)}), bf16[16,168,512]{2,1,0:T(8,128)(2,1)S(1)}, u32[]{:S(2)}, u32[]{:S(2)}) async-start(bf16[16,168,512]{2,1,0:T(8,128)(2,1)} %bitcast.97), calls=%async_computation.1 | async-start | bytes 5505024 | tf_op jit(solution)/shard_map/all_to_all | solution.py:189
  127.8 25.4 %collective-permute-done.19 = bf16[672,256]{1,0:T(8,128)(2,1)S(1)} collective-permute-done((bf16[672,256]{1,0:T(8,128)(2,1)}, bf16[672,256]{1,0:T(8,128)(2,1)S(1)}, u32[]{:S(2)}, u32[]{:S(2)}) %collective-permute-start.19) | collective-permute-done | bytes 344096 | tf_op jit(solution)/shard_map/ppermute | solution.py:32
  153.2 0.9 collective-permute-start.25
  154.1 0.5 collective-permute-start.27
  154.6 2.1 %dynamic-slice_bitcast_fusion = (bf16[4,176,512]{2,1,0:T(8,128)(2,1)S(1)}, bf16[4,176,512]{2,1,0:T(8,128)(2,1)S(1)}, bf16[4,176,512]{2,1,0:T(8,128)(2,1)S(1)}, bf16[4,176,512]{2,1,0:T(8,128)(2,1)S(1)}) fusion(bf16[4,4,176,512]{3,2,1,0:T(8,128)(2,1)} %bitcast.95, s32[]{:T(128)S(6)} %select_n.160, s32[]{:T(128)S(6)} %select_n.156, s32[]{:T(128)S(6)} %select_n.158, ...), kind=kLoop, calls=%fused_computation.7 | loop fusion | bytes 5767184 | tf_op jit(solution)/shard_map/jit(dynamic_index_in_dim)/squeeze | solution.py:196
  156.7 0.2 collective-permute-start.21
  156.9 0.5 collective-permute-start.22
  157.5 1.0 constant_dynamic-update-slice_fusion.refs_14_
  158.6 0.2 collective-permute-start.23
  158.8 0.4 collective-permute-start.24
  159.2 0.1 collective-permute-start.28
  159.4 0.5 collective-permute-done.22.refs_3_
  159.9 1.0 collective-permute-done.23.refs_5_
  160.9 1.0 collective-permute-done.24.refs_7_
  161.9 1.0 collective-permute-done.28.refs_15_
  162.9 0.8 copy-done.10
  163.7 13.4 %table_terms.1 = f32[4,2,168,768]{3,2,1,0:T(8,128)} custom-call(s32[1]{0:T(128)} %bitcast.23.core_ref, bf16[672,512]{1,0:T(8,128)(2,1)S(1)} %bitcast.81, bf16[672,512]{1,0:T(8,128)(2,1)S(1)} %collective-permute-done.21.refs_1_, bf16[672,512]{1,0:T(8,128)(2,1)S(1)} %bitcast.83, bf16[672,512]{1,0:T(8,128)(2,1)S(1)} %collective-permute-done.22.refs_3_, ...), custom_call_target="tpu_custom_call" | custom-call | flops 8589934592 | bytes 16777216 | tf_op jit(solution)/shard_map/table_terms/pallas_call | solution.py:111
  177.1 1.1 reduce_sum.51
  (76 shorter events, 1.1 us)
Async XLA Ops:
  7.2 147.4 %all-gather.3.cloned.1.call-start = ((), (), s32[]{:S(2)}) async-start(), calls=%async_computation.2 | async-start | bytes 3063808 | tf_op jit(solution)/shard_map/all_gather | solution.py:157
  7.2 9.8 %collective-permute-start = (bf16[168,512]{1,0:T(8,128)(2,1)}, bf16[168,512]{1,0:T(8,128)(2,1)S(1)}, u32[]{:S(2)}, u32[]{:S(2)}) collective-permute-start(bf16[168,512]{1,0:T(8,128)(2,1)} %bitcast.103), channel_id=1, source_target_pairs={{0,2},{1,3},{2,4},{3,5},{4,6},{5,7},{6,0},{7,1},{8,10},{9,11},{10,... | collective-permute-start | bytes 516104 | tf_op jit(solution)/shard_map/ppermute | solution.py:20
  9.3 5.1 %collective-permute-start.1 = (bf16[168,512]{1,0:T(8,128)(2,1)}, bf16[168,512]{1,0:T(8,128)(2,1)S(1)}, u32[]{:S(2)}, u32[]{:S(2)}) collective-permute-start(bf16[168,512]{1,0:T(8,128)(2,1)} %bitcast.104), channel_id=1, source_target_pairs={{0,6},{1,7},{2,0},{3,1},{4,2},{5,3},{6,4},{7,5},{8,14},{9,15},{10,... | collective-permute-start | bytes 516104 | tf_op jit(solution)/shard_map/ppermute | solution.py:20
  12.5 9.2 %collective-permute-start.4 = (bf16[176,512]{1,0:T(8,128)(2,1)S(1)}, bf16[176,512]{1,0:T(8,128)(2,1)S(1)}, u32[]{:S(2)}, u32[]{:S(2)}) collective-permute-start(bf16[176,512]{1,0:T(8,128)(2,1)S(1)} %maximum_maximum_fusion), channel_id=1, source_target_pairs={{0,0},{1,1},{2,2},{3,3},{4,4},{5,5},{6,6},{7,7},{8,32},{9,33},{10,... | collective-permute-start | bytes 540680 | tf_op jit(solution)/shard_map/ppermute | solution.py:40
  14.5 4.1 %collective-permute-start.3 = (bf16[168,256]{1,0:T(8,128)(2,1)S(1)}, bf16[168,256]{1,0:T(8,128)(2,1)S(1)}, u32[]{:S(2)}, u32[]{:S(2)}) collective-permute-start(bf16[168,256]{1,0:T(8,128)(2,1)S(1)} %slice.110), channel_id=1, source_target_pairs={{0,6},{1,7},{2,0},{3,1},{4,2},{5,3},{6,4},{7,5},{8,14},{9,15},{10,... | collective-permute-start | bytes 258056 | tf_op jit(solution)/shard_map/ppermute | solution.py:20
  17.1 4.6 %collective-permute-start.2 = (bf16[168,256]{1,0:T(8,128)(2,1)S(1)}, bf16[168,256]{1,0:T(8,128)(2,1)S(1)}, u32[]{:S(2)}, u32[]{:S(2)}) collective-permute-start(bf16[168,256]{1,0:T(8,128)(2,1)S(1)} %slice.109), channel_id=1, source_target_pairs={{0,2},{1,3},{2,4},{3,5},{4,6},{5,7},{6,0},{7,1},{8,10},{9,11},{10,... | collective-permute-start | bytes 258056 | tf_op jit(solution)/shard_map/ppermute | solution.py:20
  21.7 18.8 %copy-start.3 = (bf16[176,512]{1,0:T(8,128)(2,1)}, bf16[176,512]{1,0:T(8,128)(2,1)S(1)}, u32[]{:S(2)}) copy-start(bf16[176,512]{1,0:T(8,128)(2,1)S(1)} %collective-permute-done.4) | copy-start | bytes 540676
  21.7 20.0 %collective-permute-start.5 = (bf16[4,168,512]{2,1,0:T(8,128)(2,1)S(1)}, bf16[4,168,512]{2,1,0:T(8,128)(2,1)}, u32[]{:S(2)}, u32[]{:S(2)}) collective-permute-start(bf16[4,168,512]{2,1,0:T(8,128)(2,1)S(1)} %fusion.5), channel_id=1, source_target_pairs={{0,8},{1,9},{2,10},{3,11},{4,12},{5,13},{6,14},{7,15},{8,16},{9,17... | collective-permute-start | bytes 2064392 | tf_op jit(solution)/shard_map/ppermute | solution.py:24
  24.5 17.2 %collective-permute-start.6 = (bf16[4,168,512]{2,1,0:T(8,128)(2,1)S(1)}, bf16[4,168,512]{2,1,0:T(8,128)(2,1)}, u32[]{:S(2)}, u32[]{:S(2)}) collective-permute-start(bf16[4,168,512]{2,1,0:T(8,128)(2,1)S(1)} %fusion.5), channel_id=1, source_target_pairs={{0,24},{1,25},{2,26},{3,27},{4,28},{5,29},{6,30},{7,31},{8,0},{9,1... | collective-permute-start | bytes 2064392 | tf_op jit(solution)/shard_map/ppermute | solution.py:24
  40.5 8.3 %copy-start = (bf16[768,5376]{0,1:T(8,128)(2,1)S(1)}, bf16[768,5376]{0,1:T(8,128)(2,1)}, u32[]{:S(2)}) copy-start(bf16[768,5376]{0,1:T(8,128)(2,1)} %copy.15) | copy-start | bytes 24772612
  43.3 9.3 %collective-permute-start.8 = (bf16[4,168,256]{2,1,0:T(8,128)(2,1)S(1)}, bf16[4,168,256]{2,1,0:T(8,128)(2,1)S(1)}, u32[]{:S(2)}, u32[]{:S(2)}) collective-permute-start(bf16[4,168,256]{2,1,0:T(8,128)(2,1)S(1)} %slice.87), channel_id=1, source_target_pairs={{0,24},{1,25},{2,26},{3,27},{4,28},{5,29},{6,30},{7,31},{8,0},{9,1... | collective-permute-start | bytes 1032200 | tf_op jit(solution)/shard_map/ppermute | solution.py:24
  46.4 7.4 %collective-permute-start.7 = (bf16[4,168,256]{2,1,0:T(8,128)(2,1)S(1)}, bf16[4,168,256]{2,1,0:T(8,128)(2,1)S(1)}, u32[]{:S(2)}, u32[]{:S(2)}) collective-permute-start(bf16[4,168,256]{2,1,0:T(8,128)(2,1)S(1)} %slice.86), channel_id=1, source_target_pairs={{0,8},{1,9},{2,10},{3,11},{4,12},{5,13},{6,14},{7,15},{8,16},{9,17... | collective-permute-start | bytes 1032200 | tf_op jit(solution)/shard_map/ppermute | solution.py:24
  53.8 15.9 %collective-permute-start.10 = (bf16[2688,512]{1,0:T(8,128)(2,1)S(1)}, bf16[2688,512]{1,0:T(8,128)(2,1)}, u32[]{:S(2)}, u32[]{:S(2)}) collective-permute-start(bf16[2688,512]{1,0:T(8,128)(2,1)S(1)} %bitcast.89), channel_id=1, source_target_pairs={{0,1},{1,0},{2,3},{3,2},{4,5},{5,4},{6,7},{7,6},{8,9},{9,8},{10,11... | collective-permute-start | bytes 8257544 | tf_op jit(solution)/shard_map/ppermute | solution.py:28
  58.9 8.4 %copy-start.1 = (bf16[16,1,168,768]{3,2,1,0:T(8,128)(2,1)S(1)}, bf16[16,1,168,768]{3,2,1,0:T(8,128)(2,1)}, u32[]{:S(2)}) copy-start(bf16[16,1,168,768]{3,2,1,0:T(8,128)(2,1)} %get-tuple-element.66) | copy-start | bytes 12386308
  58.9 54.3 %collective-permute-start.9 = (bf16[2688,768]{1,0:T(8,128)(2,1)}, bf16[2688,768]{1,0:T(8,128)(2,1)}, u32[]{:S(2)}, u32[]{:S(2)}) collective-permute-start(bf16[2688,768]{1,0:T(8,128)(2,1)} %bitcast.93), channel_id=1, source_target_pairs={{0,1},{1,0},{2,3},{3,2},{4,5},{5,4},{6,7},{7,6},{8,9},{9,8},{10,11... | collective-permute-start | bytes 12386312 | tf_op jit(solution)/shard_map/ppermute | solution.py:28
  60.2 29.8 %collective-permute-start.11 = (bf16[672,512]{1,0:T(8,128)(2,1)S(1)}, bf16[672,512]{1,0:T(8,128)(2,1)S(1)}, u32[]{:S(2)}, u32[]{:S(2)}) collective-permute-start(bf16[672,512]{1,0:T(8,128)(2,1)S(1)} %bitcast.101), channel_id=1, source_target_pairs={{0,32},{32,64},{64,96},{96,0},{1,33},{33,65},{65,97},{97,1},{2,34}... | collective-permute-start | bytes 2064392 | tf_op jit(solution)/shard_map/ppermute | solution.py:32
  61.4 28.6 %collective-permute-start.12 = (bf16[672,512]{1,0:T(8,128)(2,1)S(1)}, bf16[672,512]{1,0:T(8,128)(2,1)S(1)}, u32[]{:S(2)}, u32[]{:S(2)}) collective-permute-start(bf16[672,512]{1,0:T(8,128)(2,1)S(1)} %bitcast.100), channel_id=1, source_target_pairs={{0,96},{32,0},{64,32},{96,64},{1,97},{33,1},{65,33},{97,65},{2,98}... | collective-permute-start | bytes 2064392 | tf_op jit(solution)/shard_map/ppermute | solution.py:32
  67.2 5.4 %copy-start.2 = (bf16[16,1,168,768]{3,2,1,0:T(8,128)(2,1)S(1)}, bf16[16,1,168,768]{3,2,1,0:T(8,128)(2,1)}, u32[]{:S(2)}) copy-start(bf16[16,1,168,768]{3,2,1,0:T(8,128)(2,1)} %get-tuple-element.65) | copy-start | bytes 12386308
  67.2 22.8 %collective-permute-start.13 = (bf16[672,256]{1,0:T(8,128)(2,1)S(1)}, bf16[672,256]{1,0:T(8,128)(2,1)}, u32[]{:S(2)}, u32[]{:S(2)}) collective-permute-start(bf16[672,256]{1,0:T(8,128)(2,1)S(1)} %get-tuple-element.76), channel_id=1, source_target_pairs={{0,32},{32,64},{64,96},{96,0},{1,33},{33,65},{65,97},{97,1},{2,34}... | collective-permute-start | bytes 1032200 | tf_op jit(solution)/shard_map/ppermute | solution.py:32
  69.7 20.3 %collective-permute-start.14 = (bf16[672,256]{1,0:T(8,128)(2,1)S(1)}, bf16[672,256]{1,0:T(8,128)(2,1)}, u32[]{:S(2)}, u32[]{:S(2)}) collective-permute-start(bf16[672,256]{1,0:T(8,128)(2,1)S(1)} %get-tuple-element.75), channel_id=1, source_target_pairs={{0,96},{32,0},{64,32},{96,64},{1,97},{33,1},{65,33},{97,65},{2,98}... | collective-permute-start | bytes 1032200 | tf_op jit(solution)/shard_map/ppermute | solution.py:32
  76.8 0.7 copy-start.5
  76.8 29.2 %copy-start.6 = (f32[512]{0:T(512)S(1)}, f32[512]{0:T(512)}, u32[]{:S(2)}) copy-start(f32[512]{0:T(512)} %param.11) | copy-start | bytes 6148
  90.0 17.3 %copy-start.8 = (bf16[672,512]{1,0:T(8,128)(2,1)}, bf16[672,512]{1,0:T(8,128)(2,1)S(1)}, u32[]{:S(2)}) copy-start(bf16[672,512]{1,0:T(8,128)(2,1)S(1)} %collective-permute-done.11.refs_10_) | copy-start | bytes 2064388
  90.0 18.4 %copy-start.9 = (bf16[672,512]{1,0:T(8,128)(2,1)}, bf16[672,512]{1,0:T(8,128)(2,1)S(1)}, u32[]{:S(2)}) copy-start(bf16[672,512]{1,0:T(8,128)(2,1)S(1)} %collective-permute-done.12.refs_12_) | copy-start | bytes 2064388
  107.3 5.3 %collective-permute-start.15 = (bf16[768,512]{1,0:T(8,128)(2,1)}, bf16[768,512]{1,0:T(8,128)(2,1)S(1)}, u32[]{:S(2)}, u32[]{:S(2)}) collective-permute-start(bf16[768,512]{1,0:T(8,128)(2,1)} %fusion.3.g_ref), channel_id=1, source_target_pairs={{0,1},{1,0},{2,3},{3,2},{4,5},{5,4},{6,7},{7,6},{8,9},{9,8},{10,11... | collective-permute-start | bytes 2359304 | tf_op jit(solution)/shard_map/ppermute | solution.py:28
  108.4 45.6 %collective-permute-start.16 = (bf16[768,512]{1,0:T(8,128)(2,1)}, bf16[768,512]{1,0:T(8,128)(2,1)}, u32[]{:S(2)}, u32[]{:S(2)}) collective-permute-start(bf16[768,512]{1,0:T(8,128)(2,1)} %fusion.3.g_ref), channel_id=1, source_target_pairs={{0,32},{32,64},{64,96},{96,0},{1,33},{33,65},{65,97},{97,1},{2,34}... | collective-permute-start | bytes 2359304 | tf_op jit(solution)/shard_map/ppermute | solution.py:32
  109.3 45.3 %collective-permute-start.17 = (bf16[768,512]{1,0:T(8,128)(2,1)}, bf16[768,512]{1,0:T(8,128)(2,1)}, u32[]{:S(2)}, u32[]{:S(2)}) collective-permute-start(bf16[768,512]{1,0:T(8,128)(2,1)} %fusion.3.g_ref), channel_id=1, source_target_pairs={{0,96},{32,0},{64,32},{96,64},{1,97},{33,1},{65,33},{97,65},{2,98}... | collective-permute-start | bytes 2359304 | tf_op jit(solution)/shard_map/ppermute | solution.py:32
  111.1 43.5 %collective-permute-start.18 = (bf16[768,512]{1,0:T(8,128)(2,1)}, bf16[768,512]{1,0:T(8,128)(2,1)}, u32[]{:S(2)}, u32[]{:S(2)}) collective-permute-start(bf16[768,512]{1,0:T(8,128)(2,1)} %fusion.3.g_ref), channel_id=1, source_target_pairs={{0,64},{32,96},{64,0},{96,32},{1,65},{33,97},{65,1},{97,33},{2,66}... | collective-permute-start | bytes 2359304 | tf_op jit(solution)/shard_map/ppermute | solution.py:32
  112.6 2.8 %copy-start.7 = (bf16[768,512]{1,0:T(8,128)(2,1)}, bf16[768,512]{1,0:T(8,128)(2,1)S(1)}, u32[]{:S(2)}) copy-start(bf16[768,512]{1,0:T(8,128)(2,1)S(1)} %collective-permute-done.15.pg_ref) | copy-start | bytes 2359300
  112.6 40.6 %collective-permute-start.19 = (bf16[672,256]{1,0:T(8,128)(2,1)}, bf16[672,256]{1,0:T(8,128)(2,1)S(1)}, u32[]{:S(2)}, u32[]{:S(2)}) collective-permute-start(bf16[672,256]{1,0:T(8,128)(2,1)} %collective-permute-done.13), channel_id=1, source_target_pairs={{0,32},{32,64},{64,96},{96,0},{1,33},{33,65},{65,97},{97,1},{2,34}... | collective-permute-start | bytes 1032200 | tf_op jit(solution)/shard_map/ppermute | solution.py:32
  113.3 40.8 %collective-permute-start.20 = (bf16[672,256]{1,0:T(8,128)(2,1)}, bf16[672,256]{1,0:T(8,128)(2,1)}, u32[]{:S(2)}, u32[]{:S(2)}) collective-permute-start(bf16[672,256]{1,0:T(8,128)(2,1)} %collective-permute-done.14), channel_id=1, source_target_pairs={{0,96},{32,0},{64,32},{96,64},{1,97},{33,1},{65,33},{97,65},{2,98}... | collective-permute-start | bytes 1032200 | tf_op jit(solution)/shard_map/ppermute | solution.py:32
  124.1 53.0 %all-to-all-start.1 = ((bf16[16,168,512]{2,1,0:T(8,128)(2,1)}), bf16[16,168,512]{2,1,0:T(8,128)(2,1)S(1)}, u32[]{:S(2)}, u32[]{:S(2)}) async-start(bf16[16,168,512]{2,1,0:T(8,128)(2,1)} %bitcast.97), calls=%async_computation.1 | async-start | bytes 5505024 | tf_op jit(solution)/shard_map/all_to_all | solution.py:189
  153.2 5.4 %collective-permute-start.25 = (bf16[672,512]{1,0:T(8,128)(2,1)}, bf16[672,512]{1,0:T(8,128)(2,1)}, u32[]{:S(2)}, u32[]{:S(2)}) collective-permute-start(bf16[672,512]{1,0:T(8,128)(2,1)} %bitcast.98), channel_id=1, source_target_pairs={{0,1},{1,0},{2,3},{3,2},{4,5},{5,4},{6,7},{7,6},{8,9},{9,8},{10,11... | collective-permute-start | bytes 2064392 | tf_op jit(solution)/shard_map/ppermute | solution.py:28
  154.1 4.7 %collective-permute-start.26 = (bf16[672,512]{1,0:T(8,128)(2,1)}, bf16[672,512]{1,0:T(8,128)(2,1)}, u32[]{:S(2)}, u32[]{:S(2)}) collective-permute-start(bf16[672,512]{1,0:T(8,128)(2,1)} %copy-done.8), channel_id=1, source_target_pairs={{0,1},{1,0},{2,3},{3,2},{4,5},{5,4},{6,7},{7,6},{8,9},{9,8},{10,11... | collective-permute-start | bytes 2064392 | tf_op jit(solution)/shard_map/ppermute | solution.py:28
  154.1 5.2 %collective-permute-start.27 = (bf16[672,512]{1,0:T(8,128)(2,1)}, bf16[672,512]{1,0:T(8,128)(2,1)}, u32[]{:S(2)}, u32[]{:S(2)}) collective-permute-start(bf16[672,512]{1,0:T(8,128)(2,1)} %copy-done.9), channel_id=1, source_target_pairs={{0,1},{1,0},{2,3},{3,2},{4,5},{5,4},{6,7},{7,6},{8,9},{9,8},{10,11... | collective-permute-start | bytes 2064392 | tf_op jit(solution)/shard_map/ppermute | solution.py:28
  156.7 2.7 %collective-permute-start.21 = (bf16[672,512]{1,0:T(8,128)(2,1)S(1)}, bf16[672,512]{1,0:T(8,128)(2,1)S(1)}, u32[]{:S(2)}, u32[]{:S(2)}) collective-permute-start(bf16[672,512]{1,0:T(8,128)(2,1)S(1)} %bitcast.80), channel_id=1, source_target_pairs={{0,1},{1,0},{2,3},{3,2},{4,5},{5,4},{6,7},{7,6},{8,9},{9,8},{10,11... | collective-permute-start | bytes 2064392 | tf_op jit(solution)/shard_map/ppermute | solution.py:28
  156.9 3.0 %collective-permute-start.22 = (bf16[672,512]{1,0:T(8,128)(2,1)S(1)}, bf16[672,512]{1,0:T(8,128)(2,1)S(1)}, u32[]{:S(2)}, u32[]{:S(2)}) collective-permute-start(bf16[672,512]{1,0:T(8,128)(2,1)S(1)} %bitcast.82), channel_id=1, source_target_pairs={{0,1},{1,0},{2,3},{3,2},{4,5},{5,4},{6,7},{7,6},{8,9},{9,8},{10,11... | collective-permute-start | bytes 2064392 | tf_op jit(solution)/shard_map/ppermute | solution.py:28
  158.5 4.4 %copy-start.4 = (bf16[672,512]{1,0:T(8,128)(2,1)}, bf16[672,512]{1,0:T(8,128)(2,1)S(1)}, u32[]{:S(2)}) copy-start(bf16[672,512]{1,0:T(8,128)(2,1)S(1)} %constant_dynamic-update-slice_fusion.refs_14_) | copy-start | bytes 2064388
  158.6 2.3 %collective-permute-start.23 = (bf16[672,512]{1,0:T(8,128)(2,1)S(1)}, bf16[672,512]{1,0:T(8,128)(2,1)S(1)}, u32[]{:S(2)}, u32[]{:S(2)}) collective-permute-start(bf16[672,512]{1,0:T(8,128)(2,1)S(1)} %bitcast.84), channel_id=1, source_target_pairs={{0,1},{1,0},{2,3},{3,2},{4,5},{5,4},{6,7},{7,6},{8,9},{9,8},{10,11... | collective-permute-start | bytes 2064392 | tf_op jit(solution)/shard_map/ppermute | solution.py:28
  158.8 3.1 %collective-permute-start.24 = (bf16[672,512]{1,0:T(8,128)(2,1)S(1)}, bf16[672,512]{1,0:T(8,128)(2,1)S(1)}, u32[]{:S(2)}, u32[]{:S(2)}) collective-permute-start(bf16[672,512]{1,0:T(8,128)(2,1)S(1)} %bitcast.86), channel_id=1, source_target_pairs={{0,1},{1,0},{2,3},{3,2},{4,5},{5,4},{6,7},{7,6},{8,9},{9,8},{10,11... | collective-permute-start | bytes 2064392 | tf_op jit(solution)/shard_map/ppermute | solution.py:28
  159.2 3.6 %collective-permute-start.28 = (bf16[672,512]{1,0:T(8,128)(2,1)S(1)}, bf16[672,512]{1,0:T(8,128)(2,1)S(1)}, u32[]{:S(2)}, u32[]{:S(2)}) collective-permute-start(bf16[672,512]{1,0:T(8,128)(2,1)S(1)} %constant_dynamic-update-slice_fusion.refs_14_), channel_id=1, source_target_pairs={{0,1},{1,0},{2,3},{3,2},{4,5},{5,4},{6,7},{7,6},{8,9},{9,8},{10,11... | collective-permute-start | bytes 2064392 | tf_op jit(solution)/shard_map/ppermute | solution.py:28
  162.9 0.8 copy-start.10
Sparse Core Ops, SparseCore 0:
  59.0 50.5 all-gather.2
where the time goes:
time: 186 us; the launch traced here: 185 us
  waiting for transfers between devices  47.7 us (26%)
  starting transfers between devices  45.4 us (24%)
  local copies, waits for them, and re-layouts  27.6 us (15%)
  Pallas kernels  22.1 us (12%)
  blocking collectives  15.1 us (8%)
  between operations  14.6 us (8%)
  matrix products  6.61 us (4%)
  other arithmetic  5.9 us (3%)
    ppermute x9, waiting for transfers between devices, send_z(): return lax.ppermute(a, 'seq', [(i, (i + d) % 4) for i in range(4)])  37.5 us
    ppermute x9, starting transfers between devices, send_z(): return lax.ppermute(a, 'seq', [(i, (i + d) % 4) for i in range(4)])  16.7 us
    all_to_all x1, blocking collectives, body(): lax.all_to_all(jnp.broadcast_to(stats[None], (32,) + stats.shape), 'vocab...  15.1 us
    pallas_call x1, Pallas kernels, table_terms(): pl.pallas_call(table_kernel, out_shape=jax.ShapeDtypeStruct((4, 2, width,...  13.4 us
    unnamed x24, local copies, waits for them, and re-layouts  13 us
    ppermute x4, starting transfers between devices, send_y(): return lax.ppermute(a, 'vocab', vocab_perm(lambda y, x, c: (y + d, x, c)))  9.08 us
    ppermute x11, starting transfers between devices, send_core(): return lax.ppermute(a, 'vocab', vocab_perm(lambda y, x, c: (y, x, 1 - c)))  9.04 us
    pallas_call x1, Pallas kernels, hidden_terms(): pl.pallas_call(hidden_kernel, out_shape=[jax.ShapeDtypeStruct((columns, t...  8.73 us
  transfers between devices with their start and end apart: 31, of which 11 were waited for; matrix products, arithmetic and copies ran while one was open for 20% of the time, Pallas kernels for 12%

commit v1 on v0

--- a/solution.py
+++ b/solution.py
@@ -172,9 +172,10 @@
     total = jnp.sum(jnp.exp(logits - top[None, :]), axis=0)
     target = jnp.sum(jnp.where(hot, logits, 0.0), axis=0)
     stats = jnp.stack([top, total, target])
-    stats, hid_low, hid_high, pass_low, pass_high = tie((stats, hid_low, hid_high, pass_low, pass_high))
+    stats, hid_low, hid_high = tie((stats, hid_low, hid_high))
+    stats = lax.all_to_all(jnp.broadcast_to(stats[None], (32,) + stats.shape), "vocab", 0, 0)
+    stats, pass_low, pass_high = tie((stats, pass_low, pass_high))
     hid_far = [send_z(pass_low, 1), send_z(pass_high, -1)]
-    stats = lax.all_to_all(jnp.broadcast_to(stats[None], (32,) + stats.shape), "vocab", 0, 0)
     row_top = jnp.max(stats[:, 0], axis=0)
     exp_total = jnp.sum(stats[:, 1] * jnp.exp(stats[:, 0] - row_top[None]), axis=0)
     target_logit = jnp.sum(stats[:, 2], axis=0)

time: 186 us -> 182 us (0.978)
  blocking collectives: 15.1 us -> 0 us
  starting transfers between devices: 45.4 us -> 49.9 us
  waiting for transfers between devices: 47.7 us -> 51.9 us
  local copies, waits for them, and re-layouts: 27.6 us -> 30 us
    all_to_all x1 -> x0, blocking collectives: 15.1 us -> none  [body(): lax.all_to_all(jnp.broadcast_to(stats[None], (32,) + stats.shape), 'vocab...]
    all_to_all x0 -> x1, waiting for transfers between devices: none -> 11 us  [body(): lax.all_to_all(jnp.broadcast_to(stats[None], (32,) + stats.shape), 'vocab...]
    ppermute x9, waiting for transfers between devices: 37.5 us -> 30.7 us  [send_z(): return lax.ppermute(a, 'seq', [(i, (i + d) % 4) for i in range(4)])]
    all_to_all x0 -> x1, starting transfers between devices: none -> 5.04 us  [body(): lax.all_to_all(jnp.broadcast_to(stats[None], (32,) + stats.shape), 'vocab...]
  transfers between devices with their start and end apart: 31 -> 32, of which waited for: 11 -> 12; matrix products, arithmetic and copies ran while one was open for 20% -> 20% of each run, Pallas kernels for 12% -> 12%
where the time goes in v1:
time: 182 us; the launch traced here: 181 us
  waiting for transfers between devices  51.9 us (29%)
  starting transfers between devices  49.9 us (27%)
  local copies, waits for them, and re-layouts  30 us (16%)
  Pallas kernels  22.1 us (12%)
  between operations  14.6 us (8%)
  matrix products  6.61 us (4%)
  other arithmetic  5.87 us (3%)
    ppermute x9, waiting for transfers between devices, send_z(): return lax.ppermute(a, 'seq', [(i, (i + d) % 4) for i in range(4)])  30.7 us
    ppermute x9, starting transfers between devices, send_z(): return lax.ppermute(a, 'seq', [(i, (i + d) % 4) for i in range(4)])  16.2 us
    unnamed x24, local copies, waits for them, and re-layouts  14.6 us
    pallas_call x1, Pallas kernels, table_terms(): pl.pallas_call(table_kernel, out_shape=jax.ShapeDtypeStruct((4, 2, width,...  13.4 us
    all_to_all x1, waiting for transfers between devices, body(): lax.all_to_all(jnp.broadcast_to(stats[None], (32,) + stats.shape), 'vocab...  11 us
    ppermute x4, starting transfers between devices, send_y(): return lax.ppermute(a, 'vocab', vocab_perm(lambda y, x, c: (y + d, x, c)))  9.06 us
    ppermute x11, starting transfers between devices, send_core(): return lax.ppermute(a, 'vocab', vocab_perm(lambda y, x, c: (y, x, 1 - c)))  9.03 us
    pallas_call x1, Pallas kernels, hidden_terms(): pl.pallas_call(hidden_kernel, out_shape=[jax.ShapeDtypeStruct((columns, t...  8.75 us
  transfers between devices with their start and end apart: 32, of which 12 were waited for; matrix products, arithmetic and copies ran while one was open for 20% of the time, Pallas kernels for 12%

profile of v1, /device:TPU:1, one launch (start us, length us, event | category | flops | bytes accessed | tf_op | source)
XLA Modules:
  0.0 181.0 jit_solution(16209693851721613479)
XLA Ops:
  7.2 2.1 %collective-permute-start = (bf16[168,512]{1,0:T(8,128)(2,1)}, bf16[168,512]{1,0:T(8,128)(2,1)S(1)}, u32[]{:S(2)}, u32[]{:S(2)}) collective-permute-start(bf16[168,512]{1,0:T(8,128)(2,1)} %bitcast.101), channel_id=1, source_target_pairs={{0,2},{1,3},{2,4},{3,5},{4,6},{5,7},{6,0},{7,1},{8,10},{9,11},{10,... | collective-permute-start | bytes 516104 | tf_op jit(solution)/shard_map/ppermute | solution.py:20
  9.3 1.4 collective-permute-start.1
  10.7 0.7 fusion.8
  11.5 1.0 maximum_maximum_fusion
  12.5 0.7 collective-permute-start.4
  13.3 0.9 bitcast_dynamic-update-slice_fusion.3
  14.3 0.2 collective-permute-done.1
  14.5 2.6 %collective-permute-start.3 = (bf16[168,256]{1,0:T(8,128)(2,1)S(1)}, bf16[168,256]{1,0:T(8,128)(2,1)S(1)}, u32[]{:S(2)}, u32[]{:S(2)}) collective-permute-start(bf16[168,256]{1,0:T(8,128)(2,1)S(1)} %slice.110), channel_id=1, source_target_pairs={{0,6},{1,7},{2,0},{3,1},{4,2},{5,3},{6,4},{7,5},{8,14},{9,15},{10,... | collective-permute-start | bytes 258056 | tf_op jit(solution)/shard_map/ppermute | solution.py:20
  17.2 1.4 collective-permute-done.3
  18.6 3.1 %collective-permute-done.2 = bf16[168,256]{1,0:T(8,128)(2,1)S(1)} collective-permute-done((bf16[168,256]{1,0:T(8,128)(2,1)S(1)}, bf16[168,256]{1,0:T(8,128)(2,1)S(1)}, u32[]{:S(2)}, u32[]{:S(2)}) %collective-permute-start.2) | collective-permute-done | bytes 86048 | tf_op jit(solution)/shard_map/ppermute | solution.py:20
  21.7 2.8 %collective-permute-start.5 = (bf16[4,168,512]{2,1,0:T(8,128)(2,1)S(1)}, bf16[4,168,512]{2,1,0:T(8,128)(2,1)}, u32[]{:S(2)}, u32[]{:S(2)}) collective-permute-start(bf16[4,168,512]{2,1,0:T(8,128)(2,1)S(1)} %fusion.5), channel_id=1, source_target_pairs={{0,8},{1,9},{2,10},{3,11},{4,12},{5,13},{6,14},{7,15},{8,16},{9,17... | collective-permute-start | bytes 2064392 | tf_op jit(solution)/shard_map/ppermute | solution.py:24
  24.5 4.1 %collective-permute-start.6 = (bf16[4,168,512]{2,1,0:T(8,128)(2,1)S(1)}, bf16[4,168,512]{2,1,0:T(8,128)(2,1)}, u32[]{:S(2)}, u32[]{:S(2)}) collective-permute-start(bf16[4,168,512]{2,1,0:T(8,128)(2,1)S(1)} %fusion.5), channel_id=1, source_target_pairs={{0,24},{1,25},{2,26},{3,27},{4,28},{5,29},{6,30},{7,31},{8,0},{9,1... | collective-permute-start | bytes 2064392 | tf_op jit(solution)/shard_map/ppermute | solution.py:24
  28.7 11.8 %copy.15 = bf16[768,5376]{0,1:T(8,128)(2,1)} copy(bf16[768,5376]{1,0:T(8,128)(2,1)} %param.8) | data formatting | bytes 16515072 | tf_op args[2]
  40.5 0.2 broadcast_in_dim.56
  40.8 1.0 collective-permute-done.5
  41.8 1.5 slice.87
  43.3 2.1 %collective-permute-start.8 = (bf16[4,168,256]{2,1,0:T(8,128)(2,1)S(1)}, bf16[4,168,256]{2,1,0:T(8,128)(2,1)S(1)}, u32[]{:S(2)}, u32[]{:S(2)}) collective-permute-start(bf16[4,168,256]{2,1,0:T(8,128)(2,1)S(1)} %slice.87), channel_id=1, source_target_pairs={{0,24},{1,25},{2,26},{3,27},{4,28},{5,29},{6,30},{7,31},{8,0},{9,1... | collective-permute-start | bytes 1032200 | tf_op jit(solution)/shard_map/ppermute | solution.py:24
  45.4 1.0 slice.86
  46.4 1.2 bitcast_dynamic-update-slice_fusion.1
  47.6 1.2 bitcast_dynamic-update-slice_fusion
  48.8 3.8 %constant_dynamic-slice_fusion.4 = (bf16[16,1,168,768]{3,2,1,0:T(8,128)(2,1)}, bf16[16,1,168,768]{3,2,1,0:T(8,128)(2,1)}) fusion(bf16[16,2,168,768]{3,2,1,0:T(8,128)(2,1)S(1)} %bitcast.86, s32[]{:T(128)S(6)} %select_n.153, s32[]{:T(128)S(6)} %select_n.152), kind=kLoop, calls=%fused_computation.37 | loop fusion | bytes 16515080 | tf_op jit(solution)/shard_map/jit(dynamic_index_in_dim)/dynamic_slice | solution.py:154
  52.6 1.1 collective-permute-done.7
  53.8 5.0 %collective-permute-start.10 = (bf16[2688,512]{1,0:T(8,128)(2,1)S(1)}, bf16[2688,512]{1,0:T(8,128)(2,1)}, u32[]{:S(2)}, u32[]{:S(2)}) collective-permute-start(bf16[2688,512]{1,0:T(8,128)(2,1)S(1)} %bitcast.87), channel_id=1, source_target_pairs={{0,1},{1,0},{2,3},{3,2},{4,5},{5,4},{6,7},{7,6},{8,9},{9,8},{10,11... | collective-permute-start | bytes 8257544 | tf_op jit(solution)/shard_map/ppermute | solution.py:28
  59.0 1.1 constant_dynamic-slice_fusion
  60.2 1.2 collective-permute-start.11
  61.4 5.8 %collective-permute-start.12 = (bf16[672,512]{1,0:T(8,128)(2,1)S(1)}, bf16[672,512]{1,0:T(8,128)(2,1)S(1)}, u32[]{:S(2)}, u32[]{:S(2)}) collective-permute-start(bf16[672,512]{1,0:T(8,128)(2,1)S(1)} %bitcast.98), channel_id=1, source_target_pairs={{0,96},{32,0},{64,32},{96,64},{1,97},{33,1},{65,33},{97,65},{2,98}... | collective-permute-start | bytes 2064392 | tf_op jit(solution)/shard_map/ppermute | solution.py:32
  67.3 2.4 %fusion.23 = f32[768,512]{1,0:T(8,128)S(1)} fusion(bf16[2688,768]{1,0:T(8,128)(2,1)S(1)} %bitcast.90, bf16[2688,512]{1,0:T(8,128)(2,1)S(1)} %bitcast.88), kind=kOutput, calls=%fused_computation.75 | convolution fusion | flops 2113929216 | bytes 8454144 | tf_op jit(solution)/shard_map/dot_general | solution.py:139
  69.7 2.9 %collective-permute-start.14 = (bf16[672,256]{1,0:T(8,128)(2,1)S(1)}, bf16[672,256]{1,0:T(8,128)(2,1)}, u32[]{:S(2)}, u32[]{:S(2)}) collective-permute-start(bf16[672,256]{1,0:T(8,128)(2,1)S(1)} %get-tuple-element.75), channel_id=1, source_target_pairs={{0,96},{32,0},{64,32},{96,64},{1,97},{33,1},{65,33},{97,65},{2,98}... | collective-permute-start | bytes 1032200 | tf_op jit(solution)/shard_map/ppermute | solution.py:32
  72.6 4.2 %fusion.24 = f32[768,512]{1,0:T(8,128)S(1)} fusion(bf16[2688,768]{1,0:T(8,128)(2,1)S(1)} %bitcast.92, bf16[2688,512]{1,0:T(8,128)(2,1)} %collective-permute-done.10), kind=kOutput, calls=%fused_computation.76 | convolution fusion | flops 2113929216 | bytes 8454144 | tf_op jit(solution)/shard_map/dot_general | solution.py:139
  76.8 0.4 fusion.20
  77.2 0.2 copy-done.5
  77.5 0.4 exponential_reduce_fusion
  77.9 4.7 %collective-permute-done.11.refs_10_ = bf16[672,512]{1,0:T(8,128)(2,1)S(1)} collective-permute-done((bf16[672,512]{1,0:T(8,128)(2,1)S(1)}, bf16[672,512]{1,0:T(8,128)(2,1)S(1)}, u32[]{:S(2)}, u32[]{:S(2)}) %collective-permute-start.11) | collective-permute-done | bytes 688160 | tf_op jit(solution)/shard_map/ppermute | solution.py:32
  82.6 0.9 copy-done.8
  83.5 0.8 copy-done.9
  84.3 0.7 broadcast_in_dim.68
  85.0 5.0 %all-to-all-start = ((f32[32,3,512]{2,1,0:T(4,128)}), f32[32,3,512]{2,1,0:T(4,128)S(1)}, u32[]{:S(2)}, u32[]{:S(2)}) async-start(f32[32,3,512]{2,1,0:T(4,128)} %broadcast_in_dim.68), calls=%async_computation | async-start | bytes 524288 | tf_op jit(solution)/shard_map/all_to_all | solution.py:176
  90.1 11.0 %all-to-all-done = f32[32,3,512]{2,1,0:T(4,128)S(1)} async-done(((f32[32,3,512]{2,1,0:T(4,128)}), f32[32,3,512]{2,1,0:T(4,128)S(1)}, u32[]{:S(2)}, u32[]{:S(2)}) %all-to-all-start) | async-done | bytes 196640 | tf_op jit(solution)/shard_map/all_to_all | solution.py:176
  101.2 0.1 fusion.22
  101.3 0.6 fusion.19
  101.9 1.3 fusion.3.g_ref
  103.2 1.2 collective-permute-start.15
  104.5 2.7 %collective-permute-start.17 = (bf16[768,512]{1,0:T(8,128)(2,1)}, bf16[768,512]{1,0:T(8,128)(2,1)}, u32[]{:S(2)}, u32[]{:S(2)}) collective-permute-start(bf16[768,512]{1,0:T(8,128)(2,1)} %fusion.3.g_ref), channel_id=1, source_target_pairs={{0,96},{32,0},{64,32},{96,64},{1,97},{33,1},{65,33},{97,65},{2,98}... | collective-permute-start | bytes 2359304 | tf_op jit(solution)/shard_map/ppermute | solution.py:32
  107.1 0.9 collective-permute-start.18
  108.2 2.7 %collective-permute-start.20 = (bf16[672,256]{1,0:T(8,128)(2,1)}, bf16[672,256]{1,0:T(8,128)(2,1)}, u32[]{:S(2)}, u32[]{:S(2)}) collective-permute-start(bf16[672,256]{1,0:T(8,128)(2,1)} %collective-permute-done.14), channel_id=1, source_target_pairs={{0,96},{32,0},{64,32},{96,64},{1,97},{33,1},{65,33},{97,65},{2,98}... | collective-permute-start | bytes 1032200 | tf_op jit(solution)/shard_map/ppermute | solution.py:32
  110.8 8.7 %hidden_terms.1 = (bf16[2688,512]{1,0:T(8,128)(2,1)}, bf16[768,512]{1,0:T(8,128)(2,1)}) custom-call(bf16[2688,768]{1,0:T(8,128)(2,1)} %bitcast.89, bf16[2688,768]{1,0:T(8,128)(2,1)} %collective-permute-done.9.pair_ref, bf16[768,512]{1,0:T(8,128)(2,1)} %fusion.3.g_ref, bf16[768,512]{1,0:T(8,128)(2,1)} %copy-done.7), custom_call_target="tpu_custom_call" | custom-call | flops 4294967296 | bytes 12582912 | tf_op jit(solution)/shard_map/hidden_terms/pallas_call | solution.py:79
  119.6 3.7 %all-to-all-start.1 = ((bf16[16,168,512]{2,1,0:T(8,128)(2,1)}), bf16[16,168,512]{2,1,0:T(8,128)(2,1)S(1)}, u32[]{:S(2)}, u32[]{:S(2)}) async-start(bf16[16,168,512]{2,1,0:T(8,128)(2,1)} %bitcast.95), calls=%async_computation.1 | async-start | bytes 5505024 | tf_op jit(solution)/shard_map/all_to_all | solution.py:190
  123.3 26.0 %collective-permute-done.19 = bf16[672,256]{1,0:T(8,128)(2,1)S(1)} collective-permute-done((bf16[672,256]{1,0:T(8,128)(2,1)}, bf16[672,256]{1,0:T(8,128)(2,1)S(1)}, u32[]{:S(2)}, u32[]{:S(2)}) %collective-permute-start.19) | collective-permute-done | bytes 344096 | tf_op jit(solution)/shard_map/ppermute | solution.py:32
  149.3 0.8 collective-permute-start.25
  150.1 0.5 collective-permute-start.27
  150.6 2.1 %dynamic-slice_bitcast_fusion = (bf16[4,176,512]{2,1,0:T(8,128)(2,1)S(1)}, bf16[4,176,512]{2,1,0:T(8,128)(2,1)S(1)}, bf16[4,176,512]{2,1,0:T(8,128)(2,1)S(1)}, bf16[4,176,512]{2,1,0:T(8,128)(2,1)S(1)}) fusion(bf16[4,4,176,512]{3,2,1,0:T(8,128)(2,1)} %bitcast.93, s32[]{:T(128)S(6)} %select_n.160, s32[]{:T(128)S(6)} %select_n.156, s32[]{:T(128)S(6)} %select_n.158, ...), kind=kLoop, calls=%fused_computation.7 | loop fusion | bytes 5767184 | tf_op jit(solution)/shard_map/jit(dynamic_index_in_dim)/squeeze | solution.py:197
  152.7 0.2 collective-permute-start.21
  152.9 0.5 collective-permute-start.22
  153.5 1.0 constant_dynamic-update-slice_fusion.refs_14_
  154.6 0.2 collective-permute-start.23
  154.8 0.4 collective-permute-start.24
  155.2 0.1 collective-permute-start.28
  155.4 0.5 collective-permute-done.22.refs_3_
  155.9 1.0 collective-permute-done.23.refs_5_
  156.9 1.0 collective-permute-done.24.refs_7_
  157.9 1.0 collective-permute-done.28.refs_15_
  158.9 0.8 copy-done.10
  159.7 13.4 %table_terms.1 = f32[4,2,168,768]{3,2,1,0:T(8,128)} custom-call(s32[1]{0:T(128)} %bitcast.23.core_ref, bf16[672,512]{1,0:T(8,128)(2,1)S(1)} %bitcast.79, bf16[672,512]{1,0:T(8,128)(2,1)S(1)} %collective-permute-done.21.refs_1_, bf16[672,512]{1,0:T(8,128)(2,1)S(1)} %bitcast.81, bf16[672,512]{1,0:T(8,128)(2,1)S(1)} %collective-permute-done.22.refs_3_, ...), custom_call_target="tpu_custom_call" | custom-call | flops 8589934592 | bytes 16777216 | tf_op jit(solution)/shard_map/table_terms/pallas_call | solution.py:111
  173.1 1.1 reduce_sum.51
  (79 shorter events, 1.3 us)
Async XLA Ops:
  7.2 143.4 %all-gather.3.cloned.1.call-start = ((), (), s32[]{:S(2)}) async-start(), calls=%async_computation.2 | async-start | bytes 3063808 | tf_op jit(solution)/shard_map/all_gather | solution.py:157
  7.2 9.8 %collective-permute-start = (bf16[168,512]{1,0:T(8,128)(2,1)}, bf16[168,512]{1,0:T(8,128)(2,1)S(1)}, u32[]{:S(2)}, u32[]{:S(2)}) collective-permute-start(bf16[168,512]{1,0:T(8,128)(2,1)} %bitcast.101), channel_id=1, source_target_pairs={{0,2},{1,3},{2,4},{3,5},{4,6},{5,7},{6,0},{7,1},{8,10},{9,11},{10,... | collective-permute-start | bytes 516104 | tf_op jit(solution)/shard_map/ppermute | solution.py:20
  9.3 5.1 %collective-permute-start.1 = (bf16[168,512]{1,0:T(8,128)(2,1)}, bf16[168,512]{1,0:T(8,128)(2,1)S(1)}, u32[]{:S(2)}, u32[]{:S(2)}) collective-permute-start(bf16[168,512]{1,0:T(8,128)(2,1)} %bitcast.102), channel_id=1, source_target_pairs={{0,6},{1,7},{2,0},{3,1},{4,2},{5,3},{6,4},{7,5},{8,14},{9,15},{10,... | collective-permute-start | bytes 516104 | tf_op jit(solution)/shard_map/ppermute | solution.py:20
  12.5 9.2 %collective-permute-start.4 = (bf16[176,512]{1,0:T(8,128)(2,1)S(1)}, bf16[176,512]{1,0:T(8,128)(2,1)S(1)}, u32[]{:S(2)}, u32[]{:S(2)}) collective-permute-start(bf16[176,512]{1,0:T(8,128)(2,1)S(1)} %maximum_maximum_fusion), channel_id=1, source_target_pairs={{0,0},{1,1},{2,2},{3,3},{4,4},{5,5},{6,6},{7,7},{8,32},{9,33},{10,... | collective-permute-start | bytes 540680 | tf_op jit(solution)/shard_map/ppermute | solution.py:40
  14.5 4.1 %collective-permute-start.3 = (bf16[168,256]{1,0:T(8,128)(2,1)S(1)}, bf16[168,256]{1,0:T(8,128)(2,1)S(1)}, u32[]{:S(2)}, u32[]{:S(2)}) collective-permute-start(bf16[168,256]{1,0:T(8,128)(2,1)S(1)} %slice.110), channel_id=1, source_target_pairs={{0,6},{1,7},{2,0},{3,1},{4,2},{5,3},{6,4},{7,5},{8,14},{9,15},{10,... | collective-permute-start | bytes 258056 | tf_op jit(solution)/shard_map/ppermute | solution.py:20
  17.1 4.6 %collective-permute-start.2 = (bf16[168,256]{1,0:T(8,128)(2,1)S(1)}, bf16[168,256]{1,0:T(8,128)(2,1)S(1)}, u32[]{:S(2)}, u32[]{:S(2)}) collective-permute-start(bf16[168,256]{1,0:T(8,128)(2,1)S(1)} %slice.109), channel_id=1, source_target_pairs={{0,2},{1,3},{2,4},{3,5},{4,6},{5,7},{6,0},{7,1},{8,10},{9,11},{10,... | collective-permute-start | bytes 258056 | tf_op jit(solution)/shard_map/ppermute | solution.py:20
  21.7 18.8 %copy-start.3 = (bf16[176,512]{1,0:T(8,128)(2,1)}, bf16[176,512]{1,0:T(8,128)(2,1)S(1)}, u32[]{:S(2)}) copy-start(bf16[176,512]{1,0:T(8,128)(2,1)S(1)} %collective-permute-done.4) | copy-start | bytes 540676
  21.7 20.0 %collective-permute-start.5 = (bf16[4,168,512]{2,1,0:T(8,128)(2,1)S(1)}, bf16[4,168,512]{2,1,0:T(8,128)(2,1)}, u32[]{:S(2)}, u32[]{:S(2)}) collective-permute-start(bf16[4,168,512]{2,1,0:T(8,128)(2,1)S(1)} %fusion.5), channel_id=1, source_target_pairs={{0,8},{1,9},{2,10},{3,11},{4,12},{5,13},{6,14},{7,15},{8,16},{9,17... | collective-permute-start | bytes 2064392 | tf_op jit(solution)/shard_map/ppermute | solution.py:24
  24.5 17.2 %collective-permute-start.6 = (bf16[4,168,512]{2,1,0:T(8,128)(2,1)S(1)}, bf16[4,168,512]{2,1,0:T(8,128)(2,1)}, u32[]{:S(2)}, u32[]{:S(2)}) collective-permute-start(bf16[4,168,512]{2,1,0:T(8,128)(2,1)S(1)} %fusion.5), channel_id=1, source_target_pairs={{0,24},{1,25},{2,26},{3,27},{4,28},{5,29},{6,30},{7,31},{8,0},{9,1... | collective-permute-start | bytes 2064392 | tf_op jit(solution)/shard_map/ppermute | solution.py:24
  40.5 8.3 %copy-start = (bf16[768,5376]{0,1:T(8,128)(2,1)S(1)}, bf16[768,5376]{0,1:T(8,128)(2,1)}, u32[]{:S(2)}) copy-start(bf16[768,5376]{0,1:T(8,128)(2,1)} %copy.15) | copy-start | bytes 24772612
  43.3 9.3 %collective-permute-start.8 = (bf16[4,168,256]{2,1,0:T(8,128)(2,1)S(1)}, bf16[4,168,256]{2,1,0:T(8,128)(2,1)S(1)}, u32[]{:S(2)}, u32[]{:S(2)}) collective-permute-start(bf16[4,168,256]{2,1,0:T(8,128)(2,1)S(1)} %slice.87), channel_id=1, source_target_pairs={{0,24},{1,25},{2,26},{3,27},{4,28},{5,29},{6,30},{7,31},{8,0},{9,1... | collective-permute-start | bytes 1032200 | tf_op jit(solution)/shard_map/ppermute | solution.py:24
  46.4 7.4 %collective-permute-start.7 = (bf16[4,168,256]{2,1,0:T(8,128)(2,1)S(1)}, bf16[4,168,256]{2,1,0:T(8,128)(2,1)S(1)}, u32[]{:S(2)}, u32[]{:S(2)}) collective-permute-start(bf16[4,168,256]{2,1,0:T(8,128)(2,1)S(1)} %slice.86), channel_id=1, source_target_pairs={{0,8},{1,9},{2,10},{3,11},{4,12},{5,13},{6,14},{7,15},{8,16},{9,17... | collective-permute-start | bytes 1032200 | tf_op jit(solution)/shard_map/ppermute | solution.py:24
  53.8 15.9 %collective-permute-start.10 = (bf16[2688,512]{1,0:T(8,128)(2,1)S(1)}, bf16[2688,512]{1,0:T(8,128)(2,1)}, u32[]{:S(2)}, u32[]{:S(2)}) collective-permute-start(bf16[2688,512]{1,0:T(8,128)(2,1)S(1)} %bitcast.87), channel_id=1, source_target_pairs={{0,1},{1,0},{2,3},{3,2},{4,5},{5,4},{6,7},{7,6},{8,9},{9,8},{10,11... | collective-permute-start | bytes 8257544 | tf_op jit(solution)/shard_map/ppermute | solution.py:28
  58.9 8.4 %copy-start.1 = (bf16[16,1,168,768]{3,2,1,0:T(8,128)(2,1)S(1)}, bf16[16,1,168,768]{3,2,1,0:T(8,128)(2,1)}, u32[]{:S(2)}) copy-start(bf16[16,1,168,768]{3,2,1,0:T(8,128)(2,1)} %get-tuple-element.66) | copy-start | bytes 12386308
  58.9 49.2 %collective-permute-start.9 = (bf16[2688,768]{1,0:T(8,128)(2,1)}, bf16[2688,768]{1,0:T(8,128)(2,1)}, u32[]{:S(2)}, u32[]{:S(2)}) collective-permute-start(bf16[2688,768]{1,0:T(8,128)(2,1)} %bitcast.91), channel_id=1, source_target_pairs={{0,1},{1,0},{2,3},{3,2},{4,5},{5,4},{6,7},{7,6},{8,9},{9,8},{10,11... | collective-permute-start | bytes 12386312 | tf_op jit(solution)/shard_map/ppermute | solution.py:28
  60.2 22.4 %collective-permute-start.11 = (bf16[672,512]{1,0:T(8,128)(2,1)S(1)}, bf16[672,512]{1,0:T(8,128)(2,1)S(1)}, u32[]{:S(2)}, u32[]{:S(2)}) collective-permute-start(bf16[672,512]{1,0:T(8,128)(2,1)S(1)} %bitcast.99), channel_id=1, source_target_pairs={{0,32},{32,64},{64,96},{96,0},{1,33},{33,65},{65,97},{97,1},{2,34}... | collective-permute-start | bytes 2064392 | tf_op jit(solution)/shard_map/ppermute | solution.py:32
  61.4 21.2 %collective-permute-start.12 = (bf16[672,512]{1,0:T(8,128)(2,1)S(1)}, bf16[672,512]{1,0:T(8,128)(2,1)S(1)}, u32[]{:S(2)}, u32[]{:S(2)}) collective-permute-start(bf16[672,512]{1,0:T(8,128)(2,1)S(1)} %bitcast.98), channel_id=1, source_target_pairs={{0,96},{32,0},{64,32},{96,64},{1,97},{33,1},{65,33},{97,65},{2,98}... | collective-permute-start | bytes 2064392 | tf_op jit(solution)/shard_map/ppermute | solution.py:32
  67.2 5.4 %copy-start.2 = (bf16[16,1,168,768]{3,2,1,0:T(8,128)(2,1)S(1)}, bf16[16,1,168,768]{3,2,1,0:T(8,128)(2,1)}, u32[]{:S(2)}) copy-start(bf16[16,1,168,768]{3,2,1,0:T(8,128)(2,1)} %get-tuple-element.65) | copy-start | bytes 12386308
  67.2 22.9 %collective-permute-start.13 = (bf16[672,256]{1,0:T(8,128)(2,1)S(1)}, bf16[672,256]{1,0:T(8,128)(2,1)}, u32[]{:S(2)}, u32[]{:S(2)}) collective-permute-start(bf16[672,256]{1,0:T(8,128)(2,1)S(1)} %get-tuple-element.76), channel_id=1, source_target_pairs={{0,32},{32,64},{64,96},{96,0},{1,33},{33,65},{65,97},{97,1},{2,34}... | collective-permute-start | bytes 1032200 | tf_op jit(solution)/shard_map/ppermute | solution.py:32
  69.7 20.4 %collective-permute-start.14 = (bf16[672,256]{1,0:T(8,128)(2,1)S(1)}, bf16[672,256]{1,0:T(8,128)(2,1)}, u32[]{:S(2)}, u32[]{:S(2)}) collective-permute-start(bf16[672,256]{1,0:T(8,128)(2,1)S(1)} %get-tuple-element.75), channel_id=1, source_target_pairs={{0,96},{32,0},{64,32},{96,64},{1,97},{33,1},{65,33},{97,65},{2,98}... | collective-permute-start | bytes 1032200 | tf_op jit(solution)/shard_map/ppermute | solution.py:32
  76.8 0.7 copy-start.5
  77.2 24.7 %copy-start.6 = (f32[512]{0:T(512)S(1)}, f32[512]{0:T(512)}, u32[]{:S(2)}) copy-start(f32[512]{0:T(512)} %param.11) | copy-start | bytes 6148
  82.6 0.9 copy-start.8
  83.5 0.8 copy-start.9
  85.0 16.0 %all-to-all-start = ((f32[32,3,512]{2,1,0:T(4,128)}), f32[32,3,512]{2,1,0:T(4,128)S(1)}, u32[]{:S(2)}, u32[]{:S(2)}) async-start(f32[32,3,512]{2,1,0:T(4,128)} %broadcast_in_dim.68), calls=%async_computation | async-start | bytes 524288 | tf_op jit(solution)/shard_map/all_to_all | solution.py:176
  103.2 4.8 %collective-permute-start.15 = (bf16[768,512]{1,0:T(8,128)(2,1)}, bf16[768,512]{1,0:T(8,128)(2,1)S(1)}, u32[]{:S(2)}, u32[]{:S(2)}) collective-permute-start(bf16[768,512]{1,0:T(8,128)(2,1)} %fusion.3.g_ref), channel_id=1, source_target_pairs={{0,1},{1,0},{2,3},{3,2},{4,5},{5,4},{6,7},{7,6},{8,9},{9,8},{10,11... | collective-permute-start | bytes 2359304 | tf_op jit(solution)/shard_map/ppermute | solution.py:28
  104.5 45.6 %collective-permute-start.16 = (bf16[768,512]{1,0:T(8,128)(2,1)}, bf16[768,512]{1,0:T(8,128)(2,1)}, u32[]{:S(2)}, u32[]{:S(2)}) collective-permute-start(bf16[768,512]{1,0:T(8,128)(2,1)} %fusion.3.g_ref), channel_id=1, source_target_pairs={{0,32},{32,64},{64,96},{96,0},{1,33},{33,65},{65,97},{97,1},{2,34}... | collective-permute-start | bytes 2359304 | tf_op jit(solution)/shard_map/ppermute | solution.py:32
  104.5 46.1 %collective-permute-start.17 = (bf16[768,512]{1,0:T(8,128)(2,1)}, bf16[768,512]{1,0:T(8,128)(2,1)}, u32[]{:S(2)}, u32[]{:S(2)}) collective-permute-start(bf16[768,512]{1,0:T(8,128)(2,1)} %fusion.3.g_ref), channel_id=1, source_target_pairs={{0,96},{32,0},{64,32},{96,64},{1,97},{33,1},{65,33},{97,65},{2,98}... | collective-permute-start | bytes 2359304 | tf_op jit(solution)/shard_map/ppermute | solution.py:32
  107.1 43.5 %collective-permute-start.18 = (bf16[768,512]{1,0:T(8,128)(2,1)}, bf16[768,512]{1,0:T(8,128)(2,1)}, u32[]{:S(2)}, u32[]{:S(2)}) collective-permute-start(bf16[768,512]{1,0:T(8,128)(2,1)} %fusion.3.g_ref), channel_id=1, source_target_pairs={{0,64},{32,96},{64,0},{96,32},{1,65},{33,97},{65,1},{97,33},{2,66}... | collective-permute-start | bytes 2359304 | tf_op jit(solution)/shard_map/ppermute | solution.py:32
  108.1 2.8 %copy-start.7 = (bf16[768,512]{1,0:T(8,128)(2,1)}, bf16[768,512]{1,0:T(8,128)(2,1)S(1)}, u32[]{:S(2)}) copy-start(bf16[768,512]{1,0:T(8,128)(2,1)S(1)} %collective-permute-done.15.pg_ref) | copy-start | bytes 2359300
  108.1 41.2 %collective-permute-start.19 = (bf16[672,256]{1,0:T(8,128)(2,1)}, bf16[672,256]{1,0:T(8,128)(2,1)S(1)}, u32[]{:S(2)}, u32[]{:S(2)}) collective-permute-start(bf16[672,256]{1,0:T(8,128)(2,1)} %collective-permute-done.13), channel_id=1, source_target_pairs={{0,32},{32,64},{64,96},{96,0},{1,33},{33,65},{65,97},{97,1},{2,34}... | collective-permute-start | bytes 1032200 | tf_op jit(solution)/shard_map/ppermute | solution.py:32
  108.2 41.9 %collective-permute-start.20 = (bf16[672,256]{1,0:T(8,128)(2,1)}, bf16[672,256]{1,0:T(8,128)(2,1)}, u32[]{:S(2)}, u32[]{:S(2)}) collective-permute-start(bf16[672,256]{1,0:T(8,128)(2,1)} %collective-permute-done.14), channel_id=1, source_target_pairs={{0,96},{32,0},{64,32},{96,64},{1,97},{33,1},{65,33},{97,65},{2,98}... | collective-permute-start | bytes 1032200 | tf_op jit(solution)/shard_map/ppermute | solution.py:32
  119.6 53.5 %all-to-all-start.1 = ((bf16[16,168,512]{2,1,0:T(8,128)(2,1)}), bf16[16,168,512]{2,1,0:T(8,128)(2,1)S(1)}, u32[]{:S(2)}, u32[]{:S(2)}) async-start(bf16[16,168,512]{2,1,0:T(8,128)(2,1)} %bitcast.95), calls=%async_computation.1 | async-start | bytes 5505024 | tf_op jit(solution)/shard_map/all_to_all | solution.py:190
  149.3 5.4 %collective-permute-start.25 = (bf16[672,512]{1,0:T(8,128)(2,1)}, bf16[672,512]{1,0:T(8,128)(2,1)}, u32[]{:S(2)}, u32[]{:S(2)}) collective-permute-start(bf16[672,512]{1,0:T(8,128)(2,1)} %bitcast.96), channel_id=1, source_target_pairs={{0,1},{1,0},{2,3},{3,2},{4,5},{5,4},{6,7},{7,6},{8,9},{9,8},{10,11... | collective-permute-start | bytes 2064392 | tf_op jit(solution)/shard_map/ppermute | solution.py:28
  150.1 4.7 %collective-permute-start.26 = (bf16[672,512]{1,0:T(8,128)(2,1)}, bf16[672,512]{1,0:T(8,128)(2,1)}, u32[]{:S(2)}, u32[]{:S(2)}) collective-permute-start(bf16[672,512]{1,0:T(8,128)(2,1)} %copy-done.8), channel_id=1, source_target_pairs={{0,1},{1,0},{2,3},{3,2},{4,5},{5,4},{6,7},{7,6},{8,9},{9,8},{10,11... | collective-permute-start | bytes 2064392 | tf_op jit(solution)/shard_map/ppermute | solution.py:28
  150.1 5.2 %collective-permute-start.27 = (bf16[672,512]{1,0:T(8,128)(2,1)}, bf16[672,512]{1,0:T(8,128)(2,1)}, u32[]{:S(2)}, u32[]{:S(2)}) collective-permute-start(bf16[672,512]{1,0:T(8,128)(2,1)} %copy-done.9), channel_id=1, source_target_pairs={{0,1},{1,0},{2,3},{3,2},{4,5},{5,4},{6,7},{7,6},{8,9},{9,8},{10,11... | collective-permute-start | bytes 2064392 | tf_op jit(solution)/shard_map/ppermute | solution.py:28
  152.7 2.7 %collective-permute-start.21 = (bf16[672,512]{1,0:T(8,128)(2,1)S(1)}, bf16[672,512]{1,0:T(8,128)(2,1)S(1)}, u32[]{:S(2)}, u32[]{:S(2)}) collective-permute-start(bf16[672,512]{1,0:T(8,128)(2,1)S(1)} %bitcast.78), channel_id=1, source_target_pairs={{0,1},{1,0},{2,3},{3,2},{4,5},{5,4},{6,7},{7,6},{8,9},{9,8},{10,11... | collective-permute-start | bytes 2064392 | tf_op jit(solution)/shard_map/ppermute | solution.py:28
  152.9 3.0 %collective-permute-start.22 = (bf16[672,512]{1,0:T(8,128)(2,1)S(1)}, bf16[672,512]{1,0:T(8,128)(2,1)S(1)}, u32[]{:S(2)}, u32[]{:S(2)}) collective-permute-start(bf16[672,512]{1,0:T(8,128)(2,1)S(1)} %bitcast.80), channel_id=1, source_target_pairs={{0,1},{1,0},{2,3},{3,2},{4,5},{5,4},{6,7},{7,6},{8,9},{9,8},{10,11... | collective-permute-start | bytes 2064392 | tf_op jit(solution)/shard_map/ppermute | solution.py:28
  154.5 4.4 %copy-start.4 = (bf16[672,512]{1,0:T(8,128)(2,1)}, bf16[672,512]{1,0:T(8,128)(2,1)S(1)}, u32[]{:S(2)}) copy-start(bf16[672,512]{1,0:T(8,128)(2,1)S(1)} %constant_dynamic-update-slice_fusion.refs_14_) | copy-start | bytes 2064388
  154.6 2.3 %collective-permute-start.23 = (bf16[672,512]{1,0:T(8,128)(2,1)S(1)}, bf16[672,512]{1,0:T(8,128)(2,1)S(1)}, u32[]{:S(2)}, u32[]{:S(2)}) collective-permute-start(bf16[672,512]{1,0:T(8,128)(2,1)S(1)} %bitcast.82), channel_id=1, source_target_pairs={{0,1},{1,0},{2,3},{3,2},{4,5},{5,4},{6,7},{7,6},{8,9},{9,8},{10,11... | collective-permute-start | bytes 2064392 | tf_op jit(solution)/shard_map/ppermute | solution.py:28
  154.8 3.1 %collective-permute-start.24 = (bf16[672,512]{1,0:T(8,128)(2,1)S(1)}, bf16[672,512]{1,0:T(8,128)(2,1)S(1)}, u32[]{:S(2)}, u32[]{:S(2)}) collective-permute-start(bf16[672,512]{1,0:T(8,128)(2,1)S(1)} %bitcast.84), channel_id=1, source_target_pairs={{0,1},{1,0},{2,3},{3,2},{4,5},{5,4},{6,7},{7,6},{8,9},{9,8},{10,11... | collective-permute-start | bytes 2064392 | tf_op jit(solution)/shard_map/ppermute | solution.py:28
  155.2 3.6 %collective-permute-start.28 = (bf16[672,512]{1,0:T(8,128)(2,1)S(1)}, bf16[672,512]{1,0:T(8,128)(2,1)S(1)}, u32[]{:S(2)}, u32[]{:S(2)}) collective-permute-start(bf16[672,512]{1,0:T(8,128)(2,1)S(1)} %constant_dynamic-update-slice_fusion.refs_14_), channel_id=1, source_target_pairs={{0,1},{1,0},{2,3},{3,2},{4,5},{5,4},{6,7},{7,6},{8,9},{9,8},{10,11... | collective-permute-start | bytes 2064392 | tf_op jit(solution)/shard_map/ppermute | solution.py:28
  158.9 0.8 copy-start.10
Sparse Core Ops, SparseCore 0:
  59.0 50.5 all-gather.2

commit v2 on v0

--- a/solution.py
+++ b/solution.py
@@ -91,38 +91,66 @@
 NT = (((1,), (1,)), ((), ()))
 
 
-def table_kernel(core_ref, *refs):
-    cots, hids, grads = refs[:8], refs[8:16], refs[18:22]
-    ids_ref, entry_ref, out_ref = refs[16], refs[17], refs[22]
-    width, tile = out_ref.shape[2:]
+def near_kernel(*refs):
+    cots, hids, grads = refs[:8], refs[8:14], refs[16:19]
+    ids_ref, entry_ref, acc_ref = refs[14], refs[15], refs[19]
     hots = [(ids_ref[k] == entry_ref[...]).astype(F32).astype(BF) for k in range(4)]
     for core in range(2):
-        total = jnp.zeros((4 * width, tile), F32)
-        for k in range(4):
+        total = lax.dot_general(cots[core][...], hots[0], NT, preferred_element_type=F32)
+        for k in range(1, 4):
             total += lax.dot_general(cots[2 * k + core][...], hots[k], NT, preferred_element_type=F32)
+        for k in range(3):
             total += lax.dot_general(hids[2 * k + core][...], grads[k][...], NT, preferred_element_type=F32)
+        acc_ref[core] = total
+
+
+def near_terms(cots, hids, ids, entry, grads):
+    rows, tokens = grads[0].shape
+    columns, tile = cots[0].shape[0], 256
+    return pl.pallas_call(
+        near_kernel,
+        out_shape=jax.ShapeDtypeStruct((2, columns, rows), F32),
+        grid=(rows // tile,),
+        in_specs=[pl.BlockSpec((columns, tokens), lambda i: (0, 0))] * 14
+        + [pl.BlockSpec((4, 1, tokens), lambda i: (0, 0, 0)), pl.BlockSpec((tile, 1), lambda i: (i, 0))]
+        + [pl.BlockSpec((tile, tokens), lambda i: (i, 0))] * 3,
+        out_specs=pl.BlockSpec((2, columns, tile), lambda i: (0, 0, i)),
+        compiler_params=pltpu.CompilerParams(vmem_limit_bytes=48 << 20),
+        cost_estimate=pl.CostEstimate(flops=1 << 30, bytes_accessed=1 << 20, transcendentals=0),
+        name="near_terms",
+    )(*cots, *hids, ids, entry, *grads)
+
+
+def far_kernel(core_ref, acc_ref, own_ref, other_ref, g_ref, out_ref):
+    width, tile = out_ref.shape[2:]
+    for core, ref in enumerate((own_ref, other_ref)):
+        total = acc_ref[core] + lax.dot_general(ref[...], g_ref[...], NT, preferred_element_type=F32)
         place = core_ref[0] if core == 0 else 1 - core_ref[0]
         out_ref[:, pl.ds(place, 1)] = total.reshape(4, 1, width, tile)
 
 
-def table_terms(core, cots, hids, ids, entry, grads, width):
-    rows, tokens = grads[0].shape
-    tile = 256
+def far_terms(core, acc, own, other, grad, width):
+    rows, tokens = grad.shape
+    columns, tile = own.shape[0], 256
+    piece = pl.BlockSpec((columns, tokens), lambda i, core: (0, 0))
     return pl.pallas_call(
-        table_kernel,
+        far_kernel,
         out_shape=jax.ShapeDtypeStruct((4, 2, width, rows), F32),
         grid_spec=pltpu.PrefetchScalarGridSpec(
             num_scalar_prefetch=1,
             grid=(rows // tile,),
-            in_specs=[pl.BlockSpec((4 * width, tokens), lambda i, core: (0, 0))] * 16
-            + [pl.BlockSpec((4, 1, tokens), lambda i, core: (0, 0, 0)), pl.BlockSpec((tile, 1), lambda i, core: (i, 0))]
-            + [pl.BlockSpec((tile, tokens), lambda i, core: (i, 0))] * 4,
+            in_specs=[
+                pl.BlockSpec((2, columns, tile), lambda i, core: (0, 0, i)),
+                piece,
+                piece,
+                pl.BlockSpec((tile, tokens), lambda i, core: (i, 0)),
+            ],
             out_specs=pl.BlockSpec((4, 2, width, tile), lambda i, core: (0, 0, 0, i)),
         ),
-        compiler_params=pltpu.CompilerParams(vmem_limit_bytes=48 << 20),
-        cost_estimate=pl.CostEstimate(flops=8 << 30, bytes_accessed=16 << 20, transcendentals=0),
-        name="table_terms",
-    )(core, *cots, *hids, ids, entry, *grads)
+        compiler_params=pltpu.CompilerParams(vmem_limit_bytes=32 << 20),
+        cost_estimate=pl.CostEstimate(flops=1 << 30, bytes_accessed=8 << 20, transcendentals=0),
+        name="far_terms",
+    )(core, acc, own, other, grad)
 
 
 def body(hidden, embed_cotangent, table, token_ids, target_ids, loss_scale):
@@ -172,9 +200,8 @@
     total = jnp.sum(jnp.exp(logits - top[None, :]), axis=0)
     target = jnp.sum(jnp.where(hot, logits, 0.0), axis=0)
     stats = jnp.stack([top, total, target])
-    stats, hid_low, hid_high, pass_low, pass_high = tie((stats, hid_low, hid_high, pass_low, pass_high))
-    hid_far = [send_z(pass_low, 1), send_z(pass_high, -1)]
     stats = lax.all_to_all(jnp.broadcast_to(stats[None], (32,) + stats.shape), "vocab", 0, 0)
+    stats, hid_low, hid_high = tie((stats, hid_low, hid_high))
     row_top = jnp.max(stats[:, 0], axis=0)
     exp_total = jnp.sum(stats[:, 1] * jnp.exp(stats[:, 0] - row_top[None]), axis=0)
     target_logit = jnp.sum(stats[:, 2], axis=0)
@@ -183,23 +210,30 @@
 
     grad = loss_scale[None, :] * (jnp.exp(logits - log_norm[None, :]) - hot.astype(F32))
     grad = grad.astype(BF)
-    grads = [grad] + [send_z(grad, d) for d in (1, 3, 2)]
+    grad_low, grad_high = send_z(grad, 1), send_z(grad, -1)
     pair_grad = send_core(grad)
     terms, again = hidden_terms(own_table, pair_table, grad, pair_grad)
     terms = lax.all_to_all(terms.reshape(16, width, tokens), "vocab", 0, 0, axis_index_groups=same_core)
-    grads[0] = again
-    cols, grads, hid_far = tie((cols, grads, hid_far))
-    hid_got = [pick_z(0), hid_low, hid_high, jnp.concatenate(hid_far, 1)]
+    cols, again, grad_low, grad_high, pass_low, pass_high = tie((cols, again, grad_low, grad_high, pass_low, pass_high))
+    half = rows // 2
+    hid_far = [send_z(pass_low, 1), send_z(pass_high, -1)]
+    grad_far = [send_z(grad_low[:half], 1), send_z(grad_high[half:], -1)]
     cols = cols.reshape(4, 4, PAD, tokens)
     cots, hids, ids = [], [], []
-    for block, hid_piece in zip(order, hid_got):
+    for block in order:
         piece = lax.dynamic_index_in_dim(cols, block, 0, keepdims=False)
         pair = piece[0, width : width + 2].astype(F32)
         ids.append((pair[0] * 256.0 + pair[1]).astype(jnp.int32))
         piece = piece[:, :width].reshape(4 * width, tokens)
         cots += [piece, send_core(piece)]
-        hids += [hid_piece, send_core(hid_piece)]
-    grad_table = table_terms(c.astype(jnp.int32)[None], cots, hids, jnp.stack(ids)[:, None], entry, grads, width)
+    for piece in (pick_z(0), hid_low, hid_high):
+        hids += [piece, send_core(piece)]
+    near = near_terms(cots, hids, jnp.stack(ids)[:, None], entry, [again, grad_low, grad_high])
+    near, hid_far, grad_far = tie((near, hid_far, grad_far))
+    hid_far = jnp.concatenate(hid_far, 1)
+    grad_table = far_terms(
+        c.astype(jnp.int32)[None], near, hid_far, send_core(hid_far), jnp.concatenate(grad_far, 0), width
+    )
     terms, grad_table = tie((terms, grad_table))
     grad_hidden = jnp.sum(terms.astype(F32), axis=0).astype(BF).T
     return (grad_hidden, grad_table.reshape(8 * width, rows).T, token_loss)

time: 186 us -> 164 us (0.88)
  waiting for transfers between devices: 47.7 us -> 23.7 us
  blocking collectives: 15.1 us -> 0 us
  starting transfers between devices: 45.4 us -> 55.9 us
  local copies, waits for them, and re-layouts: 27.6 us -> 31.8 us
  Pallas kernels: 22.1 us -> 24.4 us
    ppermute x9 -> x10, waiting for transfers between devices: 37.5 us -> 8.9 us  [send_z(): return lax.ppermute(a, 'seq', [(i, (i + d) % 4) for i in range(4)])]
    all_to_all x1 -> x0, blocking collectives: 15.1 us -> none  [body(): lax.all_to_all(jnp.broadcast_to(stats[None], (32,) + stats.shape), 'vocab...]
    all_to_all x0 -> x1, waiting for transfers between devices: none -> 8.82 us  [body(): lax.all_to_all(jnp.broadcast_to(stats[None], (32,) + stats.shape), 'vocab...]
    all_to_all x0 -> x1, starting transfers between devices: none -> 7.13 us  [body(): lax.all_to_all(jnp.broadcast_to(stats[None], (32,) + stats.shape), 'vocab...]
    ppermute x4, starting transfers between devices: 9.08 us -> 12.3 us  [send_y(): return lax.ppermute(a, 'vocab', vocab_perm(lambda y, x, c: (y + d, x, c)))]
    ppermute x4, waiting for transfers between devices: 4.68 us -> 1.95 us  [send_x(): return lax.ppermute(a, 'vocab', vocab_perm(lambda y, x, c: (y, x + d, c)))]
    pallas_call x1 -> x2, Pallas kernels: 13.4 us -> 15.5 us  [the longest x1 11.9 us: near_terms(): pl.pallas_call(near_kernel, out_shape=jax.ShapeDtypeStruct((2, columns, r...]
    slice x0 -> x2, local copies, waits for them, and re-layouts: none -> 2.05 us  [body(): grad_far = [send_z(grad_low[:half], 1), send_z(grad_high[half:], -1)]]
  transfers between devices with their start and end apart: 31 -> 33, of which waited for: 11 -> 9; matrix products, arithmetic and copies ran while one was open for 20% -> 24% of each run, Pallas kernels for 12% -> 15%
where the time goes in v2:
time: 164 us; the launch traced here: 163 us
  starting transfers between devices  55.9 us (34%)
  local copies, waits for them, and re-layouts  31.8 us (19%)
  Pallas kernels  24.4 us (15%)
  waiting for transfers between devices  23.7 us (14%)
  between operations  14.6 us (9%)
  matrix products  6.61 us (4%)
  other arithmetic  5.93 us (4%)
    ppermute x10, starting transfers between devices, send_z(): return lax.ppermute(a, 'seq', [(i, (i + d) % 4) for i in range(4)])  16.1 us
    unnamed x18, local copies, waits for them, and re-layouts  14.3 us
    ppermute x4, starting transfers between devices, send_y(): return lax.ppermute(a, 'vocab', vocab_perm(lambda y, x, c: (y + d, x, c)))  12.3 us
    pallas_call x1, Pallas kernels, near_terms(): pl.pallas_call(near_kernel, out_shape=jax.ShapeDtypeStruct((2, columns, r...  11.9 us
    ppermute x11, starting transfers between devices, send_core(): return lax.ppermute(a, 'vocab', vocab_perm(lambda y, x, c: (y, x, 1 - c)))  9.67 us
    ppermute x10, waiting for transfers between devices, send_z(): return lax.ppermute(a, 'seq', [(i, (i + d) % 4) for i in range(4)])  8.9 us
    pallas_call x1, Pallas kernels, hidden_terms(): pl.pallas_call(hidden_kernel, out_shape=[jax.ShapeDtypeStruct((columns, t...  8.86 us
    all_to_all x1, waiting for transfers between devices, body(): lax.all_to_all(jnp.broadcast_to(stats[None], (32,) + stats.shape), 'vocab...  8.82 us
  transfers between devices with their start and end apart: 33, of which 9 were waited for; matrix products, arithmetic and copies ran while one was open for 24% of the time, Pallas kernels for 15%

profile of v2, /device:TPU:1, one launch (start us, length us, event | category | flops | bytes accessed | tf_op | source)
XLA Modules:
  0.0 162.9 jit_solution(6152380513374112896)
XLA Ops:
  7.2 2.1 %collective-permute-start = (bf16[168,512]{1,0:T(8,128)(2,1)}, bf16[168,512]{1,0:T(8,128)(2,1)S(1)}, u32[]{:S(2)}, u32[]{:S(2)}) collective-permute-start(bf16[168,512]{1,0:T(8,128)(2,1)} %bitcast.98), channel_id=1, source_target_pairs={{0,2},{1,3},{2,4},{3,5},{4,6},{5,7},{6,0},{7,1},{8,10},{9,11},{10,... | collective-permute-start | bytes 516104 | tf_op jit(solution)/shard_map/ppermute | solution.py:20
  9.3 1.4 collective-permute-start.1
  10.7 0.7 fusion.8
  11.5 1.0 maximum_maximum_fusion
  12.5 0.7 collective-permute-start.4
  13.3 0.9 bitcast_dynamic-update-slice_fusion.3
  14.3 0.2 collective-permute-done
  14.5 0.4 collective-permute-start.2
  14.9 2.4 %collective-permute-start.3 = (bf16[168,256]{1,0:T(8,128)(2,1)S(1)}, bf16[168,256]{1,0:T(8,128)(2,1)S(1)}, u32[]{:S(2)}, u32[]{:S(2)}) collective-permute-start(bf16[168,256]{1,0:T(8,128)(2,1)S(1)} %slice.118), channel_id=1, source_target_pairs={{0,6},{1,7},{2,0},{3,1},{4,2},{5,3},{6,4},{7,5},{8,14},{9,15},{10,... | collective-permute-start | bytes 258056 | tf_op jit(solution)/shard_map/ppermute | solution.py:20
  17.3 1.7 %collective-permute-done.2 = bf16[168,256]{1,0:T(8,128)(2,1)S(1)} collective-permute-done((bf16[168,256]{1,0:T(8,128)(2,1)S(1)}, bf16[168,256]{1,0:T(8,128)(2,1)S(1)}, u32[]{:S(2)}, u32[]{:S(2)}) %collective-permute-start.2) | collective-permute-done | bytes 86048 | tf_op jit(solution)/shard_map/ppermute | solution.py:20
  19.1 4.2 %collective-permute-start.5 = (bf16[4,168,512]{2,1,0:T(8,128)(2,1)S(1)}, bf16[4,168,512]{2,1,0:T(8,128)(2,1)}, u32[]{:S(2)}, u32[]{:S(2)}) collective-permute-start(bf16[4,168,512]{2,1,0:T(8,128)(2,1)S(1)} %fusion.5), channel_id=1, source_target_pairs={{0,8},{1,9},{2,10},{3,11},{4,12},{5,13},{6,14},{7,15},{8,16},{9,17... | collective-permute-start | bytes 2064392 | tf_op jit(solution)/shard_map/ppermute | solution.py:24
  23.3 5.3 %collective-permute-start.6 = (bf16[4,168,512]{2,1,0:T(8,128)(2,1)S(1)}, bf16[4,168,512]{2,1,0:T(8,128)(2,1)}, u32[]{:S(2)}, u32[]{:S(2)}) collective-permute-start(bf16[4,168,512]{2,1,0:T(8,128)(2,1)S(1)} %fusion.5), channel_id=1, source_target_pairs={{0,24},{1,25},{2,26},{3,27},{4,28},{5,29},{6,30},{7,31},{8,0},{9,1... | collective-permute-start | bytes 2064392 | tf_op jit(solution)/shard_map/ppermute | solution.py:24
  28.7 11.8 %copy.15 = bf16[768,5376]{0,1:T(8,128)(2,1)} copy(bf16[768,5376]{1,0:T(8,128)(2,1)} %param.8) | data formatting | bytes 16515072 | tf_op args[2]
  40.5 0.2 broadcast_in_dim.56
  40.8 1.0 collective-permute-done.5
  41.8 1.5 slice.92
  43.4 1.0 slice.93
  44.4 2.7 %collective-permute-start.8 = (bf16[4,168,256]{2,1,0:T(8,128)(2,1)S(1)}, bf16[4,168,256]{2,1,0:T(8,128)(2,1)S(1)}, u32[]{:S(2)}, u32[]{:S(2)}) collective-permute-start(bf16[4,168,256]{2,1,0:T(8,128)(2,1)S(1)} %slice.93), channel_id=1, source_target_pairs={{0,24},{1,25},{2,26},{3,27},{4,28},{5,29},{6,30},{7,31},{8,0},{9,1... | collective-permute-start | bytes 1032200 | tf_op jit(solution)/shard_map/ppermute | solution.py:24
  47.1 1.1 bitcast_dynamic-update-slice_fusion.1
  48.3 1.2 bitcast_dynamic-update-slice_fusion
  49.4 3.8 %constant_dynamic-slice_fusion.4 = (bf16[16,1,168,768]{3,2,1,0:T(8,128)(2,1)}, bf16[16,1,168,768]{3,2,1,0:T(8,128)(2,1)}) fusion(bf16[16,2,168,768]{3,2,1,0:T(8,128)(2,1)S(1)} %bitcast.86, s32[]{:T(128)S(6)} %select_n.153, s32[]{:T(128)S(6)} %select_n.152), kind=kLoop, calls=%fused_computation.38 | loop fusion | bytes 16515080 | tf_op jit(solution)/shard_map/jit(dynamic_index_in_dim)/dynamic_slice | solution.py:182
  53.3 4.2 %collective-permute-start.10 = (bf16[2688,512]{1,0:T(8,128)(2,1)S(1)}, bf16[2688,512]{1,0:T(8,128)(2,1)}, u32[]{:S(2)}, u32[]{:S(2)}) collective-permute-start(bf16[2688,512]{1,0:T(8,128)(2,1)S(1)} %bitcast.87), channel_id=1, source_target_pairs={{0,1},{1,0},{2,3},{3,2},{4,5},{5,4},{6,7},{7,6},{8,9},{9,8},{10,11... | collective-permute-start | bytes 8257544 | tf_op jit(solution)/shard_map/ppermute | solution.py:28
  57.6 0.1 collective-permute-start.9
  57.7 1.4 constant_dynamic-slice_fusion
  59.1 0.2 collective-permute-start.11
  59.3 4.9 %collective-permute-start.12 = (bf16[672,512]{1,0:T(8,128)(2,1)}, bf16[672,512]{1,0:T(8,128)(2,1)}, u32[]{:S(2)}, u32[]{:S(2)}) collective-permute-start(bf16[672,512]{1,0:T(8,128)(2,1)} %bitcast.19), channel_id=1, source_target_pairs={{0,96},{32,0},{64,32},{96,64},{1,97},{33,1},{65,33},{97,65},{2,98}... | collective-permute-start | bytes 2064392 | tf_op jit(solution)/shard_map/ppermute | solution.py:32
  64.2 2.4 %fusion.23 = f32[768,512]{1,0:T(8,128)S(1)} fusion(bf16[2688,768]{1,0:T(8,128)(2,1)S(1)} %bitcast.90, bf16[2688,512]{1,0:T(8,128)(2,1)S(1)} %bitcast.88), kind=kOutput, calls=%fused_computation.76 | convolution fusion | flops 2113929216 | bytes 8454144 | tf_op jit(solution)/shard_map/dot_general | solution.py:167
  66.7 4.2 %fusion.24 = f32[768,512]{1,0:T(8,128)S(1)} fusion(bf16[2688,768]{1,0:T(8,128)(2,1)S(1)} %bitcast.92, bf16[2688,512]{1,0:T(8,128)(2,1)} %collective-permute-done.10), kind=kOutput, calls=%fused_computation.77 | convolution fusion | flops 2113929216 | bytes 8454144 | tf_op jit(solution)/shard_map/dot_general | solution.py:167
  70.9 0.4 fusion.20
  71.3 0.2 copy-done.5
  71.6 0.4 exponential_reduce_fusion
  72.0 0.7 broadcast_in_dim.68
  72.7 7.1 %all-to-all-start = ((f32[32,3,512]{2,1,0:T(4,128)}), f32[32,3,512]{2,1,0:T(4,128)S(1)}, u32[]{:S(2)}, u32[]{:S(2)}) async-start(f32[32,3,512]{2,1,0:T(4,128)} %broadcast_in_dim.68), calls=%async_computation | async-start | bytes 524288 | tf_op jit(solution)/shard_map/all_to_all | solution.py:203
  79.9 8.8 %all-to-all-done = f32[32,3,512]{2,1,0:T(4,128)S(1)} async-done(((f32[32,3,512]{2,1,0:T(4,128)}), f32[32,3,512]{2,1,0:T(4,128)S(1)}, u32[]{:S(2)}, u32[]{:S(2)}) %all-to-all-start) | async-done | bytes 196640 | tf_op jit(solution)/shard_map/all_to_all | solution.py:203
  88.8 0.1 fusion.22
  89.0 0.6 fusion.19
  89.6 1.3 fusion.3.g_ref
  90.9 0.2 collective-permute-start.13
  91.1 2.7 %collective-permute-start.15 = (bf16[768,512]{1,0:T(8,128)(2,1)}, bf16[768,512]{1,0:T(8,128)(2,1)}, u32[]{:S(2)}, u32[]{:S(2)}) collective-permute-start(bf16[768,512]{1,0:T(8,128)(2,1)} %fusion.3.g_ref), channel_id=1, source_target_pairs={{0,96},{32,0},{64,32},{96,64},{1,97},{33,1},{65,33},{97,65},{2,98}... | collective-permute-start | bytes 2359304 | tf_op jit(solution)/shard_map/ppermute | solution.py:32
  93.9 0.9 fusion.21
  94.8 2.7 %collective-permute-start.17 = (bf16[672,256]{1,0:T(8,128)(2,1)}, bf16[672,256]{1,0:T(8,128)(2,1)}, u32[]{:S(2)}, u32[]{:S(2)}) collective-permute-start(bf16[672,256]{1,0:T(8,128)(2,1)} %get-tuple-element.77), channel_id=1, source_target_pairs={{0,96},{32,0},{64,32},{96,64},{1,97},{33,1},{65,33},{97,65},{2,98}... | collective-permute-start | bytes 1032200 | tf_op jit(solution)/shard_map/ppermute | solution.py:32
  97.5 1.4 collective-permute-start.22
  98.8 8.9 %hidden_terms.1 = (bf16[2688,512]{1,0:T(8,128)(2,1)}, bf16[768,512]{1,0:T(8,128)(2,1)}) custom-call(bf16[2688,768]{1,0:T(8,128)(2,1)} %bitcast.89, bf16[2688,768]{1,0:T(8,128)(2,1)} %collective-permute-done.9.pair_ref, bf16[768,512]{1,0:T(8,128)(2,1)} %fusion.3.g_ref, bf16[768,512]{1,0:T(8,128)(2,1)} %copy-done.7), custom_call_target="tpu_custom_call" | custom-call | flops 4294967296 | bytes 12582912 | tf_op jit(solution)/shard_map/hidden_terms/pallas_call | solution.py:79
  107.7 3.7 %all-to-all-start.1 = ((bf16[16,168,512]{2,1,0:T(8,128)(2,1)}), bf16[16,168,512]{2,1,0:T(8,128)(2,1)S(1)}, u32[]{:S(2)}, u32[]{:S(2)}) async-start(bf16[16,168,512]{2,1,0:T(8,128)(2,1)} %bitcast.96), calls=%async_computation.1 | async-start | bytes 5505024 | tf_op jit(solution)/shard_map/all_to_all | solution.py:216
  111.5 7.4 %collective-permute-done.16 = bf16[672,256]{1,0:T(8,128)(2,1)S(1)} collective-permute-done((bf16[672,256]{1,0:T(8,128)(2,1)}, bf16[672,256]{1,0:T(8,128)(2,1)S(1)}, u32[]{:S(2)}, u32[]{:S(2)}) %collective-permute-start.16) | collective-permute-done | bytes 344096 | tf_op jit(solution)/shard_map/ppermute | solution.py:32
  118.8 1.1 collective-permute-start.23
  119.9 2.1 %dynamic-slice_bitcast_fusion = (bf16[4,176,512]{2,1,0:T(8,128)(2,1)S(1)}, bf16[4,176,512]{2,1,0:T(8,128)(2,1)S(1)}, bf16[4,176,512]{2,1,0:T(8,128)(2,1)S(1)}, bf16[4,176,512]{2,1,0:T(8,128)(2,1)S(1)}) fusion(bf16[4,4,176,512]{3,2,1,0:T(8,128)(2,1)} %bitcast.94, s32[]{:T(128)S(6)} %select_n.160, s32[]{:T(128)S(6)} %select_n.156, s32[]{:T(128)S(6)} %select_n.158, ...), kind=kLoop, calls=%fused_computation.8 | loop fusion | bytes 5767184 | tf_op jit(solution)/shard_map/jit(dynamic_index_in_dim)/squeeze | solution.py:224
  122.1 0.6 collective-permute-start.18
  122.7 0.1 collective-permute-start.19
  122.9 0.6 collective-permute-start.20
  123.5 1.0 slice.114
  124.5 1.0 slice.115
  125.6 0.1 collective-permute-start.21
  125.7 0.8 collective-permute-start.27
  126.5 2.1 %collective-permute-start.28 = (bf16[384,512]{1,0:T(8,128)(2,1)S(1)}, bf16[384,512]{1,0:T(8,128)(2,1)S(1)}, u32[]{:S(2)}, u32[]{:S(2)}) collective-permute-start(bf16[384,512]{1,0:T(8,128)(2,1)S(1)} %slice.115), channel_id=1, source_target_pairs={{0,96},{32,0},{64,32},{96,64},{1,97},{33,1},{65,33},{97,65},{2,98}... | collective-permute-start | bytes 1179656 | tf_op jit(solution)/shard_map/ppermute | solution.py:32
  128.6 2.7 %collective-permute-start.26 = (bf16[672,256]{1,0:T(8,128)(2,1)}, bf16[672,256]{1,0:T(8,128)(2,1)S(1)}, u32[]{:S(2)}, u32[]{:S(2)}) collective-permute-start(bf16[672,256]{1,0:T(8,128)(2,1)} %collective-permute-done.17), channel_id=1, source_target_pairs={{0,96},{32,0},{64,32},{96,64},{1,97},{33,1},{65,33},{97,65},{2,98}... | collective-permute-start | bytes 1032200 | tf_op jit(solution)/shard_map/ppermute | solution.py:32
  131.4 11.9 %near_terms.1.acc_ref = f32[2,672,768]{2,1,0:T(8,128)} custom-call(bf16[672,512]{1,0:T(8,128)(2,1)S(1)} %bitcast.79, bf16[672,512]{1,0:T(8,128)(2,1)S(1)} %collective-permute-done.18.refs_1_, bf16[672,512]{1,0:T(8,128)(2,1)S(1)} %bitcast.81, bf16[672,512]{1,0:T(8,128)(2,1)S(1)} %collective-permute-done.19.refs_3_, bf16[672,512]{1,0:T(8,128)(2,1)S(1)} %bitcast.83, ...), custom_call_target="tpu_custom_call" | custom-call | flops 1073741824 | bytes 1048576 | tf_op jit(solution)/shard_map/near_terms/pallas_call | solution.py:110
  143.3 1.5 collective-permute-done.25
  144.8 1.3 collective-permute-start.29
  146.2 1.7 %collective-permute-done.29.other_ref = bf16[672,512]{1,0:T(8,128)(2,1)S(1)} collective-permute-done((bf16[672,512]{1,0:T(8,128)(2,1)S(1)}, bf16[672,512]{1,0:T(8,128)(2,1)S(1)}, u32[]{:S(2)}, u32[]{:S(2)}) %collective-permute-start.29) | collective-permute-done | bytes 688160 | tf_op jit(solution)/shard_map/ppermute | solution.py:28
  147.9 2.2 %copy-done = f32[2,672,768]{2,1,0:T(8,128)S(1)} copy-done((f32[2,672,768]{2,1,0:T(8,128)S(1)}, f32[2,672,768]{2,1,0:T(8,128)}, u32[]{:S(2)}) %copy-start) | copy-done | bytes 4128792
  150.1 3.6 %far_terms.1 = f32[4,2,168,768]{3,2,1,0:T(8,128)} custom-call(s32[1]{0:T(128)} %bitcast.22.core_ref, f32[2,672,768]{2,1,0:T(8,128)S(1)} %copy-done, bf16[672,512]{1,0:T(8,128)(2,1)S(1)} %constant_dynamic-update-slice_fusion.own_ref, bf16[672,512]{1,0:T(8,128)(2,1)S(1)} %collective-permute-done.29.other_ref, bf16[768,512]{1,0:T(8,128)(2,1)S(1)} %pad_maximum_fusion.g_ref), custom_call_target="tpu_custom_call" | custom-call | flops 1073741824 | bytes 8388608 | tf_op jit(solution)/shard_map/far_terms/pallas_call | solution.py:136
  153.7 1.3 all-to-all-done.1
  155.0 1.1 reduce_sum.51
  (79 shorter events, 1.2 us)
Async XLA Ops:
  7.2 112.8 %all-gather.3.cloned.1.call-start = ((), (), s32[]{:S(2)}) async-start(), calls=%async_computation.2 | async-start | bytes 3063808 | tf_op jit(solution)/shard_map/all_gather | solution.py:185
  7.2 7.2 %collective-permute-start = (bf16[168,512]{1,0:T(8,128)(2,1)}, bf16[168,512]{1,0:T(8,128)(2,1)S(1)}, u32[]{:S(2)}, u32[]{:S(2)}) collective-permute-start(bf16[168,512]{1,0:T(8,128)(2,1)} %bitcast.98), channel_id=1, source_target_pairs={{0,2},{1,3},{2,4},{3,5},{4,6},{5,7},{6,0},{7,1},{8,10},{9,11},{10,... | collective-permute-start | bytes 516104 | tf_op jit(solution)/shard_map/ppermute | solution.py:20
  9.3 5.5 %collective-permute-start.1 = (bf16[168,512]{1,0:T(8,128)(2,1)}, bf16[168,512]{1,0:T(8,128)(2,1)S(1)}, u32[]{:S(2)}, u32[]{:S(2)}) collective-permute-start(bf16[168,512]{1,0:T(8,128)(2,1)} %bitcast.99), channel_id=1, source_target_pairs={{0,6},{1,7},{2,0},{3,1},{4,2},{5,3},{6,4},{7,5},{8,14},{9,15},{10,... | collective-permute-start | bytes 516104 | tf_op jit(solution)/shard_map/ppermute | solution.py:20
  12.5 6.6 %collective-permute-start.4 = (bf16[176,512]{1,0:T(8,128)(2,1)S(1)}, bf16[176,512]{1,0:T(8,128)(2,1)S(1)}, u32[]{:S(2)}, u32[]{:S(2)}) collective-permute-start(bf16[176,512]{1,0:T(8,128)(2,1)S(1)} %maximum_maximum_fusion), channel_id=1, source_target_pairs={{0,0},{1,1},{2,2},{3,3},{4,4},{5,5},{6,6},{7,7},{8,32},{9,33},{10,... | collective-permute-start | bytes 540680 | tf_op jit(solution)/shard_map/ppermute | solution.py:40
  14.5 4.6 %collective-permute-start.2 = (bf16[168,256]{1,0:T(8,128)(2,1)S(1)}, bf16[168,256]{1,0:T(8,128)(2,1)S(1)}, u32[]{:S(2)}, u32[]{:S(2)}) collective-permute-start(bf16[168,256]{1,0:T(8,128)(2,1)S(1)} %slice.117), channel_id=1, source_target_pairs={{0,2},{1,3},{2,4},{3,5},{4,6},{5,7},{6,0},{7,1},{8,10},{9,11},{10,... | collective-permute-start | bytes 258056 | tf_op jit(solution)/shard_map/ppermute | solution.py:20
  14.9 4.2 %collective-permute-start.3 = (bf16[168,256]{1,0:T(8,128)(2,1)S(1)}, bf16[168,256]{1,0:T(8,128)(2,1)S(1)}, u32[]{:S(2)}, u32[]{:S(2)}) collective-permute-start(bf16[168,256]{1,0:T(8,128)(2,1)S(1)} %slice.118), channel_id=1, source_target_pairs={{0,6},{1,7},{2,0},{3,1},{4,2},{5,3},{6,4},{7,5},{8,14},{9,15},{10,... | collective-permute-start | bytes 258056 | tf_op jit(solution)/shard_map/ppermute | solution.py:20
  19.1 21.4 %copy-start.4 = (bf16[176,512]{1,0:T(8,128)(2,1)}, bf16[176,512]{1,0:T(8,128)(2,1)S(1)}, u32[]{:S(2)}) copy-start(bf16[176,512]{1,0:T(8,128)(2,1)S(1)} %collective-permute-done.4) | copy-start | bytes 540676
  19.1 22.6 %collective-permute-start.5 = (bf16[4,168,512]{2,1,0:T(8,128)(2,1)S(1)}, bf16[4,168,512]{2,1,0:T(8,128)(2,1)}, u32[]{:S(2)}, u32[]{:S(2)}) collective-permute-start(bf16[4,168,512]{2,1,0:T(8,128)(2,1)S(1)} %fusion.5), channel_id=1, source_target_pairs={{0,8},{1,9},{2,10},{3,11},{4,12},{5,13},{6,14},{7,15},{8,16},{9,17... | collective-permute-start | bytes 2064392 | tf_op jit(solution)/shard_map/ppermute | solution.py:24
  23.3 18.4 %collective-permute-start.6 = (bf16[4,168,512]{2,1,0:T(8,128)(2,1)S(1)}, bf16[4,168,512]{2,1,0:T(8,128)(2,1)}, u32[]{:S(2)}, u32[]{:S(2)}) collective-permute-start(bf16[4,168,512]{2,1,0:T(8,128)(2,1)S(1)} %fusion.5), channel_id=1, source_target_pairs={{0,24},{1,25},{2,26},{3,27},{4,28},{5,29},{6,30},{7,31},{8,0},{9,1... | collective-permute-start | bytes 2064392 | tf_op jit(solution)/shard_map/ppermute | solution.py:24
  40.5 8.9 %copy-start.1 = (bf16[768,5376]{0,1:T(8,128)(2,1)S(1)}, bf16[768,5376]{0,1:T(8,128)(2,1)}, u32[]{:S(2)}) copy-start(bf16[768,5376]{0,1:T(8,128)(2,1)} %copy.15) | copy-start | bytes 24772612
  43.3 10.0 %collective-permute-start.7 = (bf16[4,168,256]{2,1,0:T(8,128)(2,1)S(1)}, bf16[4,168,256]{2,1,0:T(8,128)(2,1)S(1)}, u32[]{:S(2)}, u32[]{:S(2)}) collective-permute-start(bf16[4,168,256]{2,1,0:T(8,128)(2,1)S(1)} %slice.92), channel_id=1, source_target_pairs={{0,8},{1,9},{2,10},{3,11},{4,12},{5,13},{6,14},{7,15},{8,16},{9,17... | collective-permute-start | bytes 1032200 | tf_op jit(solution)/shard_map/ppermute | solution.py:24
  44.4 8.9 %collective-permute-start.8 = (bf16[4,168,256]{2,1,0:T(8,128)(2,1)S(1)}, bf16[4,168,256]{2,1,0:T(8,128)(2,1)S(1)}, u32[]{:S(2)}, u32[]{:S(2)}) collective-permute-start(bf16[4,168,256]{2,1,0:T(8,128)(2,1)S(1)} %slice.93), channel_id=1, source_target_pairs={{0,24},{1,25},{2,26},{3,27},{4,28},{5,29},{6,30},{7,31},{8,0},{9,1... | collective-permute-start | bytes 1032200 | tf_op jit(solution)/shard_map/ppermute | solution.py:24
  53.3 13.3 %collective-permute-start.10 = (bf16[2688,512]{1,0:T(8,128)(2,1)S(1)}, bf16[2688,512]{1,0:T(8,128)(2,1)}, u32[]{:S(2)}, u32[]{:S(2)}) collective-permute-start(bf16[2688,512]{1,0:T(8,128)(2,1)S(1)} %bitcast.87), channel_id=1, source_target_pairs={{0,1},{1,0},{2,3},{3,2},{4,5},{5,4},{6,7},{7,6},{8,9},{9,8},{10,11... | collective-permute-start | bytes 8257544 | tf_op jit(solution)/shard_map/ppermute | solution.py:28
  57.6 6.6 %copy-start.2 = (bf16[16,1,168,768]{3,2,1,0:T(8,128)(2,1)S(1)}, bf16[16,1,168,768]{3,2,1,0:T(8,128)(2,1)}, u32[]{:S(2)}) copy-start(bf16[16,1,168,768]{3,2,1,0:T(8,128)(2,1)} %get-tuple-element.68) | copy-start | bytes 12386308
  57.6 39.8 %collective-permute-start.9 = (bf16[2688,768]{1,0:T(8,128)(2,1)}, bf16[2688,768]{1,0:T(8,128)(2,1)}, u32[]{:S(2)}, u32[]{:S(2)}) collective-permute-start(bf16[2688,768]{1,0:T(8,128)(2,1)} %bitcast.91), channel_id=1, source_target_pairs={{0,1},{1,0},{2,3},{3,2},{4,5},{5,4},{6,7},{7,6},{8,9},{9,8},{10,11... | collective-permute-start | bytes 12386312 | tf_op jit(solution)/shard_map/ppermute | solution.py:28
  59.1 20.8 %collective-permute-start.11 = (bf16[672,512]{1,0:T(8,128)(2,1)}, bf16[672,512]{1,0:T(8,128)(2,1)}, u32[]{:S(2)}, u32[]{:S(2)}) collective-permute-start(bf16[672,512]{1,0:T(8,128)(2,1)} %bitcast.18), channel_id=1, source_target_pairs={{0,32},{32,64},{64,96},{96,0},{1,33},{33,65},{65,97},{97,1},{2,34}... | collective-permute-start | bytes 2064392 | tf_op jit(solution)/shard_map/ppermute | solution.py:32
  59.3 7.3 %copy-start.3 = (bf16[16,1,168,768]{3,2,1,0:T(8,128)(2,1)S(1)}, bf16[16,1,168,768]{3,2,1,0:T(8,128)(2,1)}, u32[]{:S(2)}) copy-start(bf16[16,1,168,768]{3,2,1,0:T(8,128)(2,1)} %get-tuple-element.67) | copy-start | bytes 12386308
  59.3 20.6 %collective-permute-start.12 = (bf16[672,512]{1,0:T(8,128)(2,1)}, bf16[672,512]{1,0:T(8,128)(2,1)}, u32[]{:S(2)}, u32[]{:S(2)}) collective-permute-start(bf16[672,512]{1,0:T(8,128)(2,1)} %bitcast.19), channel_id=1, source_target_pairs={{0,96},{32,0},{64,32},{96,64},{1,97},{33,1},{65,33},{97,65},{2,98}... | collective-permute-start | bytes 2064392 | tf_op jit(solution)/shard_map/ppermute | solution.py:32
  70.9 0.7 copy-start.5
  71.3 18.3 %copy-start.6 = (f32[512]{0:T(512)S(1)}, f32[512]{0:T(512)}, u32[]{:S(2)}) copy-start(f32[512]{0:T(512)} %param.11) | copy-start | bytes 6148
  72.7 16.0 %all-to-all-start = ((f32[32,3,512]{2,1,0:T(4,128)}), f32[32,3,512]{2,1,0:T(4,128)S(1)}, u32[]{:S(2)}, u32[]{:S(2)}) async-start(f32[32,3,512]{2,1,0:T(4,128)} %broadcast_in_dim.68), calls=%async_computation | async-start | bytes 524288 | tf_op jit(solution)/shard_map/all_to_all | solution.py:203
  90.9 3.9 %collective-permute-start.13 = (bf16[768,512]{1,0:T(8,128)(2,1)}, bf16[768,512]{1,0:T(8,128)(2,1)S(1)}, u32[]{:S(2)}, u32[]{:S(2)}) collective-permute-start(bf16[768,512]{1,0:T(8,128)(2,1)} %fusion.3.g_ref), channel_id=1, source_target_pairs={{0,1},{1,0},{2,3},{3,2},{4,5},{5,4},{6,7},{7,6},{8,9},{9,8},{10,11... | collective-permute-start | bytes 2359304 | tf_op jit(solution)/shard_map/ppermute | solution.py:28
  91.1 28.8 %collective-permute-start.14 = (bf16[768,512]{1,0:T(8,128)(2,1)}, bf16[768,512]{1,0:T(8,128)(2,1)}, u32[]{:S(2)}, u32[]{:S(2)}) collective-permute-start(bf16[768,512]{1,0:T(8,128)(2,1)} %fusion.3.g_ref), channel_id=1, source_target_pairs={{0,32},{32,64},{64,96},{96,0},{1,33},{33,65},{65,97},{97,1},{2,34}... | collective-permute-start | bytes 2359304 | tf_op jit(solution)/shard_map/ppermute | solution.py:32
  91.1 28.8 %collective-permute-start.15 = (bf16[768,512]{1,0:T(8,128)(2,1)}, bf16[768,512]{1,0:T(8,128)(2,1)}, u32[]{:S(2)}, u32[]{:S(2)}) collective-permute-start(bf16[768,512]{1,0:T(8,128)(2,1)} %fusion.3.g_ref), channel_id=1, source_target_pairs={{0,96},{32,0},{64,32},{96,64},{1,97},{33,1},{65,33},{97,65},{2,98}... | collective-permute-start | bytes 2359304 | tf_op jit(solution)/shard_map/ppermute | solution.py:32
  94.8 24.0 %collective-permute-start.16 = (bf16[672,256]{1,0:T(8,128)(2,1)}, bf16[672,256]{1,0:T(8,128)(2,1)S(1)}, u32[]{:S(2)}, u32[]{:S(2)}) collective-permute-start(bf16[672,256]{1,0:T(8,128)(2,1)} %get-tuple-element.78), channel_id=1, source_target_pairs={{0,32},{32,64},{64,96},{96,0},{1,33},{33,65},{65,97},{97,1},{2,34}... | collective-permute-start | bytes 1032200 | tf_op jit(solution)/shard_map/ppermute | solution.py:32
  94.8 4.1 %copy-start.7 = (bf16[768,512]{1,0:T(8,128)(2,1)}, bf16[768,512]{1,0:T(8,128)(2,1)S(1)}, u32[]{:S(2)}) copy-start(bf16[768,512]{1,0:T(8,128)(2,1)S(1)} %collective-permute-done.13.pg_ref) | copy-start | bytes 2359300
  94.8 25.1 %collective-permute-start.17 = (bf16[672,256]{1,0:T(8,128)(2,1)}, bf16[672,256]{1,0:T(8,128)(2,1)}, u32[]{:S(2)}, u32[]{:S(2)}) collective-permute-start(bf16[672,256]{1,0:T(8,128)(2,1)} %get-tuple-element.77), channel_id=1, source_target_pairs={{0,96},{32,0},{64,32},{96,64},{1,97},{33,1},{65,33},{97,65},{2,98}... | collective-permute-start | bytes 1032200 | tf_op jit(solution)/shard_map/ppermute | solution.py:32
  97.5 25.4 %collective-permute-start.22 = (bf16[672,512]{1,0:T(8,128)(2,1)}, bf16[672,512]{1,0:T(8,128)(2,1)}, u32[]{:S(2)}, u32[]{:S(2)}) collective-permute-start(bf16[672,512]{1,0:T(8,128)(2,1)} %bitcast.34.refs_8_), channel_id=1, source_target_pairs={{0,1},{1,0},{2,3},{3,2},{4,5},{5,4},{6,7},{7,6},{8,9},{9,8},{10,11... | collective-permute-start | bytes 2064392 | tf_op jit(solution)/shard_map/ppermute | solution.py:28
  107.7 47.2 %all-to-all-start.1 = ((bf16[16,168,512]{2,1,0:T(8,128)(2,1)}), bf16[16,168,512]{2,1,0:T(8,128)(2,1)S(1)}, u32[]{:S(2)}, u32[]{:S(2)}) async-start(bf16[16,168,512]{2,1,0:T(8,128)(2,1)} %bitcast.96), calls=%async_computation.1 | async-start | bytes 5505024 | tf_op jit(solution)/shard_map/all_to_all | solution.py:216
  118.8 6.8 %collective-permute-start.23 = (bf16[672,512]{1,0:T(8,128)(2,1)}, bf16[672,512]{1,0:T(8,128)(2,1)}, u32[]{:S(2)}, u32[]{:S(2)}) collective-permute-start(bf16[672,512]{1,0:T(8,128)(2,1)} %collective-permute-done.11.refs_10_), channel_id=1, source_target_pairs={{0,1},{1,0},{2,3},{3,2},{4,5},{5,4},{6,7},{7,6},{8,9},{9,8},{10,11... | collective-permute-start | bytes 2064392 | tf_op jit(solution)/shard_map/ppermute | solution.py:28
  119.9 5.8 %collective-permute-start.24 = (bf16[672,512]{1,0:T(8,128)(2,1)}, bf16[672,512]{1,0:T(8,128)(2,1)}, u32[]{:S(2)}, u32[]{:S(2)}) collective-permute-start(bf16[672,512]{1,0:T(8,128)(2,1)} %collective-permute-done.12.refs_12_), channel_id=1, source_target_pairs={{0,1},{1,0},{2,3},{3,2},{4,5},{5,4},{6,7},{7,6},{8,9},{9,8},{10,11... | collective-permute-start | bytes 2064392 | tf_op jit(solution)/shard_map/ppermute | solution.py:28
  122.1 4.4 %collective-permute-start.18 = (bf16[672,512]{1,0:T(8,128)(2,1)S(1)}, bf16[672,512]{1,0:T(8,128)(2,1)S(1)}, u32[]{:S(2)}, u32[]{:S(2)}) collective-permute-start(bf16[672,512]{1,0:T(8,128)(2,1)S(1)} %bitcast.78), channel_id=1, source_target_pairs={{0,1},{1,0},{2,3},{3,2},{4,5},{5,4},{6,7},{7,6},{8,9},{9,8},{10,11... | collective-permute-start | bytes 2064392 | tf_op jit(solution)/shard_map/ppermute | solution.py:28
  122.7 6.0 %collective-permute-start.19 = (bf16[672,512]{1,0:T(8,128)(2,1)S(1)}, bf16[672,512]{1,0:T(8,128)(2,1)S(1)}, u32[]{:S(2)}, u32[]{:S(2)}) collective-permute-start(bf16[672,512]{1,0:T(8,128)(2,1)S(1)} %bitcast.80), channel_id=1, source_target_pairs={{0,1},{1,0},{2,3},{3,2},{4,5},{5,4},{6,7},{7,6},{8,9},{9,8},{10,11... | collective-permute-start | bytes 2064392 | tf_op jit(solution)/shard_map/ppermute | solution.py:28
  122.9 5.8 %collective-permute-start.20 = (bf16[672,512]{1,0:T(8,128)(2,1)S(1)}, bf16[672,512]{1,0:T(8,128)(2,1)S(1)}, u32[]{:S(2)}, u32[]{:S(2)}) collective-permute-start(bf16[672,512]{1,0:T(8,128)(2,1)S(1)} %bitcast.82), channel_id=1, source_target_pairs={{0,1},{1,0},{2,3},{3,2},{4,5},{5,4},{6,7},{7,6},{8,9},{9,8},{10,11... | collective-permute-start | bytes 2064392 | tf_op jit(solution)/shard_map/ppermute | solution.py:28
  125.6 5.8 %collective-permute-start.21 = (bf16[672,512]{1,0:T(8,128)(2,1)S(1)}, bf16[672,512]{1,0:T(8,128)(2,1)S(1)}, u32[]{:S(2)}, u32[]{:S(2)}) collective-permute-start(bf16[672,512]{1,0:T(8,128)(2,1)S(1)} %bitcast.84), channel_id=1, source_target_pairs={{0,1},{1,0},{2,3},{3,2},{4,5},{5,4},{6,7},{7,6},{8,9},{9,8},{10,11... | collective-permute-start | bytes 2064392 | tf_op jit(solution)/shard_map/ppermute | solution.py:28
  125.7 19.0 %collective-permute-start.27 = (bf16[384,512]{1,0:T(8,128)(2,1)S(1)}, bf16[384,512]{1,0:T(8,128)(2,1)S(1)}, u32[]{:S(2)}, u32[]{:S(2)}) collective-permute-start(bf16[384,512]{1,0:T(8,128)(2,1)S(1)} %slice.114), channel_id=1, source_target_pairs={{0,32},{32,64},{64,96},{96,0},{1,33},{33,65},{65,97},{97,1},{2,34}... | collective-permute-start | bytes 1179656 | tf_op jit(solution)/shard_map/ppermute | solution.py:32
  126.5 18.2 %collective-permute-start.28 = (bf16[384,512]{1,0:T(8,128)(2,1)S(1)}, bf16[384,512]{1,0:T(8,128)(2,1)S(1)}, u32[]{:S(2)}, u32[]{:S(2)}) collective-permute-start(bf16[384,512]{1,0:T(8,128)(2,1)S(1)} %slice.115), channel_id=1, source_target_pairs={{0,96},{32,0},{64,32},{96,64},{1,97},{33,1},{65,33},{97,65},{2,98}... | collective-permute-start | bytes 1179656 | tf_op jit(solution)/shard_map/ppermute | solution.py:32
  128.6 16.1 %collective-permute-start.25 = (bf16[672,256]{1,0:T(8,128)(2,1)S(1)}, bf16[672,256]{1,0:T(8,128)(2,1)S(1)}, u32[]{:S(2)}, u32[]{:S(2)}) collective-permute-start(bf16[672,256]{1,0:T(8,128)(2,1)S(1)} %collective-permute-done.16), channel_id=1, source_target_pairs={{0,32},{32,64},{64,96},{96,0},{1,33},{33,65},{65,97},{97,1},{2,34}... | collective-permute-start | bytes 1032200 | tf_op jit(solution)/shard_map/ppermute | solution.py:32
  128.6 16.1 %collective-permute-start.26 = (bf16[672,256]{1,0:T(8,128)(2,1)}, bf16[672,256]{1,0:T(8,128)(2,1)S(1)}, u32[]{:S(2)}, u32[]{:S(2)}) collective-permute-start(bf16[672,256]{1,0:T(8,128)(2,1)} %collective-permute-done.17), channel_id=1, source_target_pairs={{0,96},{32,0},{64,32},{96,64},{1,97},{33,1},{65,33},{97,65},{2,98}... | collective-permute-start | bytes 1032200 | tf_op jit(solution)/shard_map/ppermute | solution.py:32
  144.8 3.1 %collective-permute-start.29 = (bf16[672,512]{1,0:T(8,128)(2,1)S(1)}, bf16[672,512]{1,0:T(8,128)(2,1)S(1)}, u32[]{:S(2)}, u32[]{:S(2)}) collective-permute-start(bf16[672,512]{1,0:T(8,128)(2,1)S(1)} %constant_dynamic-update-slice_fusion.own_ref), channel_id=1, source_target_pairs={{0,1},{1,0},{2,3},{3,2},{4,5},{5,4},{6,7},{7,6},{8,9},{9,8},{10,11... | collective-permute-start | bytes 2064392 | tf_op jit(solution)/shard_map/ppermute | solution.py:28
  147.9 2.2 %copy-start = (f32[2,672,768]{2,1,0:T(8,128)S(1)}, f32[2,672,768]{2,1,0:T(8,128)}, u32[]{:S(2)}) copy-start(f32[2,672,768]{2,1,0:T(8,128)} %near_terms.1.acc_ref) | copy-start | bytes 12386308
Sparse Core Ops, SparseCore 0:
  57.7 51.1 all-gather.2

commit v3 on v2

--- a/solution.py
+++ b/solution.py
@@ -46,6 +46,9 @@
 
 def ring_far(near, send):
     low, high = near
+    if low.ndim == 3:
+        half = low.shape[0] // 2
+        return send(low[:half], 1), send(high[half:], -1)
     half = low.shape[-1] // 2
     return send(low[..., :half], 1), send(high[..., half:], -1)
 
@@ -55,7 +58,7 @@
     out = lax.dynamic_update_index_in_dim(out, a, me, 0)
     out = lax.dynamic_update_index_in_dim(out, near[0], (me + 3) % 4, 0)
     out = lax.dynamic_update_index_in_dim(out, near[1], (me + 1) % 4, 0)
-    return lax.dynamic_update_index_in_dim(out, jnp.concatenate(far, -1), (me + 2) % 4, 0)
+    return lax.dynamic_update_index_in_dim(out, jnp.concatenate(far, 0 if a.ndim == 3 else -1), (me + 2) % 4, 0)
 
 
 PAD = 176
@@ -201,7 +204,8 @@
     target = jnp.sum(jnp.where(hot, logits, 0.0), axis=0)
     stats = jnp.stack([top, total, target])
     stats = lax.all_to_all(jnp.broadcast_to(stats[None], (32,) + stats.shape), "vocab", 0, 0)
-    stats, hid_low, hid_high = tie((stats, hid_low, hid_high))
+    stats, hid_low, hid_high, pass_low, pass_high = tie((stats, hid_low, hid_high, pass_low, pass_high))
+    hid_far = [send_z(pass_low, 1), send_z(pass_high, -1)]
     row_top = jnp.max(stats[:, 0], axis=0)
     exp_total = jnp.sum(stats[:, 1] * jnp.exp(stats[:, 0] - row_top[None]), axis=0)
     target_logit = jnp.sum(stats[:, 2], axis=0)
@@ -214,9 +218,8 @@
     pair_grad = send_core(grad)
     terms, again = hidden_terms(own_table, pair_table, grad, pair_grad)
     terms = lax.all_to_all(terms.reshape(16, width, tokens), "vocab", 0, 0, axis_index_groups=same_core)
-    cols, again, grad_low, grad_high, pass_low, pass_high = tie((cols, again, grad_low, grad_high, pass_low, pass_high))
+    cols, again, grad_low, grad_high = tie((cols, again, grad_low, grad_high))
     half = rows // 2
-    hid_far = [send_z(pass_low, 1), send_z(pass_high, -1)]
     grad_far = [send_z(grad_low[:half], 1), send_z(grad_high[half:], -1)]
     cols = cols.reshape(4, 4, PAD, tokens)
     cots, hids, ids = [], [], []

time: 164 us -> 165 us (level)
    all_to_all x1, waiting for transfers between devices: 1.27 us -> 5.56 us  [body(): lax.all_to_all(terms.reshape(16, width, tokens), 'vocab', 0, 0, axis_inde...]
    all_to_all x1, waiting for transfers between devices: 8.82 us -> 4.87 us  [body(): lax.all_to_all(jnp.broadcast_to(stats[None], (32,) + stats.shape), 'vocab...]
    slice x0 -> x2, local copies, waits for them, and re-layouts: none -> 2.53 us  [ring_far(): return (send(low[:half], 1), send(high[half:], -1))]
    slice x4 -> x2, local copies, waits for them, and re-layouts: 2.55 us -> 0.01 us  [ring_far(): return (send(low[..., :half], 1), send(high[..., half:], -1))]
    unnamed x18 -> x20, local copies, waits for them, and re-layouts: 14.3 us -> 14.6 us
where the time goes in v3:
time: 165 us; the launch traced here: 164 us
  starting transfers between devices  56 us (34%)
  local copies, waits for them, and re-layouts  32.2 us (20%)
  Pallas kernels  24.3 us (15%)
  waiting for transfers between devices  24.1 us (15%)
  between operations  14.6 us (9%)
  matrix products  6.68 us (4%)
  other arithmetic  5.94 us (4%)
    ppermute x10, starting transfers between devices, send_z(): return lax.ppermute(a, 'seq', [(i, (i + d) % 4) for i in range(4)])  16.1 us
    unnamed x20, local copies, waits for them, and re-layouts  14.6 us
    ppermute x4, starting transfers between devices, send_y(): return lax.ppermute(a, 'vocab', vocab_perm(lambda y, x, c: (y + d, x, c)))  12.3 us
    pallas_call x1, Pallas kernels, near_terms(): pl.pallas_call(near_kernel, out_shape=jax.ShapeDtypeStruct((2, columns, r...  11.9 us
    ppermute x11, starting transfers between devices, send_core(): return lax.ppermute(a, 'vocab', vocab_perm(lambda y, x, c: (y, x, 1 - c)))  9.3 us
    ppermute x10, waiting for transfers between devices, send_z(): return lax.ppermute(a, 'seq', [(i, (i + d) % 4) for i in range(4)])  8.98 us
    pallas_call x1, Pallas kernels, hidden_terms(): pl.pallas_call(hidden_kernel, out_shape=[jax.ShapeDtypeStruct((columns, t...  8.72 us
    all_to_all x1, starting transfers between devices, body(): lax.all_to_all(jnp.broadcast_to(stats[None], (32,) + stats.shape), 'vocab...  7.64 us
  transfers between devices with their start and end apart: 33, of which 9 were waited for; matrix products, arithmetic and copies ran while one was open for 24% of the time, Pallas kernels for 15%

profile of v3, /device:TPU:1, one launch (start us, length us, event | category | flops | bytes accessed | tf_op | source)
XLA Modules:
  0.0 163.8 jit_solution(13531412515164909477)
XLA Ops:
  7.2 2.1 %collective-permute-start = (bf16[168,512]{1,0:T(8,128)(2,1)}, bf16[168,512]{1,0:T(8,128)(2,1)S(1)}, u32[]{:S(2)}, u32[]{:S(2)}) collective-permute-start(bf16[168,512]{1,0:T(8,128)(2,1)} %bitcast.98), channel_id=1, source_target_pairs={{0,2},{1,3},{2,4},{3,5},{4,6},{5,7},{6,0},{7,1},{8,10},{9,11},{10,... | collective-permute-start | bytes 516104 | tf_op jit(solution)/shard_map/ppermute | solution.py:20
  9.3 1.4 collective-permute-start.1
  10.7 0.7 fusion.8
  11.5 1.0 maximum_maximum_fusion
  12.5 0.7 collective-permute-start.4
  13.3 0.9 bitcast_dynamic-update-slice_fusion.3
  14.3 0.2 collective-permute-done
  14.5 0.4 collective-permute-start.2
  14.9 2.4 %collective-permute-start.3 = (bf16[168,256]{1,0:T(8,128)(2,1)S(1)}, bf16[168,256]{1,0:T(8,128)(2,1)S(1)}, u32[]{:S(2)}, u32[]{:S(2)}) collective-permute-start(bf16[168,256]{1,0:T(8,128)(2,1)S(1)} %slice.118), channel_id=1, source_target_pairs={{0,6},{1,7},{2,0},{3,1},{4,2},{5,3},{6,4},{7,5},{8,14},{9,15},{10,... | collective-permute-start | bytes 258056 | tf_op jit(solution)/shard_map/ppermute | solution.py:20
  17.3 1.7 %collective-permute-done.2 = bf16[168,256]{1,0:T(8,128)(2,1)S(1)} collective-permute-done((bf16[168,256]{1,0:T(8,128)(2,1)S(1)}, bf16[168,256]{1,0:T(8,128)(2,1)S(1)}, u32[]{:S(2)}, u32[]{:S(2)}) %collective-permute-start.2) | collective-permute-done | bytes 86048 | tf_op jit(solution)/shard_map/ppermute | solution.py:20
  19.1 4.2 %collective-permute-start.5 = (bf16[4,168,512]{2,1,0:T(8,128)(2,1)S(1)}, bf16[4,168,512]{2,1,0:T(8,128)(2,1)}, u32[]{:S(2)}, u32[]{:S(2)}) collective-permute-start(bf16[4,168,512]{2,1,0:T(8,128)(2,1)S(1)} %fusion.5), channel_id=1, source_target_pairs={{0,8},{1,9},{2,10},{3,11},{4,12},{5,13},{6,14},{7,15},{8,16},{9,17... | collective-permute-start | bytes 2064392 | tf_op jit(solution)/shard_map/ppermute | solution.py:24
  23.3 5.3 %collective-permute-start.6 = (bf16[4,168,512]{2,1,0:T(8,128)(2,1)S(1)}, bf16[4,168,512]{2,1,0:T(8,128)(2,1)}, u32[]{:S(2)}, u32[]{:S(2)}) collective-permute-start(bf16[4,168,512]{2,1,0:T(8,128)(2,1)S(1)} %fusion.5), channel_id=1, source_target_pairs={{0,24},{1,25},{2,26},{3,27},{4,28},{5,29},{6,30},{7,31},{8,0},{9,1... | collective-permute-start | bytes 2064392 | tf_op jit(solution)/shard_map/ppermute | solution.py:24
  28.7 11.8 %copy.15 = bf16[768,5376]{0,1:T(8,128)(2,1)} copy(bf16[768,5376]{1,0:T(8,128)(2,1)} %param.8) | data formatting | bytes 16515072 | tf_op args[2]
  40.5 0.2 broadcast_in_dim.56
  40.8 1.0 collective-permute-done.5
  41.8 1.5 slice.92
  43.4 1.0 slice.93
  44.4 2.7 %collective-permute-start.8 = (bf16[2,168,512]{2,1,0:T(8,128)(2,1)S(1)}, bf16[2,168,512]{2,1,0:T(8,128)(2,1)S(1)}, u32[]{:S(2)}, u32[]{:S(2)}) collective-permute-start(bf16[2,168,512]{2,1,0:T(8,128)(2,1)S(1)} %slice.93), channel_id=1, source_target_pairs={{0,24},{1,25},{2,26},{3,27},{4,28},{5,29},{6,30},{7,31},{8,0},{9,1... | collective-permute-start | bytes 1032200 | tf_op jit(solution)/shard_map/ppermute | solution.py:24
  47.1 1.1 bitcast_dynamic-update-slice_fusion.1
  48.3 1.2 bitcast_dynamic-update-slice_fusion
  49.4 3.8 %constant_dynamic-slice_fusion.4 = (bf16[16,1,168,768]{3,2,1,0:T(8,128)(2,1)}, bf16[16,1,168,768]{3,2,1,0:T(8,128)(2,1)}) fusion(bf16[16,2,168,768]{3,2,1,0:T(8,128)(2,1)S(1)} %bitcast.86, s32[]{:T(128)S(6)} %select_n.153, s32[]{:T(128)S(6)} %select_n.152), kind=kLoop, calls=%fused_computation.38 | loop fusion | bytes 16515080 | tf_op jit(solution)/shard_map/jit(dynamic_index_in_dim)/dynamic_slice | solution.py:185
  53.3 4.2 %collective-permute-start.10 = (bf16[2688,512]{1,0:T(8,128)(2,1)S(1)}, bf16[2688,512]{1,0:T(8,128)(2,1)}, u32[]{:S(2)}, u32[]{:S(2)}) collective-permute-start(bf16[2688,512]{1,0:T(8,128)(2,1)S(1)} %bitcast.87), channel_id=1, source_target_pairs={{0,1},{1,0},{2,3},{3,2},{4,5},{5,4},{6,7},{7,6},{8,9},{9,8},{10,11... | collective-permute-start | bytes 8257544 | tf_op jit(solution)/shard_map/ppermute | solution.py:28
  57.7 1.4 constant_dynamic-slice_fusion
  59.1 0.9 fusion.21
  60.0 0.2 collective-permute-start.13
  60.3 4.9 %collective-permute-start.14 = (bf16[672,256]{1,0:T(8,128)(2,1)}, bf16[672,256]{1,0:T(8,128)(2,1)}, u32[]{:S(2)}, u32[]{:S(2)}) collective-permute-start(bf16[672,256]{1,0:T(8,128)(2,1)} %get-tuple-element.77), channel_id=1, source_target_pairs={{0,96},{32,0},{64,32},{96,64},{1,97},{33,1},{65,33},{97,65},{2,98}... | collective-permute-start | bytes 1032200 | tf_op jit(solution)/shard_map/ppermute | solution.py:32
  65.2 2.4 %fusion.23 = f32[768,512]{1,0:T(8,128)S(1)} fusion(bf16[2688,768]{1,0:T(8,128)(2,1)S(1)} %bitcast.90, bf16[2688,512]{1,0:T(8,128)(2,1)S(1)} %bitcast.88), kind=kOutput, calls=%fused_computation.76 | convolution fusion | flops 2113929216 | bytes 8454144 | tf_op jit(solution)/shard_map/dot_general | solution.py:170
  67.6 2.7 %collective-permute-start.12 = (bf16[672,512]{1,0:T(8,128)(2,1)}, bf16[672,512]{1,0:T(8,128)(2,1)}, u32[]{:S(2)}, u32[]{:S(2)}) collective-permute-start(bf16[672,512]{1,0:T(8,128)(2,1)} %bitcast.19), channel_id=1, source_target_pairs={{0,96},{32,0},{64,32},{96,64},{1,97},{33,1},{65,33},{97,65},{2,98}... | collective-permute-start | bytes 2064392 | tf_op jit(solution)/shard_map/ppermute | solution.py:32
  70.4 4.3 %fusion.24 = f32[768,512]{1,0:T(8,128)S(1)} fusion(bf16[2688,768]{1,0:T(8,128)(2,1)S(1)} %bitcast.92, bf16[2688,512]{1,0:T(8,128)(2,1)} %collective-permute-done.10), kind=kOutput, calls=%fused_computation.77 | convolution fusion | flops 2113929216 | bytes 8454144 | tf_op jit(solution)/shard_map/dot_general | solution.py:170
  74.6 0.4 fusion.20
  75.1 0.2 copy-done.6
  75.3 0.4 exponential_reduce_fusion
  75.7 0.8 broadcast_in_dim.68
  76.5 7.6 %all-to-all-start = ((f32[32,3,512]{2,1,0:T(4,128)}), f32[32,3,512]{2,1,0:T(4,128)S(1)}, u32[]{:S(2)}, u32[]{:S(2)}) async-start(f32[32,3,512]{2,1,0:T(4,128)} %broadcast_in_dim.68), calls=%async_computation | async-start | bytes 524288 | tf_op jit(solution)/shard_map/all_to_all | solution.py:206
  84.1 4.0 %collective-permute-done.11.refs_10_ = bf16[672,512]{1,0:T(8,128)(2,1)S(1)} collective-permute-done((bf16[672,512]{1,0:T(8,128)(2,1)}, bf16[672,512]{1,0:T(8,128)(2,1)S(1)}, u32[]{:S(2)}, u32[]{:S(2)}) %collective-permute-start.11) | collective-permute-done | bytes 688160 | tf_op jit(solution)/shard_map/ppermute | solution.py:32
  88.1 4.9 %all-to-all-done = f32[32,3,512]{2,1,0:T(4,128)S(1)} async-done(((f32[32,3,512]{2,1,0:T(4,128)}), f32[32,3,512]{2,1,0:T(4,128)S(1)}, u32[]{:S(2)}, u32[]{:S(2)}) %all-to-all-start) | async-done | bytes 196640 | tf_op jit(solution)/shard_map/all_to_all | solution.py:206
  93.1 0.1 fusion.22
  93.3 0.6 fusion.19
  93.9 1.3 fusion.3.g_ref
  95.2 0.2 collective-permute-start.15
  95.4 2.7 %collective-permute-start.17 = (bf16[768,512]{1,0:T(8,128)(2,1)}, bf16[768,512]{1,0:T(8,128)(2,1)}, u32[]{:S(2)}, u32[]{:S(2)}) collective-permute-start(bf16[768,512]{1,0:T(8,128)(2,1)} %fusion.3.g_ref), channel_id=1, source_target_pairs={{0,96},{32,0},{64,32},{96,64},{1,97},{33,1},{65,33},{97,65},{2,98}... | collective-permute-start | bytes 2359304 | tf_op jit(solution)/shard_map/ppermute | solution.py:32
  98.1 0.9 collective-permute-start.22
  99.1 0.1 collective-permute-start.23
  99.2 0.4 collective-permute-start.24
  99.6 0.4 copy-done.8
  99.9 8.7 %hidden_terms.1 = (bf16[2688,512]{1,0:T(8,128)(2,1)}, bf16[768,512]{1,0:T(8,128)(2,1)}) custom-call(bf16[2688,768]{1,0:T(8,128)(2,1)} %bitcast.89, bf16[2688,768]{1,0:T(8,128)(2,1)} %collective-permute-done.9.pair_ref, bf16[768,512]{1,0:T(8,128)(2,1)} %fusion.3.g_ref, bf16[768,512]{1,0:T(8,128)(2,1)} %copy-done.8), custom_call_target="tpu_custom_call" | custom-call | flops 4294967296 | bytes 12582912 | tf_op jit(solution)/shard_map/hidden_terms/pallas_call | solution.py:82
  108.7 3.7 %all-to-all-start.1 = ((bf16[16,168,512]{2,1,0:T(8,128)(2,1)}), bf16[16,168,512]{2,1,0:T(8,128)(2,1)S(1)}, u32[]{:S(2)}, u32[]{:S(2)}) async-start(bf16[16,168,512]{2,1,0:T(8,128)(2,1)} %bitcast.96), calls=%async_computation.1 | async-start | bytes 5505024 | tf_op jit(solution)/shard_map/all_to_all | solution.py:220
  112.4 3.4 %collective-permute-done.16.refs_17_ = bf16[768,512]{1,0:T(8,128)(2,1)} collective-permute-done((bf16[768,512]{1,0:T(8,128)(2,1)}, bf16[768,512]{1,0:T(8,128)(2,1)}, u32[]{:S(2)}, u32[]{:S(2)}) %collective-permute-start.16) | collective-permute-done | bytes 786464 | tf_op jit(solution)/shard_map/ppermute | solution.py:32
  115.8 2.0 %dynamic-slice_bitcast_fusion = (bf16[4,176,512]{2,1,0:T(8,128)(2,1)S(1)}, bf16[4,176,512]{2,1,0:T(8,128)(2,1)S(1)}, bf16[4,176,512]{2,1,0:T(8,128)(2,1)S(1)}, bf16[4,176,512]{2,1,0:T(8,128)(2,1)S(1)}) fusion(bf16[4,4,176,512]{3,2,1,0:T(8,128)(2,1)} %bitcast.94, s32[]{:T(128)S(6)} %select_n.160, s32[]{:T(128)S(6)} %select_n.156, s32[]{:T(128)S(6)} %select_n.158, ...), kind=kLoop, calls=%fused_computation.8 | loop fusion | bytes 5767184 | tf_op jit(solution)/shard_map/jit(dynamic_index_in_dim)/squeeze | solution.py:227
  117.9 1.2 collective-permute-start.18
  119.3 0.6 collective-permute-start.20
  120.0 1.0 slice.114
  121.0 1.0 slice.115
  122.0 0.1 collective-permute-start.21
  122.3 2.7 %collective-permute-start.26 = (bf16[672,256]{1,0:T(8,128)(2,1)}, bf16[672,256]{1,0:T(8,128)(2,1)S(1)}, u32[]{:S(2)}, u32[]{:S(2)}) collective-permute-start(bf16[672,256]{1,0:T(8,128)(2,1)} %collective-permute-done.14), channel_id=1, source_target_pairs={{0,96},{32,0},{64,32},{96,64},{1,97},{33,1},{65,33},{97,65},{2,98}... | collective-permute-start | bytes 1032200 | tf_op jit(solution)/shard_map/ppermute | solution.py:32
  125.0 2.7 %collective-permute-start.28 = (bf16[384,512]{1,0:T(8,128)(2,1)S(1)}, bf16[384,512]{1,0:T(8,128)(2,1)S(1)}, u32[]{:S(2)}, u32[]{:S(2)}) collective-permute-start(bf16[384,512]{1,0:T(8,128)(2,1)S(1)} %slice.115), channel_id=1, source_target_pairs={{0,96},{32,0},{64,32},{96,64},{1,97},{33,1},{65,33},{97,65},{2,98}... | collective-permute-start | bytes 1179656 | tf_op jit(solution)/shard_map/ppermute | solution.py:32
  127.8 11.9 %near_terms.1.acc_ref = f32[2,672,768]{2,1,0:T(8,128)} custom-call(bf16[672,512]{1,0:T(8,128)(2,1)S(1)} %bitcast.79, bf16[672,512]{1,0:T(8,128)(2,1)S(1)} %collective-permute-done.18.refs_1_, bf16[672,512]{1,0:T(8,128)(2,1)S(1)} %bitcast.81, bf16[672,512]{1,0:T(8,128)(2,1)S(1)} %collective-permute-done.19.refs_3_, bf16[672,512]{1,0:T(8,128)(2,1)S(1)} %bitcast.83, ...), custom_call_target="tpu_custom_call" | custom-call | flops 1073741824 | bytes 1048576 | tf_op jit(solution)/shard_map/near_terms/pallas_call | solution.py:113
  139.7 1.6 collective-permute-done.27
  141.3 1.4 collective-permute-start.29
  142.8 1.7 %collective-permute-done.29.other_ref = bf16[672,512]{1,0:T(8,128)(2,1)S(1)} collective-permute-done((bf16[672,512]{1,0:T(8,128)(2,1)S(1)}, bf16[672,512]{1,0:T(8,128)(2,1)S(1)}, u32[]{:S(2)}, u32[]{:S(2)}) %collective-permute-start.29) | collective-permute-done | bytes 688160 | tf_op jit(solution)/shard_map/ppermute | solution.py:28
  144.5 2.2 %copy-done = f32[2,672,768]{2,1,0:T(8,128)S(1)} copy-done((f32[2,672,768]{2,1,0:T(8,128)S(1)}, f32[2,672,768]{2,1,0:T(8,128)}, u32[]{:S(2)}) %copy-start) | copy-done | bytes 4128792
  146.7 3.6 %far_terms.1 = f32[4,2,168,768]{3,2,1,0:T(8,128)} custom-call(s32[1]{0:T(128)} %bitcast.23.core_ref, f32[2,672,768]{2,1,0:T(8,128)S(1)} %copy-done, bf16[672,512]{1,0:T(8,128)(2,1)S(1)} %constant_dynamic-update-slice_fusion.own_ref, bf16[672,512]{1,0:T(8,128)(2,1)S(1)} %collective-permute-done.29.other_ref, bf16[768,512]{1,0:T(8,128)(2,1)S(1)} %pad_maximum_fusion.g_ref), custom_call_target="tpu_custom_call" | custom-call | flops 1073741824 | bytes 8388608 | tf_op jit(solution)/shard_map/far_terms/pallas_call | solution.py:139
  150.3 5.6 %all-to-all-done.1 = bf16[16,168,512]{2,1,0:T(8,128)(2,1)S(1)} async-done(((bf16[16,168,512]{2,1,0:T(8,128)(2,1)}), bf16[16,168,512]{2,1,0:T(8,128)(2,1)S(1)}, u32[]{:S(2)}, u32[]{:S(2)}) %all-to-all-start.1) | async-done | bytes 2752544 | tf_op jit(solution)/shard_map/all_to_all | solution.py:220
  155.8 1.1 reduce_sum.51
  (81 shorter events, 1.3 us)
Async XLA Ops:
  7.2 108.7 %all-gather.3.cloned.1.call-start = ((), (), s32[]{:S(2)}) async-start(), calls=%async_computation.2 | async-start | bytes 3063808 | tf_op jit(solution)/shard_map/all_gather | solution.py:188
  7.2 7.2 %collective-permute-start = (bf16[168,512]{1,0:T(8,128)(2,1)}, bf16[168,512]{1,0:T(8,128)(2,1)S(1)}, u32[]{:S(2)}, u32[]{:S(2)}) collective-permute-start(bf16[168,512]{1,0:T(8,128)(2,1)} %bitcast.98), channel_id=1, source_target_pairs={{0,2},{1,3},{2,4},{3,5},{4,6},{5,7},{6,0},{7,1},{8,10},{9,11},{10,... | collective-permute-start | bytes 516104 | tf_op jit(solution)/shard_map/ppermute | solution.py:20
  9.3 5.5 %collective-permute-start.1 = (bf16[168,512]{1,0:T(8,128)(2,1)}, bf16[168,512]{1,0:T(8,128)(2,1)S(1)}, u32[]{:S(2)}, u32[]{:S(2)}) collective-permute-start(bf16[168,512]{1,0:T(8,128)(2,1)} %bitcast.99), channel_id=1, source_target_pairs={{0,6},{1,7},{2,0},{3,1},{4,2},{5,3},{6,4},{7,5},{8,14},{9,15},{10,... | collective-permute-start | bytes 516104 | tf_op jit(solution)/shard_map/ppermute | solution.py:20
  12.5 6.6 %collective-permute-start.4 = (bf16[176,512]{1,0:T(8,128)(2,1)S(1)}, bf16[176,512]{1,0:T(8,128)(2,1)S(1)}, u32[]{:S(2)}, u32[]{:S(2)}) collective-permute-start(bf16[176,512]{1,0:T(8,128)(2,1)S(1)} %maximum_maximum_fusion), channel_id=1, source_target_pairs={{0,0},{1,1},{2,2},{3,3},{4,4},{5,5},{6,6},{7,7},{8,32},{9,33},{10,... | collective-permute-start | bytes 540680 | tf_op jit(solution)/shard_map/ppermute | solution.py:40
  14.5 4.6 %collective-permute-start.2 = (bf16[168,256]{1,0:T(8,128)(2,1)S(1)}, bf16[168,256]{1,0:T(8,128)(2,1)S(1)}, u32[]{:S(2)}, u32[]{:S(2)}) collective-permute-start(bf16[168,256]{1,0:T(8,128)(2,1)S(1)} %slice.117), channel_id=1, source_target_pairs={{0,2},{1,3},{2,4},{3,5},{4,6},{5,7},{6,0},{7,1},{8,10},{9,11},{10,... | collective-permute-start | bytes 258056 | tf_op jit(solution)/shard_map/ppermute | solution.py:20
  14.9 4.2 %collective-permute-start.3 = (bf16[168,256]{1,0:T(8,128)(2,1)S(1)}, bf16[168,256]{1,0:T(8,128)(2,1)S(1)}, u32[]{:S(2)}, u32[]{:S(2)}) collective-permute-start(bf16[168,256]{1,0:T(8,128)(2,1)S(1)} %slice.118), channel_id=1, source_target_pairs={{0,6},{1,7},{2,0},{3,1},{4,2},{5,3},{6,4},{7,5},{8,14},{9,15},{10,... | collective-permute-start | bytes 258056 | tf_op jit(solution)/shard_map/ppermute | solution.py:20
  19.1 21.4 %copy-start.5 = (bf16[176,512]{1,0:T(8,128)(2,1)}, bf16[176,512]{1,0:T(8,128)(2,1)S(1)}, u32[]{:S(2)}) copy-start(bf16[176,512]{1,0:T(8,128)(2,1)S(1)} %collective-permute-done.4) | copy-start | bytes 540676
  19.1 22.6 %collective-permute-start.5 = (bf16[4,168,512]{2,1,0:T(8,128)(2,1)S(1)}, bf16[4,168,512]{2,1,0:T(8,128)(2,1)}, u32[]{:S(2)}, u32[]{:S(2)}) collective-permute-start(bf16[4,168,512]{2,1,0:T(8,128)(2,1)S(1)} %fusion.5), channel_id=1, source_target_pairs={{0,8},{1,9},{2,10},{3,11},{4,12},{5,13},{6,14},{7,15},{8,16},{9,17... | collective-permute-start | bytes 2064392 | tf_op jit(solution)/shard_map/ppermute | solution.py:24
  23.3 18.4 %collective-permute-start.6 = (bf16[4,168,512]{2,1,0:T(8,128)(2,1)S(1)}, bf16[4,168,512]{2,1,0:T(8,128)(2,1)}, u32[]{:S(2)}, u32[]{:S(2)}) collective-permute-start(bf16[4,168,512]{2,1,0:T(8,128)(2,1)S(1)} %fusion.5), channel_id=1, source_target_pairs={{0,24},{1,25},{2,26},{3,27},{4,28},{5,29},{6,30},{7,31},{8,0},{9,1... | collective-permute-start | bytes 2064392 | tf_op jit(solution)/shard_map/ppermute | solution.py:24
  40.5 9.0 %copy-start.1 = (bf16[768,5376]{0,1:T(8,128)(2,1)S(1)}, bf16[768,5376]{0,1:T(8,128)(2,1)}, u32[]{:S(2)}) copy-start(bf16[768,5376]{0,1:T(8,128)(2,1)} %copy.15) | copy-start | bytes 24772612
  43.3 10.0 %collective-permute-start.7 = (bf16[2,168,512]{2,1,0:T(8,128)(2,1)S(1)}, bf16[2,168,512]{2,1,0:T(8,128)(2,1)S(1)}, u32[]{:S(2)}, u32[]{:S(2)}) collective-permute-start(bf16[2,168,512]{2,1,0:T(8,128)(2,1)S(1)} %slice.92), channel_id=1, source_target_pairs={{0,8},{1,9},{2,10},{3,11},{4,12},{5,13},{6,14},{7,15},{8,16},{9,17... | collective-permute-start | bytes 1032200 | tf_op jit(solution)/shard_map/ppermute | solution.py:24
  44.4 8.9 %collective-permute-start.8 = (bf16[2,168,512]{2,1,0:T(8,128)(2,1)S(1)}, bf16[2,168,512]{2,1,0:T(8,128)(2,1)S(1)}, u32[]{:S(2)}, u32[]{:S(2)}) collective-permute-start(bf16[2,168,512]{2,1,0:T(8,128)(2,1)S(1)} %slice.93), channel_id=1, source_target_pairs={{0,24},{1,25},{2,26},{3,27},{4,28},{5,29},{6,30},{7,31},{8,0},{9,1... | collective-permute-start | bytes 1032200 | tf_op jit(solution)/shard_map/ppermute | solution.py:24
  53.3 14.3 %collective-permute-start.10 = (bf16[2688,512]{1,0:T(8,128)(2,1)S(1)}, bf16[2688,512]{1,0:T(8,128)(2,1)}, u32[]{:S(2)}, u32[]{:S(2)}) collective-permute-start(bf16[2688,512]{1,0:T(8,128)(2,1)S(1)} %bitcast.87), channel_id=1, source_target_pairs={{0,1},{1,0},{2,3},{3,2},{4,5},{5,4},{6,7},{7,6},{8,9},{9,8},{10,11... | collective-permute-start | bytes 8257544 | tf_op jit(solution)/shard_map/ppermute | solution.py:28
  57.6 7.6 %copy-start.2 = (bf16[16,1,168,768]{3,2,1,0:T(8,128)(2,1)S(1)}, bf16[16,1,168,768]{3,2,1,0:T(8,128)(2,1)}, u32[]{:S(2)}) copy-start(bf16[16,1,168,768]{3,2,1,0:T(8,128)(2,1)} %get-tuple-element.68) | copy-start | bytes 12386308
  57.6 41.5 %collective-permute-start.9 = (bf16[2688,768]{1,0:T(8,128)(2,1)}, bf16[2688,768]{1,0:T(8,128)(2,1)}, u32[]{:S(2)}, u32[]{:S(2)}) collective-permute-start(bf16[2688,768]{1,0:T(8,128)(2,1)} %bitcast.91), channel_id=1, source_target_pairs={{0,1},{1,0},{2,3},{3,2},{4,5},{5,4},{6,7},{7,6},{8,9},{9,8},{10,11... | collective-permute-start | bytes 12386312 | tf_op jit(solution)/shard_map/ppermute | solution.py:28
  60.0 24.1 %collective-permute-start.13 = (bf16[672,256]{1,0:T(8,128)(2,1)}, bf16[672,256]{1,0:T(8,128)(2,1)}, u32[]{:S(2)}, u32[]{:S(2)}) collective-permute-start(bf16[672,256]{1,0:T(8,128)(2,1)} %get-tuple-element.78), channel_id=1, source_target_pairs={{0,32},{32,64},{64,96},{96,0},{1,33},{33,65},{65,97},{97,1},{2,34}... | collective-permute-start | bytes 1032200 | tf_op jit(solution)/shard_map/ppermute | solution.py:32
  60.3 23.9 %collective-permute-start.14 = (bf16[672,256]{1,0:T(8,128)(2,1)}, bf16[672,256]{1,0:T(8,128)(2,1)}, u32[]{:S(2)}, u32[]{:S(2)}) collective-permute-start(bf16[672,256]{1,0:T(8,128)(2,1)} %get-tuple-element.77), channel_id=1, source_target_pairs={{0,96},{32,0},{64,32},{96,64},{1,97},{33,1},{65,33},{97,65},{2,98}... | collective-permute-start | bytes 1032200 | tf_op jit(solution)/shard_map/ppermute | solution.py:32
  65.2 5.2 %copy-start.3 = (bf16[16,1,168,768]{3,2,1,0:T(8,128)(2,1)S(1)}, bf16[16,1,168,768]{3,2,1,0:T(8,128)(2,1)}, u32[]{:S(2)}) copy-start(bf16[16,1,168,768]{3,2,1,0:T(8,128)(2,1)} %get-tuple-element.67) | copy-start | bytes 12386308
  65.2 23.0 %collective-permute-start.11 = (bf16[672,512]{1,0:T(8,128)(2,1)}, bf16[672,512]{1,0:T(8,128)(2,1)S(1)}, u32[]{:S(2)}, u32[]{:S(2)}) collective-permute-start(bf16[672,512]{1,0:T(8,128)(2,1)} %bitcast.18), channel_id=1, source_target_pairs={{0,32},{32,64},{64,96},{96,0},{1,33},{33,65},{65,97},{97,1},{2,34}... | collective-permute-start | bytes 2064392 | tf_op jit(solution)/shard_map/ppermute | solution.py:32
  67.6 20.5 %collective-permute-start.12 = (bf16[672,512]{1,0:T(8,128)(2,1)}, bf16[672,512]{1,0:T(8,128)(2,1)}, u32[]{:S(2)}, u32[]{:S(2)}) collective-permute-start(bf16[672,512]{1,0:T(8,128)(2,1)} %bitcast.19), channel_id=1, source_target_pairs={{0,96},{32,0},{64,32},{96,64},{1,97},{33,1},{65,33},{97,65},{2,98}... | collective-permute-start | bytes 2064392 | tf_op jit(solution)/shard_map/ppermute | solution.py:32
  74.6 0.7 copy-start.6
  75.1 18.8 %copy-start.7 = (f32[512]{0:T(512)S(1)}, f32[512]{0:T(512)}, u32[]{:S(2)}) copy-start(f32[512]{0:T(512)} %param.11) | copy-start | bytes 6148
  76.5 16.5 %all-to-all-start = ((f32[32,3,512]{2,1,0:T(4,128)}), f32[32,3,512]{2,1,0:T(4,128)S(1)}, u32[]{:S(2)}, u32[]{:S(2)}) async-start(f32[32,3,512]{2,1,0:T(4,128)} %broadcast_in_dim.68), calls=%async_computation | async-start | bytes 524288 | tf_op jit(solution)/shard_map/all_to_all | solution.py:206
  88.1 10.0 %copy-start.4 = (bf16[672,512]{1,0:T(8,128)(2,1)}, bf16[672,512]{1,0:T(8,128)(2,1)S(1)}, u32[]{:S(2)}) copy-start(bf16[672,512]{1,0:T(8,128)(2,1)S(1)} %collective-permute-done.11.refs_10_) | copy-start | bytes 2064388
  95.2 3.9 %collective-permute-start.15 = (bf16[768,512]{1,0:T(8,128)(2,1)}, bf16[768,512]{1,0:T(8,128)(2,1)S(1)}, u32[]{:S(2)}, u32[]{:S(2)}) collective-permute-start(bf16[768,512]{1,0:T(8,128)(2,1)} %fusion.3.g_ref), channel_id=1, source_target_pairs={{0,1},{1,0},{2,3},{3,2},{4,5},{5,4},{6,7},{7,6},{8,9},{9,8},{10,11... | collective-permute-start | bytes 2359304 | tf_op jit(solution)/shard_map/ppermute | solution.py:28
  95.4 20.4 %collective-permute-start.16 = (bf16[768,512]{1,0:T(8,128)(2,1)}, bf16[768,512]{1,0:T(8,128)(2,1)}, u32[]{:S(2)}, u32[]{:S(2)}) collective-permute-start(bf16[768,512]{1,0:T(8,128)(2,1)} %fusion.3.g_ref), channel_id=1, source_target_pairs={{0,32},{32,64},{64,96},{96,0},{1,33},{33,65},{65,97},{97,1},{2,34}... | collective-permute-start | bytes 2359304 | tf_op jit(solution)/shard_map/ppermute | solution.py:32
  95.4 20.4 %collective-permute-start.17 = (bf16[768,512]{1,0:T(8,128)(2,1)}, bf16[768,512]{1,0:T(8,128)(2,1)}, u32[]{:S(2)}, u32[]{:S(2)}) collective-permute-start(bf16[768,512]{1,0:T(8,128)(2,1)} %fusion.3.g_ref), channel_id=1, source_target_pairs={{0,96},{32,0},{64,32},{96,64},{1,97},{33,1},{65,33},{97,65},{2,98}... | collective-permute-start | bytes 2359304 | tf_op jit(solution)/shard_map/ppermute | solution.py:32
  98.1 21.2 %collective-permute-start.22 = (bf16[672,512]{1,0:T(8,128)(2,1)}, bf16[672,512]{1,0:T(8,128)(2,1)}, u32[]{:S(2)}, u32[]{:S(2)}) collective-permute-start(bf16[672,512]{1,0:T(8,128)(2,1)} %bitcast.34.refs_8_), channel_id=1, source_target_pairs={{0,1},{1,0},{2,3},{3,2},{4,5},{5,4},{6,7},{7,6},{8,9},{9,8},{10,11... | collective-permute-start | bytes 2064392 | tf_op jit(solution)/shard_map/ppermute | solution.py:28
  99.0 0.9 copy-start.8
  99.1 23.0 %collective-permute-start.23 = (bf16[672,512]{1,0:T(8,128)(2,1)}, bf16[672,512]{1,0:T(8,128)(2,1)}, u32[]{:S(2)}, u32[]{:S(2)}) collective-permute-start(bf16[672,512]{1,0:T(8,128)(2,1)} %copy-done.4), channel_id=1, source_target_pairs={{0,1},{1,0},{2,3},{3,2},{4,5},{5,4},{6,7},{7,6},{8,9},{9,8},{10,11... | collective-permute-start | bytes 2064392 | tf_op jit(solution)/shard_map/ppermute | solution.py:28
  99.2 23.0 %collective-permute-start.24 = (bf16[672,512]{1,0:T(8,128)(2,1)}, bf16[672,512]{1,0:T(8,128)(2,1)}, u32[]{:S(2)}, u32[]{:S(2)}) collective-permute-start(bf16[672,512]{1,0:T(8,128)(2,1)} %collective-permute-done.12.refs_12_), channel_id=1, source_target_pairs={{0,1},{1,0},{2,3},{3,2},{4,5},{5,4},{6,7},{7,6},{8,9},{9,8},{10,11... | collective-permute-start | bytes 2064392 | tf_op jit(solution)/shard_map/ppermute | solution.py:28
  108.7 47.2 %all-to-all-start.1 = ((bf16[16,168,512]{2,1,0:T(8,128)(2,1)}), bf16[16,168,512]{2,1,0:T(8,128)(2,1)S(1)}, u32[]{:S(2)}, u32[]{:S(2)}) async-start(bf16[16,168,512]{2,1,0:T(8,128)(2,1)} %bitcast.96), calls=%async_computation.1 | async-start | bytes 5505024 | tf_op jit(solution)/shard_map/all_to_all | solution.py:220
  117.9 4.3 %collective-permute-start.18 = (bf16[672,512]{1,0:T(8,128)(2,1)S(1)}, bf16[672,512]{1,0:T(8,128)(2,1)S(1)}, u32[]{:S(2)}, u32[]{:S(2)}) collective-permute-start(bf16[672,512]{1,0:T(8,128)(2,1)S(1)} %bitcast.78), channel_id=1, source_target_pairs={{0,1},{1,0},{2,3},{3,2},{4,5},{5,4},{6,7},{7,6},{8,9},{9,8},{10,11... | collective-permute-start | bytes 2064392 | tf_op jit(solution)/shard_map/ppermute | solution.py:28
  119.1 5.9 %collective-permute-start.19 = (bf16[672,512]{1,0:T(8,128)(2,1)S(1)}, bf16[672,512]{1,0:T(8,128)(2,1)S(1)}, u32[]{:S(2)}, u32[]{:S(2)}) collective-permute-start(bf16[672,512]{1,0:T(8,128)(2,1)S(1)} %bitcast.80), channel_id=1, source_target_pairs={{0,1},{1,0},{2,3},{3,2},{4,5},{5,4},{6,7},{7,6},{8,9},{9,8},{10,11... | collective-permute-start | bytes 2064392 | tf_op jit(solution)/shard_map/ppermute | solution.py:28
  119.3 5.7 %collective-permute-start.20 = (bf16[672,512]{1,0:T(8,128)(2,1)S(1)}, bf16[672,512]{1,0:T(8,128)(2,1)S(1)}, u32[]{:S(2)}, u32[]{:S(2)}) collective-permute-start(bf16[672,512]{1,0:T(8,128)(2,1)S(1)} %bitcast.82), channel_id=1, source_target_pairs={{0,1},{1,0},{2,3},{3,2},{4,5},{5,4},{6,7},{7,6},{8,9},{9,8},{10,11... | collective-permute-start | bytes 2064392 | tf_op jit(solution)/shard_map/ppermute | solution.py:28
  122.0 5.7 %collective-permute-start.21 = (bf16[672,512]{1,0:T(8,128)(2,1)S(1)}, bf16[672,512]{1,0:T(8,128)(2,1)S(1)}, u32[]{:S(2)}, u32[]{:S(2)}) collective-permute-start(bf16[672,512]{1,0:T(8,128)(2,1)S(1)} %bitcast.84), channel_id=1, source_target_pairs={{0,1},{1,0},{2,3},{3,2},{4,5},{5,4},{6,7},{7,6},{8,9},{9,8},{10,11... | collective-permute-start | bytes 2064392 | tf_op jit(solution)/shard_map/ppermute | solution.py:28
  122.2 17.5 %collective-permute-start.25 = (bf16[672,256]{1,0:T(8,128)(2,1)}, bf16[672,256]{1,0:T(8,128)(2,1)S(1)}, u32[]{:S(2)}, u32[]{:S(2)}) collective-permute-start(bf16[672,256]{1,0:T(8,128)(2,1)} %collective-permute-done.13), channel_id=1, source_target_pairs={{0,32},{32,64},{64,96},{96,0},{1,33},{33,65},{65,97},{97,1},{2,34}... | collective-permute-start | bytes 1032200 | tf_op jit(solution)/shard_map/ppermute | solution.py:32
  122.3 17.4 %collective-permute-start.26 = (bf16[672,256]{1,0:T(8,128)(2,1)}, bf16[672,256]{1,0:T(8,128)(2,1)S(1)}, u32[]{:S(2)}, u32[]{:S(2)}) collective-permute-start(bf16[672,256]{1,0:T(8,128)(2,1)} %collective-permute-done.14), channel_id=1, source_target_pairs={{0,96},{32,0},{64,32},{96,64},{1,97},{33,1},{65,33},{97,65},{2,98}... | collective-permute-start | bytes 1032200 | tf_op jit(solution)/shard_map/ppermute | solution.py:32
  125.0 16.2 %collective-permute-start.27 = (bf16[384,512]{1,0:T(8,128)(2,1)S(1)}, bf16[384,512]{1,0:T(8,128)(2,1)S(1)}, u32[]{:S(2)}, u32[]{:S(2)}) collective-permute-start(bf16[384,512]{1,0:T(8,128)(2,1)S(1)} %slice.114), channel_id=1, source_target_pairs={{0,32},{32,64},{64,96},{96,0},{1,33},{33,65},{65,97},{97,1},{2,34}... | collective-permute-start | bytes 1179656 | tf_op jit(solution)/shard_map/ppermute | solution.py:32
  125.0 16.2 %collective-permute-start.28 = (bf16[384,512]{1,0:T(8,128)(2,1)S(1)}, bf16[384,512]{1,0:T(8,128)(2,1)S(1)}, u32[]{:S(2)}, u32[]{:S(2)}) collective-permute-start(bf16[384,512]{1,0:T(8,128)(2,1)S(1)} %slice.115), channel_id=1, source_target_pairs={{0,96},{32,0},{64,32},{96,64},{1,97},{33,1},{65,33},{97,65},{2,98}... | collective-permute-start | bytes 1179656 | tf_op jit(solution)/shard_map/ppermute | solution.py:32
  141.3 3.2 %collective-permute-start.29 = (bf16[672,512]{1,0:T(8,128)(2,1)S(1)}, bf16[672,512]{1,0:T(8,128)(2,1)S(1)}, u32[]{:S(2)}, u32[]{:S(2)}) collective-permute-start(bf16[672,512]{1,0:T(8,128)(2,1)S(1)} %constant_dynamic-update-slice_fusion.own_ref), channel_id=1, source_target_pairs={{0,1},{1,0},{2,3},{3,2},{4,5},{5,4},{6,7},{7,6},{8,9},{9,8},{10,11... | collective-permute-start | bytes 2064392 | tf_op jit(solution)/shard_map/ppermute | solution.py:28
  144.5 2.2 %copy-start = (f32[2,672,768]{2,1,0:T(8,128)S(1)}, f32[2,672,768]{2,1,0:T(8,128)}, u32[]{:S(2)}) copy-start(f32[2,672,768]{2,1,0:T(8,128)} %near_terms.1.acc_ref) | copy-start | bytes 12386308
Sparse Core Ops, SparseCore 0:
  57.7 49.2 all-gather.2

commit v4 on v2

--- a/solution.py
+++ b/solution.py
@@ -46,6 +46,9 @@
 
 def ring_far(near, send):
     low, high = near
+    if low.ndim == 3:
+        half = low.shape[0] // 2
+        return send(low[:half], 1), send(high[half:], -1)
     half = low.shape[-1] // 2
     return send(low[..., :half], 1), send(high[..., half:], -1)
 
@@ -55,7 +58,7 @@
     out = lax.dynamic_update_index_in_dim(out, a, me, 0)
     out = lax.dynamic_update_index_in_dim(out, near[0], (me + 3) % 4, 0)
     out = lax.dynamic_update_index_in_dim(out, near[1], (me + 1) % 4, 0)
-    return lax.dynamic_update_index_in_dim(out, jnp.concatenate(far, -1), (me + 2) % 4, 0)
+    return lax.dynamic_update_index_in_dim(out, jnp.concatenate(far, 0 if a.ndim == 3 else -1), (me + 2) % 4, 0)
 
 
 PAD = 176

time: 164 us -> 164 us (level)
    slice x0 -> x2, local copies, waits for them, and re-layouts: none -> 2.53 us  [ring_far(): return (send(low[:half], 1), send(high[half:], -1))]
    slice x4 -> x2, local copies, waits for them, and re-layouts: 2.55 us -> 0.01 us  [ring_far(): return (send(low[..., :half], 1), send(high[..., half:], -1))]
where the time goes in v4:
time: 164 us; the launch traced here: 163 us
  starting transfers between devices  55.9 us (34%)
  local copies, waits for them, and re-layouts  31.8 us (19%)
  Pallas kernels  24.4 us (15%)
  waiting for transfers between devices  23.7 us (14%)
  between operations  14.6 us (9%)
  matrix products  6.61 us (4%)
  other arithmetic  5.93 us (4%)
    ppermute x10, starting transfers between devices, send_z(): return lax.ppermute(a, 'seq', [(i, (i + d) % 4) for i in range(4)])  16.1 us
    unnamed x18, local copies, waits for them, and re-layouts  14.3 us
    ppermute x4, starting transfers between devices, send_y(): return lax.ppermute(a, 'vocab', vocab_perm(lambda y, x, c: (y + d, x, c)))  12.3 us
    pallas_call x1, Pallas kernels, near_terms(): pl.pallas_call(near_kernel, out_shape=jax.ShapeDtypeStruct((2, columns, r...  11.9 us
    ppermute x11, starting transfers between devices, send_core(): return lax.ppermute(a, 'vocab', vocab_perm(lambda y, x, c: (y, x, 1 - c)))  9.67 us
    ppermute x10, waiting for transfers between devices, send_z(): return lax.ppermute(a, 'seq', [(i, (i + d) % 4) for i in range(4)])  8.9 us
    pallas_call x1, Pallas kernels, hidden_terms(): pl.pallas_call(hidden_kernel, out_shape=[jax.ShapeDtypeStruct((columns, t...  8.87 us
    all_to_all x1, waiting for transfers between devices, body(): lax.all_to_all(jnp.broadcast_to(stats[None], (32,) + stats.shape), 'vocab...  8.82 us
  transfers between devices with their start and end apart: 33, of which 9 were waited for; matrix products, arithmetic and copies ran while one was open for 24% of the time, Pallas kernels for 15%

profile of v4, /device:TPU:1, one launch (start us, length us, event | category | flops | bytes accessed | tf_op | source)
XLA Modules:
  0.0 162.9 jit_solution(4850510993203798514)
XLA Ops:
  7.2 2.1 %collective-permute-start = (bf16[168,512]{1,0:T(8,128)(2,1)}, bf16[168,512]{1,0:T(8,128)(2,1)S(1)}, u32[]{:S(2)}, u32[]{:S(2)}) collective-permute-start(bf16[168,512]{1,0:T(8,128)(2,1)} %bitcast.98), channel_id=1, source_target_pairs={{0,2},{1,3},{2,4},{3,5},{4,6},{5,7},{6,0},{7,1},{8,10},{9,11},{10,... | collective-permute-start | bytes 516104 | tf_op jit(solution)/shard_map/ppermute | solution.py:20
  9.3 1.4 collective-permute-start.1
  10.7 0.7 fusion.8
  11.5 1.0 maximum_maximum_fusion
  12.5 0.7 collective-permute-start.4
  13.3 0.9 bitcast_dynamic-update-slice_fusion.3
  14.3 0.2 collective-permute-done
  14.5 0.4 collective-permute-start.2
  14.9 2.4 %collective-permute-start.3 = (bf16[168,256]{1,0:T(8,128)(2,1)S(1)}, bf16[168,256]{1,0:T(8,128)(2,1)S(1)}, u32[]{:S(2)}, u32[]{:S(2)}) collective-permute-start(bf16[168,256]{1,0:T(8,128)(2,1)S(1)} %slice.118), channel_id=1, source_target_pairs={{0,6},{1,7},{2,0},{3,1},{4,2},{5,3},{6,4},{7,5},{8,14},{9,15},{10,... | collective-permute-start | bytes 258056 | tf_op jit(solution)/shard_map/ppermute | solution.py:20
  17.3 1.7 %collective-permute-done.2 = bf16[168,256]{1,0:T(8,128)(2,1)S(1)} collective-permute-done((bf16[168,256]{1,0:T(8,128)(2,1)S(1)}, bf16[168,256]{1,0:T(8,128)(2,1)S(1)}, u32[]{:S(2)}, u32[]{:S(2)}) %collective-permute-start.2) | collective-permute-done | bytes 86048 | tf_op jit(solution)/shard_map/ppermute | solution.py:20
  19.1 4.2 %collective-permute-start.5 = (bf16[4,168,512]{2,1,0:T(8,128)(2,1)S(1)}, bf16[4,168,512]{2,1,0:T(8,128)(2,1)}, u32[]{:S(2)}, u32[]{:S(2)}) collective-permute-start(bf16[4,168,512]{2,1,0:T(8,128)(2,1)S(1)} %fusion.5), channel_id=1, source_target_pairs={{0,8},{1,9},{2,10},{3,11},{4,12},{5,13},{6,14},{7,15},{8,16},{9,17... | collective-permute-start | bytes 2064392 | tf_op jit(solution)/shard_map/ppermute | solution.py:24
  23.3 5.3 %collective-permute-start.6 = (bf16[4,168,512]{2,1,0:T(8,128)(2,1)S(1)}, bf16[4,168,512]{2,1,0:T(8,128)(2,1)}, u32[]{:S(2)}, u32[]{:S(2)}) collective-permute-start(bf16[4,168,512]{2,1,0:T(8,128)(2,1)S(1)} %fusion.5), channel_id=1, source_target_pairs={{0,24},{1,25},{2,26},{3,27},{4,28},{5,29},{6,30},{7,31},{8,0},{9,1... | collective-permute-start | bytes 2064392 | tf_op jit(solution)/shard_map/ppermute | solution.py:24
  28.7 11.8 %copy.15 = bf16[768,5376]{0,1:T(8,128)(2,1)} copy(bf16[768,5376]{1,0:T(8,128)(2,1)} %param.8) | data formatting | bytes 16515072 | tf_op args[2]
  40.5 0.2 broadcast_in_dim.56
  40.8 1.0 collective-permute-done.5
  41.8 1.5 slice.92
  43.4 1.0 slice.93
  44.4 2.7 %collective-permute-start.8 = (bf16[2,168,512]{2,1,0:T(8,128)(2,1)S(1)}, bf16[2,168,512]{2,1,0:T(8,128)(2,1)S(1)}, u32[]{:S(2)}, u32[]{:S(2)}) collective-permute-start(bf16[2,168,512]{2,1,0:T(8,128)(2,1)S(1)} %slice.93), channel_id=1, source_target_pairs={{0,24},{1,25},{2,26},{3,27},{4,28},{5,29},{6,30},{7,31},{8,0},{9,1... | collective-permute-start | bytes 1032200 | tf_op jit(solution)/shard_map/ppermute | solution.py:24
  47.1 1.1 bitcast_dynamic-update-slice_fusion.1
  48.3 1.2 bitcast_dynamic-update-slice_fusion
  49.4 3.8 %constant_dynamic-slice_fusion.4 = (bf16[16,1,168,768]{3,2,1,0:T(8,128)(2,1)}, bf16[16,1,168,768]{3,2,1,0:T(8,128)(2,1)}) fusion(bf16[16,2,168,768]{3,2,1,0:T(8,128)(2,1)S(1)} %bitcast.86, s32[]{:T(128)S(6)} %select_n.153, s32[]{:T(128)S(6)} %select_n.152), kind=kLoop, calls=%fused_computation.38 | loop fusion | bytes 16515080 | tf_op jit(solution)/shard_map/jit(dynamic_index_in_dim)/dynamic_slice | solution.py:185
  53.3 4.2 %collective-permute-start.10 = (bf16[2688,512]{1,0:T(8,128)(2,1)S(1)}, bf16[2688,512]{1,0:T(8,128)(2,1)}, u32[]{:S(2)}, u32[]{:S(2)}) collective-permute-start(bf16[2688,512]{1,0:T(8,128)(2,1)S(1)} %bitcast.87), channel_id=1, source_target_pairs={{0,1},{1,0},{2,3},{3,2},{4,5},{5,4},{6,7},{7,6},{8,9},{9,8},{10,11... | collective-permute-start | bytes 8257544 | tf_op jit(solution)/shard_map/ppermute | solution.py:28
  57.6 0.1 collective-permute-start.9
  57.7 1.4 constant_dynamic-slice_fusion
  59.1 0.2 collective-permute-start.11
  59.3 4.9 %collective-permute-start.12 = (bf16[672,512]{1,0:T(8,128)(2,1)}, bf16[672,512]{1,0:T(8,128)(2,1)}, u32[]{:S(2)}, u32[]{:S(2)}) collective-permute-start(bf16[672,512]{1,0:T(8,128)(2,1)} %bitcast.19), channel_id=1, source_target_pairs={{0,96},{32,0},{64,32},{96,64},{1,97},{33,1},{65,33},{97,65},{2,98}... | collective-permute-start | bytes 2064392 | tf_op jit(solution)/shard_map/ppermute | solution.py:32
  64.2 2.4 %fusion.23 = f32[768,512]{1,0:T(8,128)S(1)} fusion(bf16[2688,768]{1,0:T(8,128)(2,1)S(1)} %bitcast.90, bf16[2688,512]{1,0:T(8,128)(2,1)S(1)} %bitcast.88), kind=kOutput, calls=%fused_computation.76 | convolution fusion | flops 2113929216 | bytes 8454144 | tf_op jit(solution)/shard_map/dot_general | solution.py:170
  66.7 4.2 %fusion.24 = f32[768,512]{1,0:T(8,128)S(1)} fusion(bf16[2688,768]{1,0:T(8,128)(2,1)S(1)} %bitcast.92, bf16[2688,512]{1,0:T(8,128)(2,1)} %collective-permute-done.10), kind=kOutput, calls=%fused_computation.77 | convolution fusion | flops 2113929216 | bytes 8454144 | tf_op jit(solution)/shard_map/dot_general | solution.py:170
  70.9 0.4 fusion.20
  71.3 0.2 copy-done.5
  71.6 0.4 exponential_reduce_fusion
  72.0 0.7 broadcast_in_dim.68
  72.7 7.1 %all-to-all-start = ((f32[32,3,512]{2,1,0:T(4,128)}), f32[32,3,512]{2,1,0:T(4,128)S(1)}, u32[]{:S(2)}, u32[]{:S(2)}) async-start(f32[32,3,512]{2,1,0:T(4,128)} %broadcast_in_dim.68), calls=%async_computation | async-start | bytes 524288 | tf_op jit(solution)/shard_map/all_to_all | solution.py:206
  79.9 8.8 %all-to-all-done = f32[32,3,512]{2,1,0:T(4,128)S(1)} async-done(((f32[32,3,512]{2,1,0:T(4,128)}), f32[32,3,512]{2,1,0:T(4,128)S(1)}, u32[]{:S(2)}, u32[]{:S(2)}) %all-to-all-start) | async-done | bytes 196640 | tf_op jit(solution)/shard_map/all_to_all | solution.py:206
  88.8 0.1 fusion.22
  89.0 0.6 fusion.19
  89.6 1.3 fusion.3.g_ref
  90.9 0.2 collective-permute-start.13
  91.1 2.7 %collective-permute-start.15 = (bf16[768,512]{1,0:T(8,128)(2,1)}, bf16[768,512]{1,0:T(8,128)(2,1)}, u32[]{:S(2)}, u32[]{:S(2)}) collective-permute-start(bf16[768,512]{1,0:T(8,128)(2,1)} %fusion.3.g_ref), channel_id=1, source_target_pairs={{0,96},{32,0},{64,32},{96,64},{1,97},{33,1},{65,33},{97,65},{2,98}... | collective-permute-start | bytes 2359304 | tf_op jit(solution)/shard_map/ppermute | solution.py:32
  93.9 0.9 fusion.21
  94.8 2.7 %collective-permute-start.17 = (bf16[672,256]{1,0:T(8,128)(2,1)}, bf16[672,256]{1,0:T(8,128)(2,1)}, u32[]{:S(2)}, u32[]{:S(2)}) collective-permute-start(bf16[672,256]{1,0:T(8,128)(2,1)} %get-tuple-element.77), channel_id=1, source_target_pairs={{0,96},{32,0},{64,32},{96,64},{1,97},{33,1},{65,33},{97,65},{2,98}... | collective-permute-start | bytes 1032200 | tf_op jit(solution)/shard_map/ppermute | solution.py:32
  97.5 1.4 collective-permute-start.22
  98.8 8.9 %hidden_terms.1 = (bf16[2688,512]{1,0:T(8,128)(2,1)}, bf16[768,512]{1,0:T(8,128)(2,1)}) custom-call(bf16[2688,768]{1,0:T(8,128)(2,1)} %bitcast.89, bf16[2688,768]{1,0:T(8,128)(2,1)} %collective-permute-done.9.pair_ref, bf16[768,512]{1,0:T(8,128)(2,1)} %fusion.3.g_ref, bf16[768,512]{1,0:T(8,128)(2,1)} %copy-done.7), custom_call_target="tpu_custom_call" | custom-call | flops 4294967296 | bytes 12582912 | tf_op jit(solution)/shard_map/hidden_terms/pallas_call | solution.py:82
  107.7 3.7 %all-to-all-start.1 = ((bf16[16,168,512]{2,1,0:T(8,128)(2,1)}), bf16[16,168,512]{2,1,0:T(8,128)(2,1)S(1)}, u32[]{:S(2)}, u32[]{:S(2)}) async-start(bf16[16,168,512]{2,1,0:T(8,128)(2,1)} %bitcast.96), calls=%async_computation.1 | async-start | bytes 5505024 | tf_op jit(solution)/shard_map/all_to_all | solution.py:219
  111.5 7.3 %collective-permute-done.16 = bf16[672,256]{1,0:T(8,128)(2,1)S(1)} collective-permute-done((bf16[672,256]{1,0:T(8,128)(2,1)}, bf16[672,256]{1,0:T(8,128)(2,1)S(1)}, u32[]{:S(2)}, u32[]{:S(2)}) %collective-permute-start.16) | collective-permute-done | bytes 344096 | tf_op jit(solution)/shard_map/ppermute | solution.py:32
  118.8 1.1 collective-permute-start.23
  119.9 2.1 %dynamic-slice_bitcast_fusion = (bf16[4,176,512]{2,1,0:T(8,128)(2,1)S(1)}, bf16[4,176,512]{2,1,0:T(8,128)(2,1)S(1)}, bf16[4,176,512]{2,1,0:T(8,128)(2,1)S(1)}, bf16[4,176,512]{2,1,0:T(8,128)(2,1)S(1)}) fusion(bf16[4,4,176,512]{3,2,1,0:T(8,128)(2,1)} %bitcast.94, s32[]{:T(128)S(6)} %select_n.160, s32[]{:T(128)S(6)} %select_n.156, s32[]{:T(128)S(6)} %select_n.158, ...), kind=kLoop, calls=%fused_computation.8 | loop fusion | bytes 5767184 | tf_op jit(solution)/shard_map/jit(dynamic_index_in_dim)/squeeze | solution.py:227
  122.1 0.6 collective-permute-start.18
  122.7 0.1 collective-permute-start.19
  122.9 0.6 collective-permute-start.20
  123.5 1.0 slice.114
  124.5 1.0 slice.115
  125.6 0.1 collective-permute-start.21
  125.7 0.8 collective-permute-start.27
  126.5 2.1 %collective-permute-start.28 = (bf16[384,512]{1,0:T(8,128)(2,1)S(1)}, bf16[384,512]{1,0:T(8,128)(2,1)S(1)}, u32[]{:S(2)}, u32[]{:S(2)}) collective-permute-start(bf16[384,512]{1,0:T(8,128)(2,1)S(1)} %slice.115), channel_id=1, source_target_pairs={{0,96},{32,0},{64,32},{96,64},{1,97},{33,1},{65,33},{97,65},{2,98}... | collective-permute-start | bytes 1179656 | tf_op jit(solution)/shard_map/ppermute | solution.py:32
  128.6 2.7 %collective-permute-start.26 = (bf16[672,256]{1,0:T(8,128)(2,1)}, bf16[672,256]{1,0:T(8,128)(2,1)S(1)}, u32[]{:S(2)}, u32[]{:S(2)}) collective-permute-start(bf16[672,256]{1,0:T(8,128)(2,1)} %collective-permute-done.17), channel_id=1, source_target_pairs={{0,96},{32,0},{64,32},{96,64},{1,97},{33,1},{65,33},{97,65},{2,98}... | collective-permute-start | bytes 1032200 | tf_op jit(solution)/shard_map/ppermute | solution.py:32
  131.4 11.9 %near_terms.1.acc_ref = f32[2,672,768]{2,1,0:T(8,128)} custom-call(bf16[672,512]{1,0:T(8,128)(2,1)S(1)} %bitcast.79, bf16[672,512]{1,0:T(8,128)(2,1)S(1)} %collective-permute-done.18.refs_1_, bf16[672,512]{1,0:T(8,128)(2,1)S(1)} %bitcast.81, bf16[672,512]{1,0:T(8,128)(2,1)S(1)} %collective-permute-done.19.refs_3_, bf16[672,512]{1,0:T(8,128)(2,1)S(1)} %bitcast.83, ...), custom_call_target="tpu_custom_call" | custom-call | flops 1073741824 | bytes 1048576 | tf_op jit(solution)/shard_map/near_terms/pallas_call | solution.py:113
  143.3 1.5 collective-permute-done.25
  144.8 1.3 collective-permute-start.29
  146.2 1.7 %collective-permute-done.29.other_ref = bf16[672,512]{1,0:T(8,128)(2,1)S(1)} collective-permute-done((bf16[672,512]{1,0:T(8,128)(2,1)S(1)}, bf16[672,512]{1,0:T(8,128)(2,1)S(1)}, u32[]{:S(2)}, u32[]{:S(2)}) %collective-permute-start.29) | collective-permute-done | bytes 688160 | tf_op jit(solution)/shard_map/ppermute | solution.py:28
  147.9 2.2 %copy-done = f32[2,672,768]{2,1,0:T(8,128)S(1)} copy-done((f32[2,672,768]{2,1,0:T(8,128)S(1)}, f32[2,672,768]{2,1,0:T(8,128)}, u32[]{:S(2)}) %copy-start) | copy-done | bytes 4128792
  150.1 3.6 %far_terms.1 = f32[4,2,168,768]{3,2,1,0:T(8,128)} custom-call(s32[1]{0:T(128)} %bitcast.22.core_ref, f32[2,672,768]{2,1,0:T(8,128)S(1)} %copy-done, bf16[672,512]{1,0:T(8,128)(2,1)S(1)} %constant_dynamic-update-slice_fusion.own_ref, bf16[672,512]{1,0:T(8,128)(2,1)S(1)} %collective-permute-done.29.other_ref, bf16[768,512]{1,0:T(8,128)(2,1)S(1)} %pad_maximum_fusion.g_ref), custom_call_target="tpu_custom_call" | custom-call | flops 1073741824 | bytes 8388608 | tf_op jit(solution)/shard_map/far_terms/pallas_call | solution.py:139
  153.7 1.3 all-to-all-done.1
  155.0 1.1 reduce_sum.51
  (79 shorter events, 1.2 us)
Async XLA Ops:
  7.2 112.8 %all-gather.3.cloned.1.call-start = ((), (), s32[]{:S(2)}) async-start(), calls=%async_computation.2 | async-start | bytes 3063808 | tf_op jit(solution)/shard_map/all_gather | solution.py:188
  7.2 7.2 %collective-permute-start = (bf16[168,512]{1,0:T(8,128)(2,1)}, bf16[168,512]{1,0:T(8,128)(2,1)S(1)}, u32[]{:S(2)}, u32[]{:S(2)}) collective-permute-start(bf16[168,512]{1,0:T(8,128)(2,1)} %bitcast.98), channel_id=1, source_target_pairs={{0,2},{1,3},{2,4},{3,5},{4,6},{5,7},{6,0},{7,1},{8,10},{9,11},{10,... | collective-permute-start | bytes 516104 | tf_op jit(solution)/shard_map/ppermute | solution.py:20
  9.3 5.5 %collective-permute-start.1 = (bf16[168,512]{1,0:T(8,128)(2,1)}, bf16[168,512]{1,0:T(8,128)(2,1)S(1)}, u32[]{:S(2)}, u32[]{:S(2)}) collective-permute-start(bf16[168,512]{1,0:T(8,128)(2,1)} %bitcast.99), channel_id=1, source_target_pairs={{0,6},{1,7},{2,0},{3,1},{4,2},{5,3},{6,4},{7,5},{8,14},{9,15},{10,... | collective-permute-start | bytes 516104 | tf_op jit(solution)/shard_map/ppermute | solution.py:20
  12.5 6.6 %collective-permute-start.4 = (bf16[176,512]{1,0:T(8,128)(2,1)S(1)}, bf16[176,512]{1,0:T(8,128)(2,1)S(1)}, u32[]{:S(2)}, u32[]{:S(2)}) collective-permute-start(bf16[176,512]{1,0:T(8,128)(2,1)S(1)} %maximum_maximum_fusion), channel_id=1, source_target_pairs={{0,0},{1,1},{2,2},{3,3},{4,4},{5,5},{6,6},{7,7},{8,32},{9,33},{10,... | collective-permute-start | bytes 540680 | tf_op jit(solution)/shard_map/ppermute | solution.py:40
  14.5 4.6 %collective-permute-start.2 = (bf16[168,256]{1,0:T(8,128)(2,1)S(1)}, bf16[168,256]{1,0:T(8,128)(2,1)S(1)}, u32[]{:S(2)}, u32[]{:S(2)}) collective-permute-start(bf16[168,256]{1,0:T(8,128)(2,1)S(1)} %slice.117), channel_id=1, source_target_pairs={{0,2},{1,3},{2,4},{3,5},{4,6},{5,7},{6,0},{7,1},{8,10},{9,11},{10,... | collective-permute-start | bytes 258056 | tf_op jit(solution)/shard_map/ppermute | solution.py:20
  14.9 4.2 %collective-permute-start.3 = (bf16[168,256]{1,0:T(8,128)(2,1)S(1)}, bf16[168,256]{1,0:T(8,128)(2,1)S(1)}, u32[]{:S(2)}, u32[]{:S(2)}) collective-permute-start(bf16[168,256]{1,0:T(8,128)(2,1)S(1)} %slice.118), channel_id=1, source_target_pairs={{0,6},{1,7},{2,0},{3,1},{4,2},{5,3},{6,4},{7,5},{8,14},{9,15},{10,... | collective-permute-start | bytes 258056 | tf_op jit(solution)/shard_map/ppermute | solution.py:20
  19.1 21.4 %copy-start.4 = (bf16[176,512]{1,0:T(8,128)(2,1)}, bf16[176,512]{1,0:T(8,128)(2,1)S(1)}, u32[]{:S(2)}) copy-start(bf16[176,512]{1,0:T(8,128)(2,1)S(1)} %collective-permute-done.4) | copy-start | bytes 540676
  19.1 22.6 %collective-permute-start.5 = (bf16[4,168,512]{2,1,0:T(8,128)(2,1)S(1)}, bf16[4,168,512]{2,1,0:T(8,128)(2,1)}, u32[]{:S(2)}, u32[]{:S(2)}) collective-permute-start(bf16[4,168,512]{2,1,0:T(8,128)(2,1)S(1)} %fusion.5), channel_id=1, source_target_pairs={{0,8},{1,9},{2,10},{3,11},{4,12},{5,13},{6,14},{7,15},{8,16},{9,17... | collective-permute-start | bytes 2064392 | tf_op jit(solution)/shard_map/ppermute | solution.py:24
  23.3 18.4 %collective-permute-start.6 = (bf16[4,168,512]{2,1,0:T(8,128)(2,1)S(1)}, bf16[4,168,512]{2,1,0:T(8,128)(2,1)}, u32[]{:S(2)}, u32[]{:S(2)}) collective-permute-start(bf16[4,168,512]{2,1,0:T(8,128)(2,1)S(1)} %fusion.5), channel_id=1, source_target_pairs={{0,24},{1,25},{2,26},{3,27},{4,28},{5,29},{6,30},{7,31},{8,0},{9,1... | collective-permute-start | bytes 2064392 | tf_op jit(solution)/shard_map/ppermute | solution.py:24
  40.5 8.9 %copy-start.1 = (bf16[768,5376]{0,1:T(8,128)(2,1)S(1)}, bf16[768,5376]{0,1:T(8,128)(2,1)}, u32[]{:S(2)}) copy-start(bf16[768,5376]{0,1:T(8,128)(2,1)} %copy.15) | copy-start | bytes 24772612
  43.3 10.0 %collective-permute-start.7 = (bf16[2,168,512]{2,1,0:T(8,128)(2,1)S(1)}, bf16[2,168,512]{2,1,0:T(8,128)(2,1)S(1)}, u32[]{:S(2)}, u32[]{:S(2)}) collective-permute-start(bf16[2,168,512]{2,1,0:T(8,128)(2,1)S(1)} %slice.92), channel_id=1, source_target_pairs={{0,8},{1,9},{2,10},{3,11},{4,12},{5,13},{6,14},{7,15},{8,16},{9,17... | collective-permute-start | bytes 1032200 | tf_op jit(solution)/shard_map/ppermute | solution.py:24
  44.4 8.9 %collective-permute-start.8 = (bf16[2,168,512]{2,1,0:T(8,128)(2,1)S(1)}, bf16[2,168,512]{2,1,0:T(8,128)(2,1)S(1)}, u32[]{:S(2)}, u32[]{:S(2)}) collective-permute-start(bf16[2,168,512]{2,1,0:T(8,128)(2,1)S(1)} %slice.93), channel_id=1, source_target_pairs={{0,24},{1,25},{2,26},{3,27},{4,28},{5,29},{6,30},{7,31},{8,0},{9,1... | collective-permute-start | bytes 1032200 | tf_op jit(solution)/shard_map/ppermute | solution.py:24
  53.3 13.3 %collective-permute-start.10 = (bf16[2688,512]{1,0:T(8,128)(2,1)S(1)}, bf16[2688,512]{1,0:T(8,128)(2,1)}, u32[]{:S(2)}, u32[]{:S(2)}) collective-permute-start(bf16[2688,512]{1,0:T(8,128)(2,1)S(1)} %bitcast.87), channel_id=1, source_target_pairs={{0,1},{1,0},{2,3},{3,2},{4,5},{5,4},{6,7},{7,6},{8,9},{9,8},{10,11... | collective-permute-start | bytes 8257544 | tf_op jit(solution)/shard_map/ppermute | solution.py:28
  57.6 6.6 %copy-start.2 = (bf16[16,1,168,768]{3,2,1,0:T(8,128)(2,1)S(1)}, bf16[16,1,168,768]{3,2,1,0:T(8,128)(2,1)}, u32[]{:S(2)}) copy-start(bf16[16,1,168,768]{3,2,1,0:T(8,128)(2,1)} %get-tuple-element.68) | copy-start | bytes 12386308
  57.6 39.8 %collective-permute-start.9 = (bf16[2688,768]{1,0:T(8,128)(2,1)}, bf16[2688,768]{1,0:T(8,128)(2,1)}, u32[]{:S(2)}, u32[]{:S(2)}) collective-permute-start(bf16[2688,768]{1,0:T(8,128)(2,1)} %bitcast.91), channel_id=1, source_target_pairs={{0,1},{1,0},{2,3},{3,2},{4,5},{5,4},{6,7},{7,6},{8,9},{9,8},{10,11... | collective-permute-start | bytes 12386312 | tf_op jit(solution)/shard_map/ppermute | solution.py:28
  59.1 20.8 %collective-permute-start.11 = (bf16[672,512]{1,0:T(8,128)(2,1)}, bf16[672,512]{1,0:T(8,128)(2,1)}, u32[]{:S(2)}, u32[]{:S(2)}) collective-permute-start(bf16[672,512]{1,0:T(8,128)(2,1)} %bitcast.18), channel_id=1, source_target_pairs={{0,32},{32,64},{64,96},{96,0},{1,33},{33,65},{65,97},{97,1},{2,34}... | collective-permute-start | bytes 2064392 | tf_op jit(solution)/shard_map/ppermute | solution.py:32
  59.3 7.3 %copy-start.3 = (bf16[16,1,168,768]{3,2,1,0:T(8,128)(2,1)S(1)}, bf16[16,1,168,768]{3,2,1,0:T(8,128)(2,1)}, u32[]{:S(2)}) copy-start(bf16[16,1,168,768]{3,2,1,0:T(8,128)(2,1)} %get-tuple-element.67) | copy-start | bytes 12386308
  59.3 20.6 %collective-permute-start.12 = (bf16[672,512]{1,0:T(8,128)(2,1)}, bf16[672,512]{1,0:T(8,128)(2,1)}, u32[]{:S(2)}, u32[]{:S(2)}) collective-permute-start(bf16[672,512]{1,0:T(8,128)(2,1)} %bitcast.19), channel_id=1, source_target_pairs={{0,96},{32,0},{64,32},{96,64},{1,97},{33,1},{65,33},{97,65},{2,98}... | collective-permute-start | bytes 2064392 | tf_op jit(solution)/shard_map/ppermute | solution.py:32
  70.9 0.7 copy-start.5
  71.3 18.3 %copy-start.6 = (f32[512]{0:T(512)S(1)}, f32[512]{0:T(512)}, u32[]{:S(2)}) copy-start(f32[512]{0:T(512)} %param.11) | copy-start | bytes 6148
  72.7 16.0 %all-to-all-start = ((f32[32,3,512]{2,1,0:T(4,128)}), f32[32,3,512]{2,1,0:T(4,128)S(1)}, u32[]{:S(2)}, u32[]{:S(2)}) async-start(f32[32,3,512]{2,1,0:T(4,128)} %broadcast_in_dim.68), calls=%async_computation | async-start | bytes 524288 | tf_op jit(solution)/shard_map/all_to_all | solution.py:206
  90.9 3.9 %collective-permute-start.13 = (bf16[768,512]{1,0:T(8,128)(2,1)}, bf16[768,512]{1,0:T(8,128)(2,1)S(1)}, u32[]{:S(2)}, u32[]{:S(2)}) collective-permute-start(bf16[768,512]{1,0:T(8,128)(2,1)} %fusion.3.g_ref), channel_id=1, source_target_pairs={{0,1},{1,0},{2,3},{3,2},{4,5},{5,4},{6,7},{7,6},{8,9},{9,8},{10,11... | collective-permute-start | bytes 2359304 | tf_op jit(solution)/shard_map/ppermute | solution.py:28
  91.1 28.8 %collective-permute-start.14 = (bf16[768,512]{1,0:T(8,128)(2,1)}, bf16[768,512]{1,0:T(8,128)(2,1)}, u32[]{:S(2)}, u32[]{:S(2)}) collective-permute-start(bf16[768,512]{1,0:T(8,128)(2,1)} %fusion.3.g_ref), channel_id=1, source_target_pairs={{0,32},{32,64},{64,96},{96,0},{1,33},{33,65},{65,97},{97,1},{2,34}... | collective-permute-start | bytes 2359304 | tf_op jit(solution)/shard_map/ppermute | solution.py:32
  91.1 28.8 %collective-permute-start.15 = (bf16[768,512]{1,0:T(8,128)(2,1)}, bf16[768,512]{1,0:T(8,128)(2,1)}, u32[]{:S(2)}, u32[]{:S(2)}) collective-permute-start(bf16[768,512]{1,0:T(8,128)(2,1)} %fusion.3.g_ref), channel_id=1, source_target_pairs={{0,96},{32,0},{64,32},{96,64},{1,97},{33,1},{65,33},{97,65},{2,98}... | collective-permute-start | bytes 2359304 | tf_op jit(solution)/shard_map/ppermute | solution.py:32
  94.8 24.0 %collective-permute-start.16 = (bf16[672,256]{1,0:T(8,128)(2,1)}, bf16[672,256]{1,0:T(8,128)(2,1)S(1)}, u32[]{:S(2)}, u32[]{:S(2)}) collective-permute-start(bf16[672,256]{1,0:T(8,128)(2,1)} %get-tuple-element.78), channel_id=1, source_target_pairs={{0,32},{32,64},{64,96},{96,0},{1,33},{33,65},{65,97},{97,1},{2,34}... | collective-permute-start | bytes 1032200 | tf_op jit(solution)/shard_map/ppermute | solution.py:32
  94.8 4.1 %copy-start.7 = (bf16[768,512]{1,0:T(8,128)(2,1)}, bf16[768,512]{1,0:T(8,128)(2,1)S(1)}, u32[]{:S(2)}) copy-start(bf16[768,512]{1,0:T(8,128)(2,1)S(1)} %collective-permute-done.13.pg_ref) | copy-start | bytes 2359300
  94.8 25.1 %collective-permute-start.17 = (bf16[672,256]{1,0:T(8,128)(2,1)}, bf16[672,256]{1,0:T(8,128)(2,1)}, u32[]{:S(2)}, u32[]{:S(2)}) collective-permute-start(bf16[672,256]{1,0:T(8,128)(2,1)} %get-tuple-element.77), channel_id=1, source_target_pairs={{0,96},{32,0},{64,32},{96,64},{1,97},{33,1},{65,33},{97,65},{2,98}... | collective-permute-start | bytes 1032200 | tf_op jit(solution)/shard_map/ppermute | solution.py:32
  97.5 25.4 %collective-permute-start.22 = (bf16[672,512]{1,0:T(8,128)(2,1)}, bf16[672,512]{1,0:T(8,128)(2,1)}, u32[]{:S(2)}, u32[]{:S(2)}) collective-permute-start(bf16[672,512]{1,0:T(8,128)(2,1)} %bitcast.34.refs_8_), channel_id=1, source_target_pairs={{0,1},{1,0},{2,3},{3,2},{4,5},{5,4},{6,7},{7,6},{8,9},{9,8},{10,11... | collective-permute-start | bytes 2064392 | tf_op jit(solution)/shard_map/ppermute | solution.py:28
  107.7 47.2 %all-to-all-start.1 = ((bf16[16,168,512]{2,1,0:T(8,128)(2,1)}), bf16[16,168,512]{2,1,0:T(8,128)(2,1)S(1)}, u32[]{:S(2)}, u32[]{:S(2)}) async-start(bf16[16,168,512]{2,1,0:T(8,128)(2,1)} %bitcast.96), calls=%async_computation.1 | async-start | bytes 5505024 | tf_op jit(solution)/shard_map/all_to_all | solution.py:219
  118.8 6.8 %collective-permute-start.23 = (bf16[672,512]{1,0:T(8,128)(2,1)}, bf16[672,512]{1,0:T(8,128)(2,1)}, u32[]{:S(2)}, u32[]{:S(2)}) collective-permute-start(bf16[672,512]{1,0:T(8,128)(2,1)} %collective-permute-done.11.refs_10_), channel_id=1, source_target_pairs={{0,1},{1,0},{2,3},{3,2},{4,5},{5,4},{6,7},{7,6},{8,9},{9,8},{10,11... | collective-permute-start | bytes 2064392 | tf_op jit(solution)/shard_map/ppermute | solution.py:28
  119.9 5.8 %collective-permute-start.24 = (bf16[672,512]{1,0:T(8,128)(2,1)}, bf16[672,512]{1,0:T(8,128)(2,1)}, u32[]{:S(2)}, u32[]{:S(2)}) collective-permute-start(bf16[672,512]{1,0:T(8,128)(2,1)} %collective-permute-done.12.refs_12_), channel_id=1, source_target_pairs={{0,1},{1,0},{2,3},{3,2},{4,5},{5,4},{6,7},{7,6},{8,9},{9,8},{10,11... | collective-permute-start | bytes 2064392 | tf_op jit(solution)/shard_map/ppermute | solution.py:28
  122.1 4.4 %collective-permute-start.18 = (bf16[672,512]{1,0:T(8,128)(2,1)S(1)}, bf16[672,512]{1,0:T(8,128)(2,1)S(1)}, u32[]{:S(2)}, u32[]{:S(2)}) collective-permute-start(bf16[672,512]{1,0:T(8,128)(2,1)S(1)} %bitcast.78), channel_id=1, source_target_pairs={{0,1},{1,0},{2,3},{3,2},{4,5},{5,4},{6,7},{7,6},{8,9},{9,8},{10,11... | collective-permute-start | bytes 2064392 | tf_op jit(solution)/shard_map/ppermute | solution.py:28
  122.7 6.0 %collective-permute-start.19 = (bf16[672,512]{1,0:T(8,128)(2,1)S(1)}, bf16[672,512]{1,0:T(8,128)(2,1)S(1)}, u32[]{:S(2)}, u32[]{:S(2)}) collective-permute-start(bf16[672,512]{1,0:T(8,128)(2,1)S(1)} %bitcast.80), channel_id=1, source_target_pairs={{0,1},{1,0},{2,3},{3,2},{4,5},{5,4},{6,7},{7,6},{8,9},{9,8},{10,11... | collective-permute-start | bytes 2064392 | tf_op jit(solution)/shard_map/ppermute | solution.py:28
  122.9 5.8 %collective-permute-start.20 = (bf16[672,512]{1,0:T(8,128)(2,1)S(1)}, bf16[672,512]{1,0:T(8,128)(2,1)S(1)}, u32[]{:S(2)}, u32[]{:S(2)}) collective-permute-start(bf16[672,512]{1,0:T(8,128)(2,1)S(1)} %bitcast.82), channel_id=1, source_target_pairs={{0,1},{1,0},{2,3},{3,2},{4,5},{5,4},{6,7},{7,6},{8,9},{9,8},{10,11... | collective-permute-start | bytes 2064392 | tf_op jit(solution)/shard_map/ppermute | solution.py:28
  125.6 5.8 %collective-permute-start.21 = (bf16[672,512]{1,0:T(8,128)(2,1)S(1)}, bf16[672,512]{1,0:T(8,128)(2,1)S(1)}, u32[]{:S(2)}, u32[]{:S(2)}) collective-permute-start(bf16[672,512]{1,0:T(8,128)(2,1)S(1)} %bitcast.84), channel_id=1, source_target_pairs={{0,1},{1,0},{2,3},{3,2},{4,5},{5,4},{6,7},{7,6},{8,9},{9,8},{10,11... | collective-permute-start | bytes 2064392 | tf_op jit(solution)/shard_map/ppermute | solution.py:28
  125.7 19.0 %collective-permute-start.27 = (bf16[384,512]{1,0:T(8,128)(2,1)S(1)}, bf16[384,512]{1,0:T(8,128)(2,1)S(1)}, u32[]{:S(2)}, u32[]{:S(2)}) collective-permute-start(bf16[384,512]{1,0:T(8,128)(2,1)S(1)} %slice.114), channel_id=1, source_target_pairs={{0,32},{32,64},{64,96},{96,0},{1,33},{33,65},{65,97},{97,1},{2,34}... | collective-permute-start | bytes 1179656 | tf_op jit(solution)/shard_map/ppermute | solution.py:32
  126.5 18.2 %collective-permute-start.28 = (bf16[384,512]{1,0:T(8,128)(2,1)S(1)}, bf16[384,512]{1,0:T(8,128)(2,1)S(1)}, u32[]{:S(2)}, u32[]{:S(2)}) collective-permute-start(bf16[384,512]{1,0:T(8,128)(2,1)S(1)} %slice.115), channel_id=1, source_target_pairs={{0,96},{32,0},{64,32},{96,64},{1,97},{33,1},{65,33},{97,65},{2,98}... | collective-permute-start | bytes 1179656 | tf_op jit(solution)/shard_map/ppermute | solution.py:32
  128.6 16.1 %collective-permute-start.25 = (bf16[672,256]{1,0:T(8,128)(2,1)S(1)}, bf16[672,256]{1,0:T(8,128)(2,1)S(1)}, u32[]{:S(2)}, u32[]{:S(2)}) collective-permute-start(bf16[672,256]{1,0:T(8,128)(2,1)S(1)} %collective-permute-done.16), channel_id=1, source_target_pairs={{0,32},{32,64},{64,96},{96,0},{1,33},{33,65},{65,97},{97,1},{2,34}... | collective-permute-start | bytes 1032200 | tf_op jit(solution)/shard_map/ppermute | solution.py:32
  128.6 16.1 %collective-permute-start.26 = (bf16[672,256]{1,0:T(8,128)(2,1)}, bf16[672,256]{1,0:T(8,128)(2,1)S(1)}, u32[]{:S(2)}, u32[]{:S(2)}) collective-permute-start(bf16[672,256]{1,0:T(8,128)(2,1)} %collective-permute-done.17), channel_id=1, source_target_pairs={{0,96},{32,0},{64,32},{96,64},{1,97},{33,1},{65,33},{97,65},{2,98}... | collective-permute-start | bytes 1032200 | tf_op jit(solution)/shard_map/ppermute | solution.py:32
  144.8 3.1 %collective-permute-start.29 = (bf16[672,512]{1,0:T(8,128)(2,1)S(1)}, bf16[672,512]{1,0:T(8,128)(2,1)S(1)}, u32[]{:S(2)}, u32[]{:S(2)}) collective-permute-start(bf16[672,512]{1,0:T(8,128)(2,1)S(1)} %constant_dynamic-update-slice_fusion.own_ref), channel_id=1, source_target_pairs={{0,1},{1,0},{2,3},{3,2},{4,5},{5,4},{6,7},{7,6},{8,9},{9,8},{10,11... | collective-permute-start | bytes 2064392 | tf_op jit(solution)/shard_map/ppermute | solution.py:28
  147.9 2.2 %copy-start = (f32[2,672,768]{2,1,0:T(8,128)S(1)}, f32[2,672,768]{2,1,0:T(8,128)}, u32[]{:S(2)}) copy-start(f32[2,672,768]{2,1,0:T(8,128)} %near_terms.1.acc_ref) | copy-start | bytes 12386308
Sparse Core Ops, SparseCore 0:
  57.7 51.1 all-gather.2
